TPU v7x, 32 devices: a whole 2x2x4 slice. The times are simulated.
32 devices in a mesh: sess: 2 (over x), ctx: 16 (over z, y, core).
Axes of the slice: x: 2, y: 2, z: 4, core: 2. Of those that a mesh axis runs over, the one named last changes fastest.
Arguments:
- mamba_input: bfloat16 [2, 2048, 8192], P('sess', 'ctx'), may hold values from -6 to 6
- step_size: bfloat16 [2, 2048, 64], P('sess', 'ctx'), may hold values from 0.19921875 to 1.5
- decay_log: bfloat16 [2, 2048, 64], P('sess', 'ctx'), may hold values from -0.8 to 0
- state_write: bfloat16 [2, 2048, 512], P('sess', 'ctx'), may hold values from -0.375 to 0.375
- state_read: bfloat16 [2, 2048, 512], P('sess', 'ctx'), may hold values from -0.75 to 0.75
- skip_gain: float32 [64], replicated, may hold values from 0.1 to 1.9
- saved_states: float32 [2, 3, 64, 8192], P('sess', None, 'ctx'), may hold values from -6 to 6
- home_slot: int32 [6], replicated, may hold values from 0 to 5, each once
- turn_lengths: int32 [2, 3], P('sess'), may hold values from 1 to 1024, 2048 in all within a row
- history_lengths: int32 [2, 3], P('sess'), may hold values from 4 to 1023
- queries: bfloat16 [2, 2048, 4096], P('sess', 'ctx'), may hold values from -150 to 150
- turn_keys: bfloat16 [2, 2048, 512], P('sess', 'ctx'), may hold values from -6 to 6
- turn_values: bfloat16 [2, 2048, 512], P('sess', 'ctx'), may hold values from -6 to 6
- cache_keys: bfloat16 [2, 3, 512, 512], P('sess', None, 'ctx'), may hold values from -6 to 6
- cache_values: bfloat16 [2, 3, 512, 512], P('sess', None, 'ctx'), may hold values from -6 to 6
- sink_keys: bfloat16 [2, 3, 4, 512], P('sess'), may hold values from -12 to 12
- sink_values: bfloat16 [2, 3, 4, 512], P('sess'), may hold values from -6 to 6
Outputs:
- mixed: bfloat16 [2, 2048, 8192], P('sess', 'ctx')
- attended: bfloat16 [2, 2048, 4096], P('sess', 'ctx')
Inputs may be any that keep to these rules, and one draw needn't show every extreme that they name: `home_slot`: entry g * 3 + s names the stored state, in the group-major list of saved_states, from which session s of group g resumes.
All inputs are finite; a program needn't handle non-finite values.
Results may differ from a plain program's by a relative error of at most 0.004.
Values may be sent and summed in bfloat16 or wider, within the bound.
No kernel may reach another device: no remote copies, remote signals or barrier semaphores. Data moves between devices by JAX's collectives and lax.ppermute only.
A program may use at most 256 MiB of HBM per device.

v0:
```python
import math

import jax
import jax.numpy as jnp
from jax import lax
from jax.sharding import PartitionSpec as P

REACH = 4
SEQS = 3
SINKS = 4
H = 64
P_SIZE = 128
N = 64
G = 8
QH = 32
KVH = 4
HD = 128
WINDOW = 512


precise = lax.Precision.HIGHEST


def carried_in(array, axis, combine, identity):
    length, place = (lax.axis_size(axis), lax.axis_index(axis))
    everything = jax.tree.map(lambda part: lax.all_gather(part, axis), array)
    start = jax.tree.map(
        lambda part, zero: jnp.broadcast_to(jnp.asarray(zero, part.dtype), part.shape),
        array,
        identity,
    )

    def turn(k, before):
        reached = k < place
        new = combine(before, jax.tree.map(lambda part: part[k], everything))
        return jax.tree.map(lambda a, b: jnp.where(reached, a, b), new, before)

    return lax.fori_loop(0, length, turn, start)


def shifted(block, axis, distance):
    devices = range(lax.axis_size(axis))
    route = [(i - distance, i) for i in devices if i - distance in devices]
    return lax.ppermute(block, axis, route)


def session_starts(lengths):
    ends = jnp.cumsum(lengths)
    return jnp.concatenate([jnp.zeros((1,), jnp.int32), ends[:-1]])


def session_of(positions, starts):
    later = positions[:, None] >= starts[None, 1:]
    return jnp.sum(later.astype(jnp.int32), axis=1)


def stretch_terms(inputs, step_sizes, log_rates, writes, read_rows, segment, relative, states):
    stretch_len = inputs.shape[0]
    sessions = states.shape[0]
    positions = jnp.arange(stretch_len, dtype=jnp.int32)
    log_rate = jnp.transpose(log_rates.astype(jnp.float32), (1, 2, 0))
    running = jnp.cumsum(log_rate, axis=2)
    before = running - log_rate
    causal = (segment[:, None] == segment[None, :]) & (positions[:, None] >= positions[None, :])
    differences = running[:, :, :, None] - running[:, :, None, :]
    decays = jnp.exp(jnp.where(causal, differences, -jnp.inf))
    intersection = jnp.einsum("tgn,sgn->gts", read_rows, writes, preferred_element_type=jnp.float32)
    step_scale = jnp.transpose(step_sizes.astype(jnp.float32), (1, 2, 0))
    mixing = (intersection[:, None] * decays * step_scale[:, :, None, :]).astype(jnp.bfloat16)
    intra_part = jnp.einsum("gkts,sgkp->tgkp", mixing, inputs, preferred_element_type=jnp.float32)
    session_ids = jnp.arange(sessions, dtype=jnp.int32)
    inside = (relative >= 0) & (relative < stretch_len)
    at_start = positions[None, :] == relative[:, None]
    base_log = jnp.sum(jnp.where(at_start[None, None], before[:, :, None, :], 0.0), axis=3)
    owned = segment[:, None] == session_ids[None, :]
    starts_here = owned & inside[None, :]
    exponent = running[:, :, None, :] - base_log[:, :, :, None]
    from_saved = jnp.exp(jnp.where(jnp.transpose(starts_here)[None, None], exponent, -jnp.inf))
    read_float = read_rows.astype(jnp.float32)
    readout = jnp.einsum("tgn,sgkpn->sgktp", read_float, states, precision=precise)
    intra_part = intra_part + jnp.einsum("gkst,sgktp->tgkp", from_saved, readout, precision=precise)
    earlier = jnp.any(owned & (relative[None, :] < 0), axis=1)
    from_incoming = jnp.where(earlier[None, None, :], jnp.exp(running), 0.0)
    last_session = segment[stretch_len - 1]
    tail_decay = jnp.exp(
        jnp.where(
            (segment == last_session)[None, None, :],
            running[:, :, stretch_len - 1 :] - running,
            -jnp.inf,
        )
    )
    loadings = (
        (tail_decay * step_scale)[:, :, :, None]
        * jnp.transpose(writes.astype(jnp.float32), (1, 0, 2))[:, None]
    ).astype(jnp.bfloat16)
    summary = jnp.einsum("sgkp,gksn->gkpn", inputs, loadings, preferred_element_type=jnp.float32)
    ending = owned[stretch_len - 1] & inside
    end_decay = jnp.exp(
        jnp.where(ending[None, None, :], running[:, :, stretch_len - 1 :] - base_log, -jnp.inf)
    )
    summary = summary + jnp.einsum("gks,sgkpn->gkpn", end_decay, states, precision=precise)
    carry_factor = jnp.where(earlier[stretch_len - 1], jnp.exp(running[:, :, stretch_len - 1]), 0.0)
    return (intra_part, from_incoming, carry_factor, summary)


def finish(intra_part, from_incoming, read_rows, state_in, inputs, skip_gains):
    carried = jnp.einsum(
        "tgn,gkpn->tgkp", read_rows.astype(jnp.float32), state_in, precision=precise
    )
    weight = jnp.transpose(from_incoming, (2, 0, 1))[..., None]
    result = (
        intra_part + weight * carried + skip_gains[None, :, :, None] * inputs.astype(jnp.float32)
    )
    return result.astype(jnp.bfloat16)


def chain_step(earlier, later):
    return (earlier[0] * later[0], later[0][:, None] * earlier[1] + later[1])


def visible(query_pos, turn_pos, starts, history):
    sessions = starts.shape[0]
    session_ids = jnp.arange(sessions, dtype=jnp.int32)
    owner = session_of(query_pos, starts)
    in_session = owner[:, None] == session_ids[None, :]
    offset = query_pos - jnp.sum(jnp.where(in_session, starts[None, :], 0), axis=1)
    sink_owner = jnp.arange(sessions * SINKS, dtype=jnp.int32) // SINKS
    sink_ok = owner[:, None] == sink_owner[None, :]
    slot_ids = jnp.arange(sessions * WINDOW, dtype=jnp.int32)
    slot_owner = slot_ids // WINDOW
    slot_place = slot_ids % WINDOW
    slot_history = jnp.sum(
        jnp.where(slot_owner[:, None] == session_ids[None, :], history[None, :], 0), axis=1
    )
    cache_ok = (
        (owner[:, None] == slot_owner[None, :])
        & (slot_place[None, :] > offset[:, None])
        & (slot_history - WINDOW + slot_place >= SINKS)[None, :]
    )
    key_owner = session_of(turn_pos, starts)
    distance = query_pos[:, None] - turn_pos[None, :]
    turn_ok = (
        (turn_pos[None, :] >= 0)
        & (key_owner[None, :] == owner[:, None])
        & (distance >= 0)
        & (distance < WINDOW)
    )
    return jnp.concatenate([sink_ok, cache_ok, turn_ok], axis=1)


def attend(queries, keys, payload_elements, valid):
    row_count = queries.shape[0]
    per_group = QH // KVH
    factor = 1.0 / math.sqrt(HD)

    def one_head(number):
        query_h = lax.dynamic_slice_in_dim(
            queries, number * per_group * HD, per_group * HD, 1
        ).reshape(row_count, per_group, HD)
        key_h = lax.dynamic_slice_in_dim(keys, number * HD, HD, 1)
        value_h = lax.dynamic_slice_in_dim(payload_elements, number * HD, HD, 1)
        scores = (
            jnp.einsum("tgd,nd->gtn", query_h, key_h, preferred_element_type=jnp.float32) * factor
        )
        scores = jnp.where(valid[None], scores, -jnp.inf)
        row_max = jnp.max(scores, axis=2, keepdims=True)
        weights = jnp.exp(scores - row_max)
        denominator = jnp.sum(weights, axis=2)
        rounded = weights.astype(jnp.bfloat16)
        mixed = jnp.einsum("gtn,nd->tgd", rounded, value_h, preferred_element_type=jnp.float32)
        return mixed / jnp.transpose(denominator)[:, :, None]

    outputs = lax.map(one_head, jnp.arange(KVH, dtype=jnp.int32))
    return jnp.transpose(outputs, (1, 0, 2, 3)).reshape(row_count, QH * HD).astype(jnp.bfloat16)


def shards(
    mamba_input,
    step_size,
    decay_log,
    state_write,
    state_read,
    skip_gain,
    saved_states,
    home_slot,
    turn_lengths,
    history_lengths,
    queries,
    turn_keys,
    turn_values,
    cache_keys,
    cache_values,
    sink_keys,
    sink_values,
):
    device_index = lax.axis_index("ctx")
    row_count = mamba_input.shape[1]
    local_heads = saved_states.shape[2]
    state_width = P_SIZE * N
    heads_per = H // G
    starts = session_starts(turn_lengths[0])
    own_slots = lax.dynamic_slice_in_dim(home_slot, lax.axis_index("sess") * SEQS, SEQS, 0)
    zeros_init = jnp.zeros((SEQS, local_heads, state_width), jnp.float32)
    piece = lax.all_gather(saved_states, "sess", axis=0, tiled=True)
    span_groups = piece.shape[0]
    slots = (
        jnp.arange(span_groups, dtype=jnp.int32)[:, None] * SEQS
        + jnp.arange(SEQS, dtype=jnp.int32)[None, :]
    ).reshape(span_groups * SEQS)
    selector = (own_slots[:, None] == slots[None, :]).astype(jnp.float32)
    flattened = piece.reshape(span_groups * SEQS, local_heads * state_width)
    restored = jnp.dot(selector, flattened, precision=precise).reshape(zeros_init.shape)
    gathered = lax.all_gather(restored, "ctx", axis=1, tiled=True)
    saved = gathered.reshape(SEQS, G, heads_per, P_SIZE, N)
    tokens_in = mamba_input[0].reshape(row_count, G, heads_per, P_SIZE)
    step_view = step_size[0].reshape(row_count, G, heads_per)
    rate_view = decay_log[0].reshape(row_count, G, heads_per)
    write_view = state_write[0].reshape(row_count, G, N)
    read_view = state_read[0].reshape(row_count, G, N)
    first_row = device_index * row_count
    segment = session_of(first_row + jnp.arange(row_count, dtype=jnp.int32), starts)
    intra_part, incoming, carry_factor, summary = stretch_terms(
        tokens_in, step_view, rate_view, write_view, read_view, segment, starts - first_row, saved
    )
    flat_factor = carry_factor.reshape(H)
    flat_summary = summary.reshape(H, state_width)
    prefix = carried_in(
        (flat_factor, flat_summary),
        "ctx",
        chain_step,
        (jnp.ones_like(flat_factor), jnp.zeros_like(flat_summary)),
    )
    state_in = prefix[1].reshape(G, heads_per, P_SIZE, N)
    mixed = finish(
        intra_part, incoming, read_view, state_in, tokens_in, skip_gain.reshape(G, heads_per)
    ).reshape(1, row_count, H * P_SIZE)
    features = turn_keys.shape[2]
    key_value = jnp.stack([turn_keys[0], turn_values[0]])
    blocks = [key_value]
    moving = key_value
    for number in range(REACH):
        moving = shifted(moving, "ctx", 1)
        blocks.append(moving)
    band_keys = jnp.concatenate(blocks[::-1], axis=1)
    history_k, history_v = (
        lax.all_gather(cache_keys, "ctx", axis=2, tiled=True),
        lax.all_gather(cache_values, "ctx", axis=2, tiled=True),
    )
    all_keys = jnp.concatenate(
        [
            sink_keys[0].reshape(SEQS * SINKS, features),
            history_k[0].reshape(SEQS * WINDOW, features),
            band_keys[0],
        ],
        axis=0,
    )
    all_values = jnp.concatenate(
        [
            sink_values[0].reshape(SEQS * SINKS, features),
            history_v[0].reshape(SEQS * WINDOW, features),
            band_keys[1],
        ],
        axis=0,
    )
    first_row = device_index * row_count
    query_pos = first_row + jnp.arange(row_count, dtype=jnp.int32)
    turn_pos = first_row - REACH * row_count + jnp.arange((REACH + 1) * row_count, dtype=jnp.int32)
    valid = visible(query_pos, turn_pos, starts, history_lengths[0])
    attended = attend(queries[0], all_keys, all_values, valid).reshape(1, row_count, QH * HD)
    return (mixed, attended)


def solution(mesh):
    return jax.shard_map(
        shards,
        mesh=mesh,
        in_specs=(
            P("sess", "ctx", None),
            P("sess", "ctx", None),
            P("sess", "ctx", None),
            P("sess", "ctx", None),
            P("sess", "ctx", None),
            P(),
            P("sess", None, "ctx", None),
            P(),
            P("sess", None),
            P("sess", None),
            P("sess", "ctx", None),
            P("sess", "ctx", None),
            P("sess", "ctx", None),
            P("sess", None, "ctx", None),
            P("sess", None, "ctx", None),
            P("sess", None, None, None),
            P("sess", None, None, None),
        ),
        out_specs=(P("sess", "ctx", None), P("sess", "ctx", None)),
        check_vma=False,
    )
```

profile of v0, /device:TPU:0, one launch (start us, length us, event | category | flops | bytes accessed | tf_op | source)
XLA Modules:
  0.0 413.7 jit_solution(16723106150592847620)
XLA Ops:
  7.4 13.0 %all_gather.18 = f32[2,3,4,8192]{3,2,1,0:T(4,128)S(1)} all-gather(f32[1,3,4,8192]{3,2,1,0:T(4,128)} %param.27), channel_id=1, replica_groups=mesh['sess'=2,'ctx'=16] {'sess'}, dimensions={0}, use_global_device_ids=true | all-gather | bytes 1179648 | tf_op jit(solution)/shard_map/all_gather | solution.py:204
  21.1 1.8 fusion.55
  27.0 3.2 copy.52
  30.4 2.3 reduce_window_sum.18
  34.9 64.5 %all-gather.6.cloned.1.call-done = f32[3,64,8192]{2,0,1:T(4,128)} async-done(((f32[3,4,8192]{2,0,1:T(4,128)}), f32[3,64,8192]{2,0,1:T(4,128)}) %all-gather.6.cloned.1.call-update) | async-done | bytes 6291472 | tf_op jit(solution)/shard_map/all_gather | solution.py:213
  99.5 9.7 %copy.54 = f32[3,64,8192]{2,1,0:T(8,128)} copy(f32[3,64,8192]{2,0,1:T(4,128)} %all-gather.6.cloned.1.call-done) | data formatting | bytes 12582912 | tf_op jit(solution)/shard_map/all_gather | solution.py:213
  109.2 10.8 %reshape.308 = f32[3,8,8,128,64]{4,3,2,1,0:T(8,128)} reshape(f32[3,64,8192]{2,1,0:T(8,128)} %copy.54) | data formatting | bytes 12582912 | tf_op jit(solution)/shard_map/reshape | solution.py:214
  120.0 8.3 %multiply_reduce_fusion = f32[8,8,128,64]{3,2,1,0:T(8,128)} fusion(f32[3,8,8,128,64]{4,3,2,1,0:T(8,128)} %reshape.308, f32[8,8,3]{1,0,2:T(8,128)S(1)} %copy.85), kind=kLoop, calls=%fused_computation.24 | loop fusion | flops 2621440 | bytes 8389376
  128.4 3.9 copy.79
  132.2 4.5 %bitcast_add_fusion.2 = f32[8,8,128,64]{2,3,1,0:T(8,128)} fusion(f32[8,8,128,64]{2,3,1,0:T(8,128)} %copy.79, bf16[128,8,8,128]{0,3,2,1:T(8,128)(2,1)S(1)} %bitcast.156, f32[8,128,64]{1,2,0:T(8,128)S(1)} %convert_bitcast_fusion, f32[8,8,128]{2,1,0:T(8,128)S(1)} %get-tuple-element.247), kind=kOutput, calls=%fused_computation.32 | convolution fusion | flops 135790592 | bytes 6586368 | tf_op jit(solution)/shard_map/sgkp,gksn->gkpn/dot_general | solution.py:96
  136.7 3.8 copy.57
  140.5 4.9 %all_gather_reshape.4 = f32[1,64,8192]{2,1,0:T(8,128)} reshape(f32[8,8,128,64]{3,2,1,0:T(8,128)} %copy.57) | data formatting | bytes 4194304 | tf_op jit(solution)/shard_map/all_gather;reshape | solution.py:26
  145.5 2.2 collective-permute-start
  148.9 1.4 and_and_fusion
  150.7 4.1 collective-permute-start.1
  155.4 7.1 %collective-permute-start.2 = (bf16[2,128,512]{2,1,0:T(8,128)(2,1)}, bf16[2,128,512]{2,1,0:T(8,128)(2,1)}, u32[]{:S(2)}, u32[]{:S(2)}) collective-permute-start(bf16[2,128,512]{2,1,0:T(8,128)(2,1)} %collective-permute-done.1), channel_id=1, source_target_pairs={{0,1},{1,2},{2,3},{3,4},{4,5},{5,6},{6,7},{7,8},{8,9},{9,10},{10,1... | collective-permute-start | bytes 786440 | tf_op jit(solution)/shard_map/ppermute | solution.py:44
  162.9 2.3 copy.59
  165.2 1.7 concatenate.33
  166.9 19.3 %all-gather = f32[16,1,64]{2,1,0:T(1,128)S(1)} all-gather(f32[1,1,64]{2,1,0:T(1,128)S(1)} %reshape.313), channel_id=1, replica_groups=mesh['sess'=2,'ctx'=16] {'ctx'}, dimensions={0}, use_global_device_ids=true | all-gather | bytes 4352 | tf_op jit(solution)/shard_map/all_gather | solution.py:26
  186.5 2.5 collective-permute-start.3
  189.0 4.8 %fusion.32 = f32[8,8,128,128]{2,3,1,0:T(8,128)} fusion(bf16[128,8,8,128]{0,3,2,1:T(8,128)(2,1)} %bitcast.157, f32[8,8,128]{2,1,0:T(8,128)} %convert_bitcast_fusion.1, f32[8,8,128]{2,1,0:T(8,128)} %copy-done.6, f32[8,128,128]{2,1,0:T(8,128)S(1)} %fusion.66, pred[128,128]{1,0:T(8,128)(4,1)S(1)} %fusion.43), kind=kOutput, calls=%fused_computation.31 | convolution fusion | flops 273678336 | bytes 6897664 | tf_op jit(solution)/shard_map/gkts,sgkp->tgkp/dot_general | solution.py:70
  196.9 13.0 %concatenate.32 = bf16[2188,512]{1,0:T(8,128)(2,1)} concatenate(bf16[12,512]{1,0:T(8,128)(2,1)S(1)} %reshape_squeeze.26, bf16[1536,512]{1,0:T(8,128)(2,1)} %bitcast.165, bf16[640,512]{1,0:T(8,128)(2,1)} %get-tuple-element.244), dimensions={0} | concatenate | bytes 4481024 | tf_op jit(solution)/shard_map/concatenate | solution.py:257
  210.0 12.3 %concatenate.34 = bf16[2188,512]{1,0:T(8,128)(2,1)} concatenate(bf16[12,512]{1,0:T(8,128)(2,1)S(1)} %reshape_squeeze.28, bf16[1536,512]{1,0:T(8,128)(2,1)} %bitcast.166, bf16[640,512]{1,0:T(8,128)(2,1)S(1)} %get-tuple-element.243), dimensions={0} | concatenate | bytes 4481024 | tf_op jit(solution)/shard_map/concatenate | solution.py:249
  222.3 40.6 %while.26 = (s32[]{:T(128)}, bf16[4,128,8,128]{1,3,2,0:T(8,128)(2,1)}, s32[4]{0:T(128)S(1)}, bf16[2188,512]{1,0:T(8,128)(2,1)}, pred[128,2188]{0,1:T(8,128)(4,1)...) while((s32[]{:T(128)}, ...), condition=%wide.region_13.14_spmd, body=%wide.region_10.13_spmd.sunk | while | flops 1162954752 | bytes 38025012 | solution.py:173
  225.0 2.4 fusion.85
  227.4 1.2 fusion.86
  228.6 2.8 fusion.87
  231.4 1.0 copy-done.2
  233.5 1.0 constant_dynamic-slice_fusion.2
  235.1 2.4 fusion.85
  237.5 1.2 fusion.86
  238.9 2.8 fusion.87
  241.7 1.0 copy-done.2
  245.3 2.4 fusion.85
  247.7 1.2 fusion.86
  249.0 2.9 fusion.87
  251.8 1.0 copy-done.2
  255.5 2.4 fusion.85
  257.9 1.2 fusion.86
  259.2 2.7 fusion.87
  261.9 1.0 copy-done.2
  262.9 2.3 copy.83
  265.2 12.8 %fusion.24 = f32[128,8,8,128]{0,3,2,1:T(8,128)} fusion(f32[128,8,8,3]{0,2,3,1:T(8,128)S(1)} %copy.84, bf16[128,8,64,1,1]{0,2,4,3,1:T(8,128)(2,1)S(1)} %bitcast.163, f32[3,8,8,128,64]{4,3,2,1,0:T(8,128)} %reshape.308), kind=kOutput, calls=%fused_computation.21 | convolution fusion | flops 2421161984 | bytes 10715136 | tf_op jit(solution)/shard_map/tgn,sgkpn->sgktp/dot_general | solution.py:80
  277.9 73.6 %all-gather.8.cloned.1.call-done = f32[16,64,8192]{2,1,0:T(8,128)} async-done(((f32[1,64,8192]{2,1,0:T(8,128)}), f32[16,64,8192]{2,1,0:T(8,128)}) %all-gather.8.cloned.1.call-update) | async-done | bytes 33554448 | tf_op jit(solution)/shard_map/all_gather | solution.py:26
  351.5 41.4 %while.27 = (s32[]{:T(128)}, f32[64,8192]{1,0:T(8,128)S(1)}, s32[]{:T(128)}, f32[16,64]{1,0:T(8,128)S(1)}, f32[16,64,8192]{2,1,0:T(8,128)}, /*index=5*/s32[]{:T(128)}, s32[]{:T(128)}) while((s32[]{:T(128)}, f32[64,8192]{1,0:T(8,128)S(1)}, s32[]{:T(128)}, f32[16,64]{1,0:T(8,128)S(1)}, f32[16,64,8192]{2,1,0:T(8,128)}, ...), condition=%wide.region_6.7_spmd.clone, body=%wide.region_5.6_spmd.clone.sunk | while | flops 2097156 | bytes 6292337 | solution.py:38
  351.5 2.5 fusion.88
  354.1 2.5 fusion.88
  356.7 2.5 fusion.88
  359.3 2.5 fusion.88
  361.9 2.5 fusion.88
  364.5 2.5 fusion.88
  367.0 2.5 fusion.88
  369.6 2.5 fusion.88
  372.2 2.5 fusion.88
  374.8 2.5 fusion.88
  377.4 2.5 fusion.88
  380.0 2.5 fusion.88
  382.6 2.5 fusion.88
  385.2 2.5 fusion.88
  387.8 2.5 fusion.88
  390.3 2.5 fusion.88
  392.9 3.0 reshape.309
  395.9 8.3 %fusion.29 = bf16[128,8,8,128]{0,3,2,1:T(8,128)(2,1)S(1)} fusion(f32[128,8,8,128]{0,3,2,1:T(8,128)} %fusion.24, f32[8,8,128,128]{2,3,1,0:T(8,128)} %fusion.32, bf16[128,8,8,128]{0,3,2,1:T(8,128)(2,1)} %bitcast.158, f32[8,8,128,64]{3,2,1,0:T(8,128)} %reshape.309, bf16[128,8,64,1]{0,2,3,1:T(8,128)(2,1)S(1)} %bitcast.164, f32[8,8]{1,0:T(8,128)S(1)} %mul.131, ...), kind=kOutput, calls=%fused_computation.28 | convolution fusion | flops 812646400 | bytes 14844160 | tf_op jit(solution)/shard_map/tgn,gkpn->tgkp/dot_general | solution.py:107
  404.3 2.9 copy.61
  (140 shorter events, 18.9 us)
Async XLA Ops:
  7.2 23.0 %copy-start.10 = (bf16[1,128,512]{2,1,0:T(8,128)(2,1)S(1)}, bf16[1,128,512]{2,1,0:T(8,128)(2,1)}, u32[]{:S(2)}) copy-start(bf16[1,128,512]{2,1,0:T(8,128)(2,1)} %param.24) | copy-start | bytes 393220
  7.2 23.2 %copy-start.12 = (bf16[1,128,64]{1,2,0:T(8,128)(2,1)S(1)}, bf16[1,128,64]{1,2,0:T(8,128)(2,1)}, u32[]{:S(2)}) copy-start(bf16[1,128,64]{1,2,0:T(8,128)(2,1)} %param.23) | copy-start | bytes 49156
  7.2 26.9 %copy-start.13 = (bf16[1,128,64]{1,2,0:T(8,128)(2,1)S(1)}, bf16[1,128,64]{1,2,0:T(8,128)(2,1)}, u32[]{:S(2)}) copy-start(bf16[1,128,64]{1,2,0:T(8,128)(2,1)} %param.22) | copy-start | bytes 49156
  7.2 92.3 %all-gather.6.cloned.1.call-start = ((), (), s32[]{:S(2)}) async-start(), calls=%async_computation | async-start | bytes 8912896 | tf_op jit(solution)/shard_map/all_gather | solution.py:213
  23.0 173.9 %all-gather.10.cloned.1.call-start = ((), (), s32[]{:S(2)}) async-start(), calls=%async_computation.2 | async-start | bytes 1671168 | tf_op jit(solution)/shard_map/all_gather | solution.py:247
  23.7 186.2 %all-gather.12.cloned.1.call-start = ((), (), s32[]{:S(2)}) async-start(), calls=%async_computation.3 | async-start | bytes 1671168 | tf_op jit(solution)/shard_map/all_gather | solution.py:246
  24.5 327.1 %all-gather.8.cloned.1.call-start = ((), (), s32[]{:S(2)}) async-start(), calls=%async_computation.1 | async-start | bytes 35651584 | tf_op jit(solution)/shard_map/all_gather | solution.py:26
  30.2 102.0 %copy-start = (bf16[1,128,8192]{1,2,0:T(8,128)(2,1)}, bf16[1,128,8192]{1,2,0:T(8,128)(2,1)S(1)}, u32[]{:S(2)}) copy-start(bf16[1,128,8192]{1,2,0:T(8,128)(2,1)S(1)} %copy.52) | copy-start | bytes 6291460
  32.6 122.3 %copy-start.6 = (f32[8,8,128]{2,1,0:T(8,128)}, f32[8,8,128]{2,1,0:T(8,128)S(1)}, u32[]{:S(2)}) copy-start(f32[8,8,128]{2,1,0:T(8,128)S(1)} %reduce_window_sum.18) | copy-start | bytes 98308
  140.5 4.9 %copy-start.3 = (bf16[1,128,512]{2,1,0:T(8,128)(2,1)S(1)}, bf16[1,128,512]{2,1,0:T(8,128)(2,1)}, u32[]{:S(2)}) copy-start(bf16[1,128,512]{2,1,0:T(8,128)(2,1)} %param.32) | copy-start | bytes 393220
  140.5 4.9 %copy-start.4 = (bf16[1,128,512]{2,1,0:T(8,128)(2,1)S(1)}, bf16[1,128,512]{2,1,0:T(8,128)(2,1)}, u32[]{:S(2)}) copy-start(bf16[1,128,512]{2,1,0:T(8,128)(2,1)} %param.33) | copy-start | bytes 393220
  140.5 7.3 %copy-start.16 = (s32[1,3]{1,0:T(1,128)S(1)}, s32[1,3]{1,0:T(1,128)}, u32[]{:S(2)}) copy-start(s32[1,3]{1,0:T(1,128)} %param.30) | copy-start | bytes 40
  140.5 22.1 %copy-start.11 = (bf16[1,128,512]{2,1,0:T(8,128)(2,1)S(1)}, bf16[1,128,512]{2,1,0:T(8,128)(2,1)}, u32[]{:S(2)}) copy-start(bf16[1,128,512]{2,1,0:T(8,128)(2,1)} %param.25) | copy-start | bytes 393220
  140.5 22.3 %copy-start.17 = (f32[64]{0:T(128)S(1)}, f32[64]{0:T(128)}, u32[]{:S(2)}) copy-start(f32[64]{0:T(128)} %param.26) | copy-start | bytes 772
  140.5 22.4 %copy-start.14 = (bf16[1,3,4,512]{3,2,1,0:T(4,128)(2,1)S(1)}, bf16[1,3,4,512]{3,2,1,0:T(4,128)(2,1)}, u32[]{:S(2)}) copy-start(bf16[1,3,4,512]{3,2,1,0:T(4,128)(2,1)} %param.37) | copy-start | bytes 36868
  140.5 22.4 %copy-start.15 = (bf16[1,3,4,512]{3,2,1,0:T(4,128)(2,1)S(1)}, bf16[1,3,4,512]{3,2,1,0:T(4,128)(2,1)}, u32[]{:S(2)}) copy-start(bf16[1,3,4,512]{3,2,1,0:T(4,128)(2,1)} %param.36) | copy-start | bytes 36868
  145.5 5.2 %collective-permute-start = (bf16[2,128,512]{2,1,0:T(8,128)(2,1)S(1)}, bf16[2,128,512]{2,1,0:T(8,128)(2,1)S(1)}, u32[]{:S(2)}, u32[]{:S(2)}) collective-permute-start(bf16[2,128,512]{2,1,0:T(8,128)(2,1)S(1)} %pad_maximum_fusion), channel_id=1, source_target_pairs={{0,1},{1,2},{2,3},{3,4},{4,5},{5,6},{6,7},{7,8},{8,9},{9,10},{10,1... | collective-permute-start | bytes 786440 | tf_op jit(solution)/shard_map/ppermute | solution.py:44
  150.7 11.9 %copy-start.7 = (bf16[2,128,512]{2,1,0:T(8,128)(2,1)}, bf16[2,128,512]{2,1,0:T(8,128)(2,1)S(1)}, u32[]{:S(2)}) copy-start(bf16[2,128,512]{2,1,0:T(8,128)(2,1)S(1)} %collective-permute-done) | copy-start | bytes 786436
  150.7 4.7 %collective-permute-start.1 = (bf16[2,128,512]{2,1,0:T(8,128)(2,1)S(1)}, bf16[2,128,512]{2,1,0:T(8,128)(2,1)}, u32[]{:S(2)}, u32[]{:S(2)}) collective-permute-start(bf16[2,128,512]{2,1,0:T(8,128)(2,1)S(1)} %collective-permute-done), channel_id=1, source_target_pairs={{0,1},{1,2},{2,3},{3,4},{4,5},{5,6},{6,7},{7,8},{8,9},{9,10},{10,1... | collective-permute-start | bytes 786440 | tf_op jit(solution)/shard_map/ppermute | solution.py:44
  155.4 31.1 %collective-permute-start.2 = (bf16[2,128,512]{2,1,0:T(8,128)(2,1)}, bf16[2,128,512]{2,1,0:T(8,128)(2,1)}, u32[]{:S(2)}, u32[]{:S(2)}) collective-permute-start(bf16[2,128,512]{2,1,0:T(8,128)(2,1)} %collective-permute-done.1), channel_id=1, source_target_pairs={{0,1},{1,2},{2,3},{3,4},{4,5},{5,6},{6,7},{7,8},{8,9},{9,10},{10,1... | collective-permute-start | bytes 786440 | tf_op jit(solution)/shard_map/ppermute | solution.py:44
  186.5 9.4 %copy-start.8 = (bf16[2,128,512]{2,1,0:T(8,128)(2,1)S(1)}, bf16[2,128,512]{2,1,0:T(8,128)(2,1)}, u32[]{:S(2)}) copy-start(bf16[2,128,512]{2,1,0:T(8,128)(2,1)} %copy-done.7) | copy-start | bytes 786436
  186.5 9.4 %copy-start.5 = (bf16[1,128,512]{2,1,0:T(8,128)(2,1)S(1)}, bf16[1,128,512]{2,1,0:T(8,128)(2,1)}, u32[]{:S(2)}) copy-start(bf16[1,128,512]{2,1,0:T(8,128)(2,1)} %param.33) | copy-start | bytes 393220
  186.5 7.4 %collective-permute-start.3 = (bf16[2,128,512]{2,1,0:T(8,128)(2,1)}, bf16[2,128,512]{2,1,0:T(8,128)(2,1)S(1)}, u32[]{:S(2)}, u32[]{:S(2)}) collective-permute-start(bf16[2,128,512]{2,1,0:T(8,128)(2,1)} %collective-permute-done.2), channel_id=1, source_target_pairs={{0,1},{1,2},{2,3},{3,4},{4,5},{5,6},{6,7},{7,8},{8,9},{9,10},{10,1... | collective-permute-start | bytes 786440 | tf_op jit(solution)/shard_map/ppermute | solution.py:44
  227.4 1.2 copy-start.1
  231.4 1.0 copy-start.2
  237.5 1.4 copy-start.1
  241.6 1.0 copy-start.2
  247.7 1.2 copy-start.1
  251.8 1.0 copy-start.2
  257.9 1.2 copy-start.1
  261.9 1.0 copy-start.2
  392.9 3.0 copy-start.9
Sparse Core Ops, SparseCore 0:
  23.1 76.3 all-gather.5
  101.7 37.9 all-gather.9
  141.8 41.1 all-gather.11
  184.5 166.9 all-gather.7
where the time goes:
time: 417 us; the launch traced here: 414 us
  waiting for transfers between devices  140 us (34%)
  local copies, waits for them, and re-layouts  90 us (22%)
  other arithmetic  62.8 us (15%)
  matrix products  53.3 us (13%)
  blocking collectives  32.2 us (8%)
  starting transfers between devices  16.1 us (4%)
  between operations  14.2 us (3%)
  loops' own time  5.24 us (1%)
    all_gather x1, waiting for transfers between devices, carried_in(): everything = jax.tree.map(lambda part: lax.all_gather(part, axis), array)  73.6 us
    all_gather x1, waiting for transfers between devices, shards(): gathered = lax.all_gather(restored, 'ctx', axis=1, tiled=True)  64.5 us
    select_n x16, other arithmetic, turn(): return jax.tree.map(lambda a, b: jnp.where(reached, a, b), new, before)  40.7 us
    all_gather x1, blocking collectives, carried_in(): everything = jax.tree.map(lambda part: lax.all_gather(part, axis), array)  19.3 us
    ppermute x4, starting transfers between devices, shifted(): return lax.ppermute(block, axis, route)  16 us
    concatenate x1, local copies, waits for them, and re-layouts, shards(): jnp.concatenate([sink_values[0].reshape(SEQS * SINKS, features), history_...  13 us
    all_gather x1, blocking collectives, shards(): piece = lax.all_gather(saved_states, 'sess', axis=0, tiled=True)  13 us
    dot_general x1, matrix products, stretch_terms(): jnp.einsum('tgn,sgkpn->sgktp', read_float, states, precision=precise)  12.8 us
  transfers between devices with their start and end apart: 8, of which 3 were waited for; matrix products, arithmetic and copies ran while one was open for 35% of the time, Pallas kernels for 0%

commit v1 on v0

v1 whole, which is shorter than its diff:
```python
import functools
import math

import jax
import jax.numpy as jnp
from jax import lax
from jax.experimental import pallas as pl
from jax.experimental.pallas import tpu as pltpu
from jax.sharding import PartitionSpec as P

REACH = 4
SEQS = 3
SINKS = 4
H = 64
P_SIZE = 128
N = 64
G = 8
QH = 32
KVH = 4
HD = 128
WINDOW = 512
TOK = 128

HEADS_PER = H // G
PAIR = 2 * HEADS_PER
STEPS = H // PAIR
EXTRA = 16
BLOCK = 64
SPAN = WINDOW + BLOCK
COLUMNS = SPAN + 64
NEG = -1e30


def session_at(position, meta):
    return (position >= meta[1]).astype(jnp.int32) + (position >= meta[2]).astype(jnp.int32)


def start_of(session, meta):
    return jnp.where(session == 0, 0, jnp.where(session == 1, meta[1], meta[2]))


def last_start(meta):
    first = meta[0] * TOK
    return jnp.maximum(start_of(session_at(first + TOK - 1, meta), meta) - first, 0)


def params(mib=48):
    return pltpu.CompilerParams(vmem_limit_bytes=mib * 1024 * 1024)


def running_rows(dl_ref, step_ref):
    both = jnp.concatenate([dl_ref[...], step_ref[...]], axis=1).astype(jnp.float32).T
    rates, steps = both[:H], both[H:]
    k = lax.broadcasted_iota(jnp.int32, (TOK, TOK), 0)
    u = lax.broadcasted_iota(jnp.int32, (TOK, TOK), 1)
    upto = (k <= u).astype(jnp.bfloat16)
    running = jnp.dot(rates.astype(jnp.bfloat16), upto, preferred_element_type=jnp.float32)
    return rates, running, steps


def summary_kernel(local, meta, x_ref, dl_ref, step_ref, write_ref, out_ref, coef_s, factor_s, write_s):
    step = pl.program_id(0)

    @pl.when(step == 0)
    def _():
        rates, running, steps = running_rows(dl_ref, step_ref)
        r = last_start(meta)
        lane = lax.broadcasted_iota(jnp.int32, (H, TOK), 1)
        last = running[:, TOK - 1 :]
        base = jnp.sum(jnp.where(lane < r, rates, 0.0), axis=1, keepdims=True)
        coef_s[...] = jnp.where(lane >= r, jnp.exp(last - running) * steps, 0.0)
        factor_s[...] = jnp.broadcast_to(jnp.exp(last - base), (H, TOK))
        write_s[...] = write_ref[...].astype(jnp.float32).T

    coef = coef_s[pl.ds(pl.multiple_of(step * PAIR, PAIR), PAIR), :]
    factor = factor_s[pl.ds(pl.multiple_of(step * PAIR, PAIR), PAIR), :]
    writes = write_s[pl.ds(pl.multiple_of(step * 2 * N, 2 * N), 2 * N), :]
    for k in range(PAIR):
        group = k // HEADS_PER
        loading = (writes[group * N : (group + 1) * N] * coef[k : k + 1]).astype(jnp.bfloat16)
        summary = jnp.dot(
            loading, x_ref[:, k * P_SIZE : (k + 1) * P_SIZE], preferred_element_type=jnp.float32
        )
        place = (k % local) * N
        out_ref[k // local, place : place + N, :] = summary.astype(jnp.bfloat16)
    for j in range(PAIR // local):
        rows = factor[j * local : (j + 1) * local]
        high = rows.astype(jnp.bfloat16).astype(jnp.float32)
        parts = [high, rows - high]
        if EXTRA > 2 * local:
            parts.append(jnp.zeros((EXTRA - 2 * local, TOK), jnp.float32))
        out_ref[j, local * N :, :] = jnp.concatenate(parts, axis=0).astype(jnp.bfloat16)


def summaries(meta, x, rates, steps, writes, local):
    owners = H // local
    rows = local * N + EXTRA
    return pl.pallas_call(
        functools.partial(summary_kernel, local),
        out_shape=jax.ShapeDtypeStruct((owners, rows, P_SIZE), jnp.bfloat16),
        grid_spec=pltpu.PrefetchScalarGridSpec(
            num_scalar_prefetch=1,
            grid=(STEPS,),
            in_specs=[
                pl.BlockSpec((TOK, PAIR * P_SIZE), lambda i, m: (0, i)),
                pl.BlockSpec((TOK, H), lambda i, m: (0, 0)),
                pl.BlockSpec((TOK, H), lambda i, m: (0, 0)),
                pl.BlockSpec((TOK, G * N), lambda i, m: (0, 0)),
            ],
            out_specs=pl.BlockSpec((PAIR // local, rows, P_SIZE), lambda i, m: (i, 0, 0)),
            scratch_shapes=[
                pltpu.VMEM((H, TOK), jnp.float32),
                pltpu.VMEM((H, TOK), jnp.float32),
                pltpu.VMEM((G * N, TOK), jnp.float32),
            ],
        ),
        compiler_params=params(),
        cost_estimate=pl.CostEstimate(flops=2 * H * TOK * N * P_SIZE, bytes_accessed=3 << 20, transcendentals=0),
        name="summaries",
    )(meta, x, rates, steps, writes)


def intra_kernel(meta, skip, x_ref, dl_ref, step_ref, write_ref, read_ref, out_ref, run_s, step_s):
    step = pl.program_id(0)

    @pl.when(step == 0)
    def _():
        _, running, steps = running_rows(dl_ref, step_ref)
        run_s[...] = running
        step_s[...] = steps

    heads = pl.ds(pl.multiple_of(step * PAIR, PAIR), PAIR)
    running = run_s[heads, :]
    sizes = step_s[heads, :]
    columns = running.T
    r = last_start(meta)
    t = lax.broadcasted_iota(jnp.int32, (TOK, TOK), 0)
    u = lax.broadcasted_iota(jnp.int32, (TOK, TOK), 1)
    causal = (u <= t) & ((u >= r) | (t < r))
    for group in range(2):
        part = slice(group * N, (group + 1) * N)
        products = lax.dot_general(
            read_ref[:, part], write_ref[:, part], (((1,), (1,)), ((), ())),
            preferred_element_type=jnp.float32,
        )
        products = jnp.where(causal, products, 0.0)
        for k in range(group * HEADS_PER, (group + 1) * HEADS_PER):
            difference = columns[:, k : k + 1] - running[k : k + 1]
            decay = jnp.exp(jnp.minimum(difference, 0.0))
            mixing = (products * decay * sizes[k : k + 1]).astype(jnp.bfloat16)
            place = slice(k * P_SIZE, (k + 1) * P_SIZE)
            x = x_ref[:, place]
            mixed = jnp.dot(mixing, x, preferred_element_type=jnp.float32)
            out_ref[:, place] = mixed + skip[step * PAIR + k] * x.astype(jnp.float32)


def intra(meta, skip, x, rates, steps, writes, reads):
    return pl.pallas_call(
        intra_kernel,
        out_shape=jax.ShapeDtypeStruct((TOK, H * P_SIZE), jnp.float32),
        grid_spec=pltpu.PrefetchScalarGridSpec(
            num_scalar_prefetch=2,
            grid=(STEPS,),
            in_specs=[
                pl.BlockSpec((TOK, PAIR * P_SIZE), lambda i, m, s: (0, i)),
                pl.BlockSpec((TOK, H), lambda i, m, s: (0, 0)),
                pl.BlockSpec((TOK, H), lambda i, m, s: (0, 0)),
                pl.BlockSpec((TOK, 2 * N), lambda i, m, s: (0, i)),
                pl.BlockSpec((TOK, 2 * N), lambda i, m, s: (0, i)),
            ],
            out_specs=pl.BlockSpec((TOK, PAIR * P_SIZE), lambda i, m, s: (0, i)),
            scratch_shapes=[
                pltpu.VMEM((H, TOK), jnp.float32),
                pltpu.VMEM((H, TOK), jnp.float32),
            ],
        ),
        compiler_params=params(),
        cost_estimate=pl.CostEstimate(
            flops=8 * H * TOK * TOK * P_SIZE, bytes_accessed=7 << 20, transcendentals=H * TOK * TOK
        ),
        name="intra",
    )(meta, skip, x, rates, steps, writes, reads)


def recurrence_kernel(local, meta, got_ref, restored_ref, out_ref):
    width = local * N
    state = [jnp.zeros((N, P_SIZE), jnp.float32) for _ in range(local)]
    for c in range(got_ref.shape[0]):
        first = c * TOK
        opening = session_at(first, meta)
        closing = session_at(first + TOK - 1, meta)
        opens = start_of(opening, meta) >= first
        closes = start_of(closing, meta) >= first
        for k in range(local):
            rows = slice(k * N, (k + 1) * N)
            entering = jnp.where(opens, restored_ref[opening, rows, :], state[k])
            out_ref[c, rows, :] = entering.astype(jnp.bfloat16)
            source = jnp.where(closes, restored_ref[closing, rows, :], state[k])
            factor = got_ref[c, width : width + EXTRA, :].astype(jnp.float32)
            decay = factor[k : k + 1] + factor[local + k : local + k + 1]
            state[k] = decay * source + got_ref[c, rows, :].astype(jnp.float32)


def recurrence(meta, got, restored, local):
    owners = got.shape[0]
    return pl.pallas_call(
        functools.partial(recurrence_kernel, local),
        out_shape=jax.ShapeDtypeStruct((owners, local * N, P_SIZE), jnp.bfloat16),
        grid_spec=pltpu.PrefetchScalarGridSpec(
            num_scalar_prefetch=1,
            grid=(1,),
            in_specs=[
                pl.BlockSpec(got.shape, lambda i, m: (0, 0, 0)),
                pl.BlockSpec(restored.shape, lambda i, m: (0, 0, 0)),
            ],
            out_specs=pl.BlockSpec((owners, local * N, P_SIZE), lambda i, m: (0, 0, 0)),
        ),
        compiler_params=params(),
        cost_estimate=pl.CostEstimate(flops=1 << 21, bytes_accessed=3 << 20, transcendentals=0),
        name="recurrence",
    )(meta, got, restored)


def finish_kernel(local, meta, part_ref, dl_ref, step_ref, read_ref, a_ref, b_ref, out_ref, factor_s):
    step = pl.program_id(0)
    r = last_start(meta)

    @pl.when(step == 0)
    def _():
        rates, running, _ = running_rows(dl_ref, step_ref)
        lane = lax.broadcasted_iota(jnp.int32, (H, TOK), 1)
        base = jnp.sum(jnp.where(lane < r, rates, 0.0), axis=1, keepdims=True)
        factor_s[...] = jnp.exp(jnp.minimum(running - jnp.where(lane >= r, base, 0.0), 0.0))

    factor = factor_s[pl.ds(pl.multiple_of(step * PAIR, PAIR), PAIR), :].T
    token = lax.broadcasted_iota(jnp.int32, (TOK, N), 0)
    resumed = (token >= r) & (r > 0)
    for group in range(2):
        reads = read_ref[:, group * N : (group + 1) * N].astype(jnp.float32)
        left = jnp.where(resumed, 0.0, reads)
        right = jnp.where(resumed, reads, 0.0)
        reads = jnp.concatenate([left, right], axis=1).astype(jnp.bfloat16)
        for k in range(group * HEADS_PER, (group + 1) * HEADS_PER):
            rows = slice((k % local) * N, (k % local + 1) * N)
            states = jnp.concatenate([a_ref[k // local, rows, :], b_ref[k // local, 0, rows, :]], axis=0)
            carried = jnp.dot(reads, states, preferred_element_type=jnp.float32)
            place = slice(k * P_SIZE, (k + 1) * P_SIZE)
            out_ref[:, place] = (part_ref[:, place] + factor[:, k : k + 1] * carried).astype(jnp.bfloat16)


def finish(meta, part, rates, steps, reads, entering, resumed, local):
    owners = PAIR // local

    def resumed_index(i, m):
        return (i, jnp.maximum(session_at(m[0] * TOK + TOK - 1, m) - 1, 0), 0, 0)

    return pl.pallas_call(
        functools.partial(finish_kernel, local),
        out_shape=jax.ShapeDtypeStruct((TOK, H * P_SIZE), jnp.bfloat16),
        grid_spec=pltpu.PrefetchScalarGridSpec(
            num_scalar_prefetch=1,
            grid=(STEPS,),
            in_specs=[
                pl.BlockSpec((TOK, PAIR * P_SIZE), lambda i, m: (0, i)),
                pl.BlockSpec((TOK, H), lambda i, m: (0, 0)),
                pl.BlockSpec((TOK, H), lambda i, m: (0, 0)),
                pl.BlockSpec((TOK, 2 * N), lambda i, m: (0, i)),
                pl.BlockSpec((owners, local * N, P_SIZE), lambda i, m: (i, 0, 0)),
                pl.BlockSpec((owners, 1, local * N, P_SIZE), resumed_index),
            ],
            out_specs=pl.BlockSpec((TOK, PAIR * P_SIZE), lambda i, m: (0, i)),
            scratch_shapes=[pltpu.VMEM((H, TOK), jnp.float32)],
        ),
        compiler_params=params(),
        cost_estimate=pl.CostEstimate(
            flops=2 * H * TOK * TOK * P_SIZE, bytes_accessed=9 << 20, transcendentals=H * TOK
        ),
        name="finish",
    )(meta, part, rates, steps, reads, entering, resumed)


def attend_kernel(
    meta, q_ref, band4, band3, band2, band1, band0, ka_ref, va_ref, kb_ref, vb_ref, sk_ref, sv_ref,
    out_ref, key_s, value_s,
):
    factor = 1.0 / math.sqrt(HD)
    first = meta[0] * TOK
    r = last_start(meta)
    opening = session_at(first, meta)
    closing = session_at(first + TOK - 1, meta)
    bands = (band4, band3, band2, band1, band0)
    length = (REACH + 1) * TOK

    def one_session(session, hk_ref, hv_ref, resuming, needed):
        start = start_of(session, meta) - first + WINDOW
        oldest = start - WINDOW + jnp.maximum(SINKS + WINDOW - meta[3 + session], 0)

        @pl.when(needed & (start > 0))
        def _():
            row = lax.broadcasted_iota(jnp.int32, (length, WINDOW), 0)
            place = lax.broadcasted_iota(jnp.int32, (length, WINDOW), 1)
            moved = (place == row - start + WINDOW).astype(jnp.bfloat16)
            keys = hk_ref[:, 0, 0].reshape(WINDOW, HD)
            values = hv_ref[:, 0, 0].reshape(WINDOW, HD)
            history = jnp.dot(
                moved, jnp.concatenate([keys, values], axis=1), preferred_element_type=jnp.float32
            )
            for i, band in enumerate(bands):
                rows = slice(i * TOK, (i + 1) * TOK)
                index = lax.broadcasted_iota(jnp.int32, (TOK, HD), 0) + i * TOK
                turn = index >= start
                key_s[rows, :] = jnp.where(
                    turn, band[0].astype(jnp.float32), history[rows, :HD]
                ).astype(jnp.bfloat16)
                value_s[rows, :] = jnp.where(
                    turn, band[1].astype(jnp.float32), history[rows, HD:]
                ).astype(jnp.bfloat16)

        @pl.when(needed & (start <= 0))
        def _():
            for i, band in enumerate(bands):
                rows = slice(i * TOK, (i + 1) * TOK)
                key_s[rows, :] = band[0]
                value_s[rows, :] = band[1]

        for b in range(TOK // BLOCK):
            inside = (b * BLOCK + BLOCK > r) if resuming else (b * BLOCK < r)

            @pl.when(needed & inside)
            def _():
                rows = slice(b * BLOCK, b * BLOCK + SPAN)
                keys = jnp.concatenate([key_s[rows, :], sk_ref[session]], axis=0)
                values = jnp.concatenate([value_s[rows, :], sv_ref[session]], axis=0)
                tokens = slice(b * BLOCK, (b + 1) * BLOCK)
                queries = jnp.concatenate(
                    [q_ref[tokens, g * HD : (g + 1) * HD] for g in range(QH // KVH)], axis=0
                )
                scores = lax.dot_general(
                    queries, keys, (((1,), (1,)), ((), ())), preferred_element_type=jnp.float32
                )
                token = lax.broadcasted_iota(jnp.int32, (BLOCK, COLUMNS), 0)
                column = lax.broadcasted_iota(jnp.int32, (BLOCK, COLUMNS), 1)
                seen = (column > token) & (column <= token + WINDOW) & (column >= oldest - b * BLOCK)
                seen = (seen & (column < SPAN)) | ((column >= SPAN) & (column < SPAN + SINKS))
                bias = jnp.where(seen, 0.0, NEG)
                weights, sums = [], []
                for g in range(QH // KVH):
                    score = scores[g * BLOCK : (g + 1) * BLOCK] * factor + bias
                    weight = jnp.exp(score - jnp.max(score, axis=1, keepdims=True))
                    sums.append(jnp.sum(weight, axis=1, keepdims=True))
                    weights.append(weight.astype(jnp.bfloat16))
                mixed = jnp.dot(
                    jnp.concatenate(weights, axis=0), values, preferred_element_type=jnp.float32
                )
                for g in range(QH // KVH):
                    result = mixed[g * BLOCK : (g + 1) * BLOCK] / sums[g]
                    lanes = slice(g * HD, (g + 1) * HD)
                    if resuming:
                        index = lax.broadcasted_iota(jnp.int32, (BLOCK, HD), 0) + b * BLOCK
                        before = out_ref[tokens, lanes].astype(jnp.float32)
                        result = jnp.where(index >= r, result, before)
                    out_ref[tokens, lanes] = result.astype(jnp.bfloat16)

    one_session(opening, ka_ref, va_ref, False, r > 0)
    one_session(closing, kb_ref, vb_ref, True, r >= 0)


def attend(meta, queries, bands, history, sink_keys, sink_values):
    owners, _, _, rows, _ = history.shape
    lanes = QH // KVH * HD

    def history_spec(which, last):
        def index(j, m):
            return (0, which, session_at(m[0] * TOK + (TOK - 1 if last else 0), m), 0, j)

        return pl.BlockSpec((owners, 1, 1, rows, HD), index)

    pad = SEQS, COLUMNS - SPAN, HD
    return pl.pallas_call(
        attend_kernel,
        out_shape=jax.ShapeDtypeStruct((TOK, QH * HD), jnp.bfloat16),
        grid_spec=pltpu.PrefetchScalarGridSpec(
            num_scalar_prefetch=1,
            grid=(KVH,),
            in_specs=[pl.BlockSpec((TOK, lanes), lambda j, m: (0, j))]
            + [pl.BlockSpec((2, TOK, HD), lambda j, m: (0, 0, j))] * (REACH + 1)
            + [history_spec(0, False), history_spec(1, False), history_spec(0, True), history_spec(1, True)]
            + [pl.BlockSpec(pad, lambda j, m: (0, 0, j))] * 2,
            out_specs=pl.BlockSpec((TOK, lanes), lambda j, m: (0, j)),
            scratch_shapes=[
                pltpu.VMEM(((REACH + 1) * TOK, HD), jnp.bfloat16),
                pltpu.VMEM(((REACH + 1) * TOK, HD), jnp.bfloat16),
            ],
        ),
        compiler_params=params(),
        cost_estimate=pl.CostEstimate(
            flops=16 * TOK * QH * COLUMNS * HD, bytes_accessed=8 << 20,
            transcendentals=2 * TOK * QH * COLUMNS,
        ),
        name="attend",
    )(meta, queries, *bands, history, history, history, history, sink_keys, sink_values)


def shifted(block, axis, distance):
    devices = range(lax.axis_size(axis))
    return lax.ppermute(block, axis, [(i - distance, i) for i in devices if i - distance in devices])


def shards(
    mamba_input,
    step_size,
    decay_log,
    state_write,
    state_read,
    skip_gain,
    saved_states,
    home_slot,
    turn_lengths,
    history_lengths,
    queries,
    turn_keys,
    turn_values,
    cache_keys,
    cache_values,
    sink_keys,
    sink_values,
):
    place = lax.axis_index("ctx")
    group = lax.axis_index("sess")
    groups = lax.axis_size("sess")
    local = saved_states.shape[2]
    lengths = turn_lengths[0]
    meta = jnp.concatenate(
        [jnp.stack([place, lengths[0], lengths[0] + lengths[1]]), history_lengths[0]]
    ).astype(jnp.int32)
    x, rates, steps = mamba_input[0], decay_log[0], step_size[0]
    writes, reads = state_write[0], state_read[0]

    stored = [saved_states[0]]
    for j in range(1, groups):
        route = [((i + j) % groups, i) for i in range(groups)]
        stored.append(lax.ppermute(saved_states[0], "sess", route))
    stored = jnp.concatenate(stored, axis=0)
    slots = lax.dynamic_slice_in_dim(home_slot, group * SEQS, SEQS, 0)
    index = (slots // SEQS - group) % groups * SEQS + slots % SEQS
    restored = jnp.concatenate(
        [lax.dynamic_slice_in_dim(stored, index[s], 1, 0) for s in range(SEQS)], axis=0
    )
    restored = jnp.swapaxes(restored.reshape(SEQS, local, P_SIZE, N), 2, 3).reshape(SEQS, local * N, P_SIZE)

    history = lax.all_gather(jnp.stack([cache_keys[0], cache_values[0]]), "ctx", axis=0)
    key_value = jnp.stack([turn_keys[0], turn_values[0]])
    bands = [shifted(key_value, "ctx", k) for k in range(REACH, 0, -1)] + [key_value]

    sent = summaries(meta, x, rates, steps, writes, local)
    got = lax.all_to_all(sent, "ctx", 0, 0, tiled=True)
    resumed = lax.all_gather(restored[1:].astype(jnp.bfloat16), "ctx", axis=0)
    part = intra(meta, skip_gain, x, rates, steps, writes, reads)
    entering = recurrence(meta, got, restored, local)
    entering = lax.all_to_all(entering, "ctx", 0, 0, tiled=True)

    sinks = [
        jnp.pad(s[0], ((0, 0), (0, COLUMNS - SPAN - SINKS), (0, 0))) for s in (sink_keys, sink_values)
    ]
    attended = attend(meta, queries[0], bands, history, *sinks)
    mixed = finish(meta, part, rates, steps, reads, entering, resumed, local)
    return mixed[None], attended[None]


def solution(mesh):
    token = P("sess", "ctx", None)
    return jax.shard_map(
        shards,
        mesh=mesh,
        in_specs=(
            token,
            token,
            token,
            token,
            token,
            P(),
            P("sess", None, "ctx", None),
            P(),
            P("sess", None),
            P("sess", None),
            token,
            token,
            token,
            P("sess", None, "ctx", None),
            P("sess", None, "ctx", None),
            P("sess", None, None, None),
            P("sess", None, None, None),
        ),
        out_specs=(token, token),
        check_vma=False,
    )
```

time: 417 us -> 169 us (0.41)
  the two profiles are of different devices: /device:TPU:0 before, /device:TPU:18 now
where the time goes in v1:
time: 169 us; the launch traced here: 168 us
  waiting for transfers between devices  74 us (44%)
  Pallas kernels  26.6 us (16%)
  starting transfers between devices  22.4 us (13%)
  between operations  21.5 us (13%)
  local copies, waits for them, and re-layouts  18.9 us (11%)
  other arithmetic  4.26 us (3%)
    all_to_all x1, waiting for transfers between devices, shards(): got = lax.all_to_all(sent, 'ctx', 0, 0, tiled=True)  34.9 us
    ppermute x4, waiting for transfers between devices, shifted(): lax.ppermute(block, axis, [(i - distance, i) for i in devices if i - dist...  24.2 us
    pallas_call x1, Pallas kernels, attend(): pl.pallas_call(attend_kernel, out_shape=jax.ShapeDtypeStruct((TOK, QH * H...  12 us
    all_to_all x1, waiting for transfers between devices, shards(): entering = lax.all_to_all(entering, 'ctx', 0, 0, tiled=True)  11.6 us
    unnamed x43, local copies, waits for them, and re-layouts  11.4 us
    ppermute x4, starting transfers between devices, shifted(): lax.ppermute(block, axis, [(i - distance, i) for i in devices if i - dist...  10.6 us
    all_to_all x1, starting transfers between devices, shards(): got = lax.all_to_all(sent, 'ctx', 0, 0, tiled=True)  6.18 us
    pallas_call x1, Pallas kernels, finish(): pl.pallas_call(functools.partial(finish_kernel, local), out_shape=jax.Sha...  6.12 us
  transfers between devices with their start and end apart: 9, of which 7 were waited for; matrix products, arithmetic and copies ran while one was open for 7% of the time, Pallas kernels for 9%

profile of v1, /device:TPU:18, one launch (start us, length us, event | category | flops | bytes accessed | tf_op | source)
XLA Modules:
  0.0 167.6 jit_solution(9189103969735952493)
XLA Ops:
  7.2 0.0 all-gather.4.cloned.1.call-start
  7.2 0.6 collective-permute-start
  7.8 0.7 fusion.3
  8.6 0.7 fusion.6
  15.1 0.0 copy-start.13
  15.1 3.2 %collective-permute-done = f32[3,4,8192]{2,1,0:T(4,128)S(1)} collective-permute-done((f32[3,4,8192]{2,1,0:T(4,128)}, f32[3,4,8192]{2,1,0:T(4,128)S(1)}, u32[]{:S(2)}, u32[]{:S(2)}) %collective-permute-start) | collective-permute-done | bytes 393248 | tf_op jit(solution)/shard_map/ppermute | solution.py:442
  18.3 1.1 fusion.1
  19.5 0.0 copy-start.14
  19.5 0.0 copy-start.15
  19.5 0.0 copy-start.18
  19.5 0.0 copy-start.19
  19.5 0.0 copy-start
  19.5 0.0 copy-start.6
  19.5 0.1 pad_maximum_fusion
  19.6 0.4 reshape.28
  20.1 0.8 copy.32
  20.9 0.0 all-gather.4.cloned.1.call-update
  20.9 0.0 all-gather.6.cloned.1.call-start
  21.0 0.0 copy-done.13
  21.0 1.6 pad_maximum_fusion.1
  22.5 0.0 all-gather.6.cloned.1.call-update
  22.6 0.0 copy-done.12
  22.6 0.0 copy-done.14
  22.6 0.1 copy.29
  22.7 0.0 copy-done.15
  22.7 0.1 copy.30
  22.8 0.0 copy-done.18
  22.8 0.6 fusion.7
  24.7 0.7 pad_add_fusion.meta
  25.4 0.0 copy-done.6
  25.4 2.2 %summaries.1 = bf16[16,272,128]{2,1,0:T(8,128)(2,1)S(1)} custom-call(s32[6]{0:T(128)S(1)} %pad_add_fusion.meta, bf16[128,8192]{1,0:T(8,128)(2,1)S(1)} %bitcast.22, bf16[128,64]{1,0:T(8,128)(2,1)S(1)} %bitcast.25, bf16[128,64]{1,0:T(8,128)(2,1)S(1)} %bitcast.28, bf16[128,512]{1,0:T(8,128)(2,1)S(1)} %bitcast.33), custom_call_target="tpu_custom_call" | custom-call | flops 134217728 | bytes 3145728 | tf_op jit(solution)/shard_map/summaries/pallas_call | solution.py:98
  27.7 0.0 copy-start.1
  27.7 1.0 copy-done.1
  28.7 6.2 %all-to-all-start = ((bf16[16,272,128]{2,1,0:T(8,128)(2,1)}), bf16[16,272,128]{2,1,0:T(8,128)(2,1)S(1)}, u32[]{:S(2)}, u32[]{:S(2)}) async-start(bf16[16,272,128]{2,1,0:T(8,128)(2,1)} %copy-done.1), calls=%async_computation | async-start | bytes 2228224 | tf_op jit(solution)/shard_map/all_to_all | solution.py:456
  34.9 2.1 %copy.31 = f32[3,4,64,128]{3,2,1,0:T(8,128)} copy(f32[3,4,64,128]{2,3,1,0:T(8,128)} %bitcast.41) | data formatting | bytes 786432 | tf_op jit(solution)/shard_map/transpose | solution.py:449
  37.0 34.9 %all-to-all-done.got_ref = bf16[16,272,128]{2,1,0:T(8,128)(2,1)S(1)} async-done(((bf16[16,272,128]{2,1,0:T(8,128)(2,1)}), bf16[16,272,128]{2,1,0:T(8,128)(2,1)S(1)}, u32[]{:S(2)}, u32[]{:S(2)}) %all-to-all-start) | async-done | bytes 1114144 | tf_op jit(solution)/shard_map/all_to_all | solution.py:456
  71.9 1.0 copy-done.4
  72.9 1.0 recurrence.1
  73.9 0.0 copy-start.2
  73.9 1.0 copy-done.2
  74.9 5.0 %all-to-all-start.1 = ((bf16[16,256,128]{2,1,0:T(8,128)(2,1)}), bf16[16,256,128]{2,1,0:T(8,128)(2,1)S(1)}, u32[]{:S(2)}, u32[]{:S(2)}) async-start(bf16[16,256,128]{2,1,0:T(8,128)(2,1)} %copy-done.2), calls=%async_computation.1 | async-start | bytes 2097152 | tf_op jit(solution)/shard_map/all_to_all | solution.py:460
  79.8 1.6 constant_dynamic-update-slice_fusion.1
  81.4 1.6 constant_dynamic-update-slice_fusion.band0
  83.0 3.4 %collective-permute-start.1 = (bf16[2,128,512]{2,1,0:T(8,128)(2,1)}, bf16[2,128,512]{2,1,0:T(8,128)(2,1)}, u32[]{:S(2)}, u32[]{:S(2)}) collective-permute-start(bf16[2,128,512]{2,1,0:T(8,128)(2,1)} %constant_dynamic-update-slice_fusion.band0), channel_id=1, source_target_pairs={{0,4},{1,5},{2,6},{3,7},{4,8},{5,9},{6,10},{7,11},{8,12},{9,13},{1... | collective-permute-start | bytes 786440 | tf_op jit(solution)/shard_map/ppermute | solution.py:406
  86.3 2.8 %collective-permute-start.2 = (bf16[2,128,512]{2,1,0:T(8,128)(2,1)}, bf16[2,128,512]{2,1,0:T(8,128)(2,1)}, u32[]{:S(2)}, u32[]{:S(2)}) collective-permute-start(bf16[2,128,512]{2,1,0:T(8,128)(2,1)} %constant_dynamic-update-slice_fusion.band0), channel_id=1, source_target_pairs={{0,3},{1,4},{2,5},{3,6},{4,7},{5,8},{6,9},{7,10},{8,11},{9,12},{10... | collective-permute-start | bytes 786440 | tf_op jit(solution)/shard_map/ppermute | solution.py:406
  89.2 2.4 %collective-permute-start.3 = (bf16[2,128,512]{2,1,0:T(8,128)(2,1)}, bf16[2,128,512]{2,1,0:T(8,128)(2,1)}, u32[]{:S(2)}, u32[]{:S(2)}) collective-permute-start(bf16[2,128,512]{2,1,0:T(8,128)(2,1)} %constant_dynamic-update-slice_fusion.band0), channel_id=1, source_target_pairs={{0,2},{1,3},{2,4},{3,5},{4,6},{5,7},{6,8},{7,9},{8,10},{9,11},{10,... | collective-permute-start | bytes 786440 | tf_op jit(solution)/shard_map/ppermute | solution.py:406
  91.6 1.9 %collective-permute-start.4 = (bf16[2,128,512]{2,1,0:T(8,128)(2,1)}, bf16[2,128,512]{2,1,0:T(8,128)(2,1)}, u32[]{:S(2)}, u32[]{:S(2)}) collective-permute-start(bf16[2,128,512]{2,1,0:T(8,128)(2,1)} %constant_dynamic-update-slice_fusion.band0), channel_id=1, source_target_pairs={{0,1},{1,2},{2,3},{3,4},{4,5},{5,6},{6,7},{7,8},{8,9},{9,10},{10,1... | collective-permute-start | bytes 786440 | tf_op jit(solution)/shard_map/ppermute | solution.py:406
  93.6 0.0 copy-done.16
  93.6 0.7 pad.7.sk_ref
  94.3 0.0 copy-done.17
  94.3 0.7 pad.8.sv_ref
  95.0 5.2 %intra.1.part_ref = f32[128,8192]{1,0:T(8,128)} custom-call(s32[6]{0:T(128)S(1)} %pad_add_fusion.meta, f32[64]{0:T(128)S(1)} %copy-done.9, bf16[128,8192]{1,0:T(8,128)(2,1)S(1)} %bitcast.23, bf16[128,64]{1,0:T(8,128)(2,1)S(1)} %bitcast.26, bf16[128,64]{1,0:T(8,128)(2,1)S(1)} %bitcast.29, bf16[128,512]{1,0:T(8,128)(2,1)S(1)} %bitcast.34, ...), custom_call_target="tpu_custom_call" | custom-call | flops 1073741824 | bytes 7340032 | tf_op jit(solution)/shard_map/intra/pallas_call | solution.py:158
  100.2 11.6 %all-to-all-done.1.a_ref = bf16[16,256,128]{2,1,0:T(8,128)(2,1)S(1)} async-done(((bf16[16,256,128]{2,1,0:T(8,128)(2,1)}), bf16[16,256,128]{2,1,0:T(8,128)(2,1)S(1)}, u32[]{:S(2)}, u32[]{:S(2)}) %all-to-all-start.1) | async-done | bytes 1048608 | tf_op jit(solution)/shard_map/all_to_all | solution.py:460
  111.8 1.6 copy-done.3
  113.4 6.1 %finish.1 = bf16[128,8192]{1,0:T(8,128)(2,1)} custom-call(s32[6]{0:T(128)S(1)} %pad_add_fusion.meta, f32[128,8192]{1,0:T(8,128)} %intra.1.part_ref, bf16[128,64]{1,0:T(8,128)(2,1)S(1)} %bitcast.27, bf16[128,64]{1,0:T(8,128)(2,1)S(1)} %bitcast.30, bf16[128,512]{1,0:T(8,128)(2,1)S(1)} %bitcast.32, bf16[16,256,128]{2,1,0:T(8,128)(2,1)S(1)} %all-to-all-done.1.a_ref, ...), custom_call_target="tpu_custom_call" | custom-call | flops 268435456 | bytes 9437184 | tf_op jit(solution)/shard_map/finish/pallas_call | solution.py:257
  119.5 7.4 %collective-permute-done.1.band4 = bf16[2,128,512]{2,1,0:T(8,128)(2,1)} collective-permute-done((bf16[2,128,512]{2,1,0:T(8,128)(2,1)}, bf16[2,128,512]{2,1,0:T(8,128)(2,1)}, u32[]{:S(2)}, u32[]{:S(2)}) %collective-permute-start.1) | collective-permute-done | bytes 262176 | tf_op jit(solution)/shard_map/ppermute | solution.py:406
  127.0 4.7 %collective-permute-done.2.band3 = bf16[2,128,512]{2,1,0:T(8,128)(2,1)} collective-permute-done((bf16[2,128,512]{2,1,0:T(8,128)(2,1)}, bf16[2,128,512]{2,1,0:T(8,128)(2,1)}, u32[]{:S(2)}, u32[]{:S(2)}) %collective-permute-start.2) | collective-permute-done | bytes 262176 | tf_op jit(solution)/shard_map/ppermute | solution.py:406
  131.7 9.8 %collective-permute-done.3.band2 = bf16[2,128,512]{2,1,0:T(8,128)(2,1)} collective-permute-done((bf16[2,128,512]{2,1,0:T(8,128)(2,1)}, bf16[2,128,512]{2,1,0:T(8,128)(2,1)}, u32[]{:S(2)}, u32[]{:S(2)}) %collective-permute-start.3) | collective-permute-done | bytes 262176 | tf_op jit(solution)/shard_map/ppermute | solution.py:406
  141.4 2.3 %collective-permute-done.4.band1 = bf16[2,128,512]{2,1,0:T(8,128)(2,1)} collective-permute-done((bf16[2,128,512]{2,1,0:T(8,128)(2,1)}, bf16[2,128,512]{2,1,0:T(8,128)(2,1)}, u32[]{:S(2)}, u32[]{:S(2)}) %collective-permute-start.4) | collective-permute-done | bytes 262176 | tf_op jit(solution)/shard_map/ppermute | solution.py:406
  143.8 0.9 copy-done.7
  144.7 0.9 copy-done.8
  145.6 1.9 %copy-done.10 = bf16[32,3,32,512]{3,2,1,0:T(8,128)(2,1)S(1)} copy-done((bf16[32,3,32,512]{3,2,1,0:T(8,128)(2,1)S(1)}, bf16[32,3,32,512]{3,2,1,0:T(8,128)(2,1)}, u32[]{:S(2)}) %copy-start.10) | copy-done | bytes 3145752
  147.5 1.2 copy-done.11
  148.7 12.0 %attend.1 = bf16[128,4096]{1,0:T(8,128)(2,1)} custom-call(s32[6]{0:T(128)S(1)} %pad_add_fusion.meta, bf16[128,4096]{1,0:T(8,128)(2,1)S(1)} %bitcast.39, bf16[2,128,512]{2,1,0:T(8,128)(2,1)} %collective-permute-done.1.band4, bf16[2,128,512]{2,1,0:T(8,128)(2,1)} %collective-permute-done.2.band3, bf16[2,128,512]{2,1,0:T(8,128)(2,1)} %collective-permute-done.3.band2, ...), custom_call_target="tpu_custom_call" | custom-call | flops 5368709120 | bytes 8388608 | tf_op jit(solution)/shard_map/attend/pallas_call | solution.py:379
  (18 shorter events, 0.1 us)
Async XLA Ops:
  7.2 104.7 %all-gather.4.cloned.1.call-start = ((), (), s32[]{:S(2)}) async-start(), calls=%async_computation.2 | async-start | bytes 2228224 | tf_op jit(solution)/shard_map/all_gather | solution.py:457
  7.2 11.1 %collective-permute-start = (f32[3,4,8192]{2,1,0:T(4,128)}, f32[3,4,8192]{2,1,0:T(4,128)S(1)}, u32[]{:S(2)}, u32[]{:S(2)}) collective-permute-start(f32[3,4,8192]{2,1,0:T(4,128)} %bitcast.44), channel_id=1, source_target_pairs={{16,0},{0,16},{17,1},{1,17},{18,2},{2,18},{19,3},{3,19},{20,4},{4,... | collective-permute-start | bytes 1179656 | tf_op jit(solution)/shard_map/ppermute | solution.py:442
  15.1 5.8 %copy-start.13 = (bf16[1,3,32,512]{3,2,1,0:T(8,128)(2,1)S(1)}, bf16[1,3,32,512]{3,2,1,0:T(8,128)(2,1)}, u32[]{:S(2)}) copy-start(bf16[1,3,32,512]{3,2,1,0:T(8,128)(2,1)} %param.31) | copy-start | bytes 294916
  19.5 3.1 %copy-start.14 = (bf16[1,128,64]{1,2,0:T(8,128)(2,1)S(1)}, bf16[1,128,64]{1,2,0:T(8,128)(2,1)}, u32[]{:S(2)}) copy-start(bf16[1,128,64]{1,2,0:T(8,128)(2,1)} %param.19) | copy-start | bytes 49156
  19.5 3.2 %copy-start.15 = (bf16[1,128,64]{1,2,0:T(8,128)(2,1)S(1)}, bf16[1,128,64]{1,2,0:T(8,128)(2,1)}, u32[]{:S(2)}) copy-start(bf16[1,128,64]{1,2,0:T(8,128)(2,1)} %param.18) | copy-start | bytes 49156
  19.5 3.3 %copy-start.18 = (s32[1,3]{1,0:T(1,128)S(1)}, s32[1,3]{1,0:T(1,128)}, u32[]{:S(2)}) copy-start(s32[1,3]{1,0:T(1,128)} %param.25) | copy-start | bytes 40
  19.5 5.2 %copy-start.19 = (s32[1,3]{1,0:T(1,128)S(1)}, s32[1,3]{1,0:T(1,128)}, u32[]{:S(2)}) copy-start(s32[1,3]{1,0:T(1,128)} %param.26) | copy-start | bytes 40
  19.5 5.9 %copy-start = (bf16[1,128,8192]{2,1,0:T(8,128)(2,1)S(1)}, bf16[1,128,8192]{2,1,0:T(8,128)(2,1)}, u32[]{:S(2)}) copy-start(bf16[1,128,8192]{2,1,0:T(8,128)(2,1)} %param.17) | copy-start | bytes 6291460
  19.5 5.9 %copy-start.6 = (bf16[1,128,512]{2,1,0:T(8,128)(2,1)S(1)}, bf16[1,128,512]{2,1,0:T(8,128)(2,1)}, u32[]{:S(2)}) copy-start(bf16[1,128,512]{2,1,0:T(8,128)(2,1)} %param.20) | copy-start | bytes 393220
  20.1 2.5 %copy-start.12 = (f32[3,4,128,64]{3,2,1,0:T(8,128)}, f32[3,4,128,64]{3,2,1,0:T(8,128)S(1)}, u32[]{:S(2)}) copy-start(f32[3,4,128,64]{3,2,1,0:T(8,128)S(1)} %reshape.28) | copy-start | bytes 1179652
  20.9 122.8 %all-gather.6.cloned.1.call-start = ((), (), s32[]{:S(2)}) async-start(), calls=%async_computation.3 | async-start | bytes 3342336 | tf_op jit(solution)/shard_map/all_gather | solution.py:451
  27.7 1.0 copy-start.1
  28.7 43.2 %all-to-all-start = ((bf16[16,272,128]{2,1,0:T(8,128)(2,1)}), bf16[16,272,128]{2,1,0:T(8,128)(2,1)S(1)}, u32[]{:S(2)}, u32[]{:S(2)}) async-start(bf16[16,272,128]{2,1,0:T(8,128)(2,1)} %copy-done.1), calls=%async_computation | async-start | bytes 2228224 | tf_op jit(solution)/shard_map/all_to_all | solution.py:456
  71.9 1.0 copy-start.4
  72.9 20.7 %copy-start.16 = (bf16[1,3,4,512]{3,2,1,0:T(4,128)(2,1)S(1)}, bf16[1,3,4,512]{3,2,1,0:T(4,128)(2,1)}, u32[]{:S(2)}) copy-start(bf16[1,3,4,512]{3,2,1,0:T(4,128)(2,1)} %param.32) | copy-start | bytes 36868
  72.9 21.4 %copy-start.17 = (bf16[1,3,4,512]{3,2,1,0:T(4,128)(2,1)S(1)}, bf16[1,3,4,512]{3,2,1,0:T(4,128)(2,1)}, u32[]{:S(2)}) copy-start(bf16[1,3,4,512]{3,2,1,0:T(4,128)(2,1)} %param.33) | copy-start | bytes 36868
  73.9 1.0 copy-start.2
  74.9 20.1 %copy-start.5 = (bf16[1,128,512]{2,1,0:T(8,128)(2,1)S(1)}, bf16[1,128,512]{2,1,0:T(8,128)(2,1)}, u32[]{:S(2)}) copy-start(bf16[1,128,512]{2,1,0:T(8,128)(2,1)} %param.21) | copy-start | bytes 393220
  74.9 20.1 %copy-start.9 = (f32[64]{0:T(128)S(1)}, f32[64]{0:T(128)}, u32[]{:S(2)}) copy-start(f32[64]{0:T(128)} %skip.1) | copy-start | bytes 772
  74.9 37.0 %all-to-all-start.1 = ((bf16[16,256,128]{2,1,0:T(8,128)(2,1)}), bf16[16,256,128]{2,1,0:T(8,128)(2,1)S(1)}, u32[]{:S(2)}, u32[]{:S(2)}) async-start(bf16[16,256,128]{2,1,0:T(8,128)(2,1)} %copy-done.2), calls=%async_computation.1 | async-start | bytes 2097152 | tf_op jit(solution)/shard_map/all_to_all | solution.py:460
  83.0 44.0 %collective-permute-start.1 = (bf16[2,128,512]{2,1,0:T(8,128)(2,1)}, bf16[2,128,512]{2,1,0:T(8,128)(2,1)}, u32[]{:S(2)}, u32[]{:S(2)}) collective-permute-start(bf16[2,128,512]{2,1,0:T(8,128)(2,1)} %constant_dynamic-update-slice_fusion.band0), channel_id=1, source_target_pairs={{0,4},{1,5},{2,6},{3,7},{4,8},{5,9},{6,10},{7,11},{8,12},{9,13},{1... | collective-permute-start | bytes 786440 | tf_op jit(solution)/shard_map/ppermute | solution.py:406
  86.3 45.3 %collective-permute-start.2 = (bf16[2,128,512]{2,1,0:T(8,128)(2,1)}, bf16[2,128,512]{2,1,0:T(8,128)(2,1)}, u32[]{:S(2)}, u32[]{:S(2)}) collective-permute-start(bf16[2,128,512]{2,1,0:T(8,128)(2,1)} %constant_dynamic-update-slice_fusion.band0), channel_id=1, source_target_pairs={{0,3},{1,4},{2,5},{3,6},{4,7},{5,8},{6,9},{7,10},{8,11},{9,12},{10... | collective-permute-start | bytes 786440 | tf_op jit(solution)/shard_map/ppermute | solution.py:406
  89.2 52.2 %collective-permute-start.3 = (bf16[2,128,512]{2,1,0:T(8,128)(2,1)}, bf16[2,128,512]{2,1,0:T(8,128)(2,1)}, u32[]{:S(2)}, u32[]{:S(2)}) collective-permute-start(bf16[2,128,512]{2,1,0:T(8,128)(2,1)} %constant_dynamic-update-slice_fusion.band0), channel_id=1, source_target_pairs={{0,2},{1,3},{2,4},{3,5},{4,6},{5,7},{6,8},{7,9},{8,10},{9,11},{10,... | collective-permute-start | bytes 786440 | tf_op jit(solution)/shard_map/ppermute | solution.py:406
  91.6 52.1 %collective-permute-start.4 = (bf16[2,128,512]{2,1,0:T(8,128)(2,1)}, bf16[2,128,512]{2,1,0:T(8,128)(2,1)}, u32[]{:S(2)}, u32[]{:S(2)}) collective-permute-start(bf16[2,128,512]{2,1,0:T(8,128)(2,1)} %constant_dynamic-update-slice_fusion.band0), channel_id=1, source_target_pairs={{0,1},{1,2},{2,3},{3,4},{4,5},{5,6},{6,7},{7,8},{8,9},{9,10},{10,1... | collective-permute-start | bytes 786440 | tf_op jit(solution)/shard_map/ppermute | solution.py:406
  111.8 1.6 copy-start.3
  143.8 0.9 copy-start.7
  144.7 0.9 copy-start.8
  145.6 1.9 %copy-start.10 = (bf16[32,3,32,512]{3,2,1,0:T(8,128)(2,1)S(1)}, bf16[32,3,32,512]{3,2,1,0:T(8,128)(2,1)}, u32[]{:S(2)}) copy-start(bf16[32,3,32,512]{3,2,1,0:T(8,128)(2,1)} %all-gather.6.cloned.1.call-done) | copy-start | bytes 9437188
  147.5 1.2 copy-start.11
Sparse Core Ops, SparseCore 0:
  21.0 49.0 all-gather.3
  72.4 58.9 all-gather.5

commit v2 on v1

--- a/solution.py
+++ b/solution.py
@@ -58,7 +58,9 @@
     return rates, running, steps
 
 
-def summary_kernel(local, meta, x_ref, dl_ref, step_ref, write_ref, out_ref, coef_s, factor_s, write_s):
+def summary_kernel(
+    local, meta, x_ref, dl_ref, step_ref, write_ref, keep_ref, send_ref, coef_s, factor_s, write_s
+):
     step = pl.program_id(0)
 
     @pl.when(step == 0)
@@ -72,32 +74,51 @@
         factor_s[...] = jnp.broadcast_to(jnp.exp(last - base), (H, TOK))
         write_s[...] = write_ref[...].astype(jnp.float32).T
 
+    even = meta[0] % 2 == 0
     coef = coef_s[pl.ds(pl.multiple_of(step * PAIR, PAIR), PAIR), :]
     factor = factor_s[pl.ds(pl.multiple_of(step * PAIR, PAIR), PAIR), :]
     writes = write_s[pl.ds(pl.multiple_of(step * 2 * N, 2 * N), 2 * N), :]
-    for k in range(PAIR):
+
+    def summary(k):
         group = k // HEADS_PER
         loading = (writes[group * N : (group + 1) * N] * coef[k : k + 1]).astype(jnp.bfloat16)
-        summary = jnp.dot(
+        return jnp.dot(
             loading, x_ref[:, k * P_SIZE : (k + 1) * P_SIZE], preferred_element_type=jnp.float32
         )
-        place = (k % local) * N
-        out_ref[k // local, place : place + N, :] = summary.astype(jnp.bfloat16)
-    for j in range(PAIR // local):
-        rows = factor[j * local : (j + 1) * local]
-        high = rows.astype(jnp.bfloat16).astype(jnp.float32)
-        parts = [high, rows - high]
-        if EXTRA > 2 * local:
-            parts.append(jnp.zeros((EXTRA - 2 * local, TOK), jnp.float32))
-        out_ref[j, local * N :, :] = jnp.concatenate(parts, axis=0).astype(jnp.bfloat16)
+
+    for chip in range(PAIR // (2 * local)):
+        low, high = 2 * local * chip, 2 * local * chip + local
+        for k in range(local):
+            first, second = summary(low + k), summary(high + k)
+            rows = slice(k * N, (k + 1) * N)
+            keep_ref[chip, rows, :] = jnp.where(even, first, second).astype(jnp.bfloat16)
+            send_ref[chip, rows, :] = jnp.where(even, second, first).astype(jnp.bfloat16)
+        first, second = factor[low : low + local], factor[high : high + local]
+        keep_ref[chip, local * N :, :] = factor_rows(jnp.where(even, first, second))
+        send_ref[chip, local * N :, :] = factor_rows(jnp.where(even, second, first))
+
+
+def factor_rows(rows):
+    high = rows.astype(jnp.bfloat16).astype(jnp.float32)
+    parts = [high, rows - high]
+    if EXTRA > 2 * rows.shape[0]:
+        parts.append(jnp.zeros((EXTRA - 2 * rows.shape[0], TOK), jnp.float32))
+    return jnp.concatenate(parts, axis=0).astype(jnp.bfloat16)
+
+
+def factors_of(block, local):
+    block = block.astype(jnp.float32)
+    return block[:local] + block[local : 2 * local]
 
 
 def summaries(meta, x, rates, steps, writes, local):
-    owners = H // local
+    chips = H // (2 * local)
     rows = local * N + EXTRA
+    shape = jax.ShapeDtypeStruct((chips, rows, P_SIZE), jnp.bfloat16)
+    spec = pl.BlockSpec((PAIR // (2 * local), rows, P_SIZE), lambda i, m: (i, 0, 0))
     return pl.pallas_call(
         functools.partial(summary_kernel, local),
-        out_shape=jax.ShapeDtypeStruct((owners, rows, P_SIZE), jnp.bfloat16),
+        out_shape=[shape, shape],
         grid_spec=pltpu.PrefetchScalarGridSpec(
             num_scalar_prefetch=1,
             grid=(STEPS,),
@@ -107,7 +128,7 @@
                 pl.BlockSpec((TOK, H), lambda i, m: (0, 0)),
                 pl.BlockSpec((TOK, G * N), lambda i, m: (0, 0)),
             ],
-            out_specs=pl.BlockSpec((PAIR // local, rows, P_SIZE), lambda i, m: (i, 0, 0)),
+            out_specs=[spec, spec],
             scratch_shapes=[
                 pltpu.VMEM((H, TOK), jnp.float32),
                 pltpu.VMEM((H, TOK), jnp.float32),
@@ -118,6 +139,111 @@
         cost_estimate=pl.CostEstimate(flops=2 * H * TOK * N * P_SIZE, bytes_accessed=3 << 20, transcendentals=0),
         name="summaries",
     )(meta, x, rates, steps, writes)
+
+
+def whole(kernel, name, meta, arrays, shapes, size=2):
+    def spec(shape):
+        return pl.BlockSpec(shape, lambda i, m: (0,) * len(shape))
+
+    return pl.pallas_call(
+        kernel,
+        out_shape=[jax.ShapeDtypeStruct(s, t) for s, t in shapes],
+        grid_spec=pltpu.PrefetchScalarGridSpec(
+            num_scalar_prefetch=1,
+            grid=(1,),
+            in_specs=[spec(a.shape) for a in arrays],
+            out_specs=[spec(s) for s, _ in shapes],
+        ),
+        compiler_params=params(),
+        cost_estimate=pl.CostEstimate(flops=1 << 21, bytes_accessed=size << 20, transcendentals=0),
+        name=name,
+    )(meta, *arrays)
+
+
+def pack_kernel(local, meta, stored_ref, keys_ref, values_ref, packed_ref, restored_ref):
+    rows = keys_ref.shape[1]
+    for which, ref in enumerate((keys_ref, values_ref)):
+        for s in range(SEQS):
+            for j in range(KVH):
+                place = ((which * SEQS + s) * KVH + j) * rows
+                packed_ref[place : place + rows, :] = ref[s, :, j * HD : (j + 1) * HD]
+    for s in range(SEQS):
+        for k in range(local):
+            state = stored_ref[meta[6 + s], k].T
+            restored_ref[s, k * N : (k + 1) * N, :] = state
+            if s > 0:
+                place = 2 * SEQS * KVH * rows + ((s - 1) * local + k) * N
+                packed_ref[place : place + N, :] = state.astype(jnp.bfloat16)
+
+
+def combine_kernel(local, meta, keep_ref, got_ref, out_ref):
+    even = meta[0] % 2 == 0
+    second = (meta[0] // 2 * 2 + 1) * TOK
+    closes = start_of(session_at(second + TOK - 1, meta), meta) >= second
+    width = local * N
+    for chip in range(keep_ref.shape[0]):
+        keep = factors_of(keep_ref[chip, width:, :], local)
+        got = factors_of(got_ref[chip, width:, :], local)
+        f0, f1 = jnp.where(even, keep, got), jnp.where(even, got, keep)
+        out_ref[chip, width:, :] = factor_rows(jnp.where(closes, f1, f0 * f1))
+        carry = jnp.where(closes, 0.0, f1)
+        for k in range(local):
+            rows = slice(k * N, (k + 1) * N)
+            keep = keep_ref[chip, rows, :].astype(jnp.float32)
+            got = got_ref[chip, rows, :].astype(jnp.float32)
+            s0, s1 = jnp.where(even, keep, got), jnp.where(even, got, keep)
+            out_ref[chip, rows, :] = (carry[k : k + 1] * s0 + s1).astype(jnp.bfloat16)
+
+
+def recurrence_kernel(local, meta, got_ref, restored_ref, out_ref):
+    width = local * N
+    span = 2 * TOK
+    state = [jnp.zeros((N, P_SIZE), jnp.float32) for _ in range(local)]
+    for c in range(got_ref.shape[0]):
+        first = c * span
+        opening = session_at(first, meta)
+        closing = session_at(first + span - 1, meta)
+        opens = start_of(opening, meta) >= first
+        closes = start_of(closing, meta) >= first
+        factor = factors_of(got_ref[c, width:, :], local)
+        for k in range(local):
+            rows = slice(k * N, (k + 1) * N)
+            entering = jnp.where(opens, restored_ref[opening, rows, :], state[k])
+            out_ref[c, rows, :] = entering.astype(jnp.bfloat16)
+            source = jnp.where(closes, restored_ref[closing, rows, :], state[k])
+            state[k] = factor[k : k + 1] * source + got_ref[c, rows, :].astype(jnp.float32)
+
+
+def middle_kernel(local, meta, entering_ref, keep_ref, got_ref, resumed_ref, own_ref, send_ref):
+    even = meta[0] % 2 == 0
+    first = meta[0] // 2 * 2 * TOK
+    second = first + TOK
+    closing = session_at(second - 1, meta)
+    opening = session_at(second, meta)
+    closes = start_of(closing, meta) > first
+    opens = start_of(opening, meta) >= second
+    width = local * N
+    base = resumed_ref.shape[1] - 2 * width
+    closing_row = pl.multiple_of(base + jnp.maximum(closing - 1, 0) * width, width)
+    opening_row = pl.multiple_of(base + jnp.maximum(opening - 1, 0) * width, width)
+    for chip in range(entering_ref.shape[0]):
+        f0 = jnp.where(
+            even,
+            factors_of(keep_ref[chip, width:, :], local),
+            factors_of(got_ref[chip, width:, :], local),
+        )
+        closing_state = resumed_ref[chip, pl.ds(closing_row, width), :].astype(jnp.float32)
+        opening_state = resumed_ref[chip, pl.ds(opening_row, width), :].astype(jnp.float32)
+        for k in range(local):
+            rows = slice(k * N, (k + 1) * N)
+            entering = entering_ref[chip, rows, :].astype(jnp.float32)
+            s0 = jnp.where(
+                even, keep_ref[chip, rows, :].astype(jnp.float32), got_ref[chip, rows, :].astype(jnp.float32)
+            )
+            middle = f0[k : k + 1] * jnp.where(closes, closing_state[rows], entering) + s0
+            middle = jnp.where(opens, opening_state[rows], middle)
+            own_ref[chip, rows, :] = jnp.where(even, entering, middle).astype(jnp.bfloat16)
+            send_ref[chip, rows, :] = jnp.where(even, middle, entering).astype(jnp.bfloat16)
 
 
 def intra_kernel(meta, skip, x_ref, dl_ref, step_ref, write_ref, read_ref, out_ref, run_s, step_s):
@@ -182,47 +308,11 @@
     )(meta, skip, x, rates, steps, writes, reads)
 
 
-def recurrence_kernel(local, meta, got_ref, restored_ref, out_ref):
-    width = local * N
-    state = [jnp.zeros((N, P_SIZE), jnp.float32) for _ in range(local)]
-    for c in range(got_ref.shape[0]):
-        first = c * TOK
-        opening = session_at(first, meta)
-        closing = session_at(first + TOK - 1, meta)
-        opens = start_of(opening, meta) >= first
-        closes = start_of(closing, meta) >= first
-        for k in range(local):
-            rows = slice(k * N, (k + 1) * N)
-            entering = jnp.where(opens, restored_ref[opening, rows, :], state[k])
-            out_ref[c, rows, :] = entering.astype(jnp.bfloat16)
-            source = jnp.where(closes, restored_ref[closing, rows, :], state[k])
-            factor = got_ref[c, width : width + EXTRA, :].astype(jnp.float32)
-            decay = factor[k : k + 1] + factor[local + k : local + k + 1]
-            state[k] = decay * source + got_ref[c, rows, :].astype(jnp.float32)
-
-
-def recurrence(meta, got, restored, local):
-    owners = got.shape[0]
-    return pl.pallas_call(
-        functools.partial(recurrence_kernel, local),
-        out_shape=jax.ShapeDtypeStruct((owners, local * N, P_SIZE), jnp.bfloat16),
-        grid_spec=pltpu.PrefetchScalarGridSpec(
-            num_scalar_prefetch=1,
-            grid=(1,),
-            in_specs=[
-                pl.BlockSpec(got.shape, lambda i, m: (0, 0, 0)),
-                pl.BlockSpec(restored.shape, lambda i, m: (0, 0, 0)),
-            ],
-            out_specs=pl.BlockSpec((owners, local * N, P_SIZE), lambda i, m: (0, 0, 0)),
-        ),
-        compiler_params=params(),
-        cost_estimate=pl.CostEstimate(flops=1 << 21, bytes_accessed=3 << 20, transcendentals=0),
-        name="recurrence",
-    )(meta, got, restored)
-
-
-def finish_kernel(local, meta, part_ref, dl_ref, step_ref, read_ref, a_ref, b_ref, out_ref, factor_s):
+def finish_kernel(
+    local, meta, part_ref, dl_ref, step_ref, read_ref, own_ref, other_ref, mine_ref, theirs_ref, out_ref, factor_s
+):
     step = pl.program_id(0)
+    even = meta[0] % 2 == 0
     r = last_start(meta)
 
     @pl.when(step == 0)
@@ -241,19 +331,31 @@
         right = jnp.where(resumed, reads, 0.0)
         reads = jnp.concatenate([left, right], axis=1).astype(jnp.bfloat16)
         for k in range(group * HEADS_PER, (group + 1) * HEADS_PER):
+            chip, half = k // (2 * local), k // local % 2
             rows = slice((k % local) * N, (k % local + 1) * N)
-            states = jnp.concatenate([a_ref[k // local, rows, :], b_ref[k // local, 0, rows, :]], axis=0)
+            own = even if half == 0 else jnp.logical_not(even)
+            states = jnp.concatenate(
+                [
+                    jnp.where(own, own_ref[chip, rows, :], other_ref[chip, rows, :]),
+                    jnp.where(own, mine_ref[chip, rows, :], theirs_ref[chip, rows, :]),
+                ],
+                axis=0,
+            )
             carried = jnp.dot(reads, states, preferred_element_type=jnp.float32)
             place = slice(k * P_SIZE, (k + 1) * P_SIZE)
             out_ref[:, place] = (part_ref[:, place] + factor[:, k : k + 1] * carried).astype(jnp.bfloat16)
 
 
-def finish(meta, part, rates, steps, reads, entering, resumed, local):
-    owners = PAIR // local
+def finish(meta, part, rates, steps, reads, own, other, mine, theirs, local):
+    chips = PAIR // (2 * local)
+    width = local * N
+    ahead = mine.shape[1] // width - 2
 
     def resumed_index(i, m):
-        return (i, jnp.maximum(session_at(m[0] * TOK + TOK - 1, m) - 1, 0), 0, 0)
-
+        return (i, ahead + jnp.maximum(session_at(m[0] * TOK + TOK - 1, m) - 1, 0), 0)
+
+    states = pl.BlockSpec((chips, width, P_SIZE), lambda i, m: (i, 0, 0))
+    resumed = pl.BlockSpec((chips, width, P_SIZE), resumed_index)
     return pl.pallas_call(
         functools.partial(finish_kernel, local),
         out_shape=jax.ShapeDtypeStruct((TOK, H * P_SIZE), jnp.bfloat16),
@@ -265,8 +367,10 @@
                 pl.BlockSpec((TOK, H), lambda i, m: (0, 0)),
                 pl.BlockSpec((TOK, H), lambda i, m: (0, 0)),
                 pl.BlockSpec((TOK, 2 * N), lambda i, m: (0, i)),
-                pl.BlockSpec((owners, local * N, P_SIZE), lambda i, m: (i, 0, 0)),
-                pl.BlockSpec((owners, 1, local * N, P_SIZE), resumed_index),
+                states,
+                states,
+                resumed,
+                resumed,
             ],
             out_specs=pl.BlockSpec((TOK, PAIR * P_SIZE), lambda i, m: (0, i)),
             scratch_shapes=[pltpu.VMEM((H, TOK), jnp.float32)],
@@ -276,13 +380,13 @@
             flops=2 * H * TOK * TOK * P_SIZE, bytes_accessed=9 << 20, transcendentals=H * TOK
         ),
         name="finish",
-    )(meta, part, rates, steps, reads, entering, resumed)
+    )(meta, part, rates, steps, reads, own, other, mine, theirs)
 
 
 def attend_kernel(
-    meta, q_ref, band4, band3, band2, band1, band0, ka_ref, va_ref, kb_ref, vb_ref, sk_ref, sv_ref,
-    out_ref, key_s, value_s,
+    meta, q_ref, band4, band3, band2, band1, band0, *refs,
 ):
+    history_refs, (sk_ref, sv_ref, out_ref, key_s, value_s) = refs[:8], refs[8:]
     factor = 1.0 / math.sqrt(HD)
     first = meta[0] * TOK
     r = last_start(meta)
@@ -291,17 +395,23 @@
     bands = (band4, band3, band2, band1, band0)
     length = (REACH + 1) * TOK
 
-    def one_session(session, hk_ref, hv_ref, resuming, needed):
+    def one_session(session, hk_mine, hv_mine, hk_theirs, hv_theirs, resuming, needed):
         start = start_of(session, meta) - first + WINDOW
         oldest = start - WINDOW + jnp.maximum(SINKS + WINDOW - meta[3 + session], 0)
 
         @pl.when(needed & (start > 0))
         def _():
             row = lax.broadcasted_iota(jnp.int32, (length, WINDOW), 0)
-            place = lax.broadcasted_iota(jnp.int32, (length, WINDOW), 1)
-            moved = (place == row - start + WINDOW).astype(jnp.bfloat16)
-            keys = hk_ref[:, 0, 0].reshape(WINDOW, HD)
-            values = hv_ref[:, 0, 0].reshape(WINDOW, HD)
+            chips, share, _ = hk_mine.shape
+            index = lax.broadcasted_iota(jnp.int32, (1, WINDOW), 1)
+            second = (index >= WINDOW // 2).astype(jnp.int32)
+            index = index - second * (WINDOW // 2)
+            core = (meta[0] + second) % 2
+            place = (2 * (index // share) + core) * share + index % share
+            moved = (row == place + start - WINDOW).astype(jnp.bfloat16)
+            half = (WINDOW // 2, HD)
+            keys = jnp.concatenate([hk_mine[...].reshape(half), hk_theirs[...].reshape(half)], axis=0)
+            values = jnp.concatenate([hv_mine[...].reshape(half), hv_theirs[...].reshape(half)], axis=0)
             history = jnp.dot(
                 moved, jnp.concatenate([keys, values], axis=1), preferred_element_type=jnp.float32
             )
@@ -361,19 +471,21 @@
                         result = jnp.where(index >= r, result, before)
                     out_ref[tokens, lanes] = result.astype(jnp.bfloat16)
 
-    one_session(opening, ka_ref, va_ref, False, r > 0)
-    one_session(closing, kb_ref, vb_ref, True, r >= 0)
-
-
-def attend(meta, queries, bands, history, sink_keys, sink_values):
-    owners, _, _, rows, _ = history.shape
+    one_session(opening, *history_refs[:4], False, r > 0)
+    one_session(closing, *history_refs[4:], True, r >= 0)
+
+
+def attend(meta, queries, bands, mine, theirs, sink_keys, sink_values):
+    chips = mine.shape[0]
+    share = WINDOW // (2 * chips)
     lanes = QH // KVH * HD
 
     def history_spec(which, last):
         def index(j, m):
-            return (0, which, session_at(m[0] * TOK + (TOK - 1 if last else 0), m), 0, j)
-
-        return pl.BlockSpec((owners, 1, 1, rows, HD), index)
+            session = session_at(m[0] * TOK + (TOK - 1 if last else 0), m)
+            return (0, (which * SEQS + session) * KVH + j, 0)
+
+        return pl.BlockSpec((chips, share, HD), index)
 
     pad = SEQS, COLUMNS - SPAN, HD
     return pl.pallas_call(
@@ -384,7 +496,8 @@
             grid=(KVH,),
             in_specs=[pl.BlockSpec((TOK, lanes), lambda j, m: (0, j))]
             + [pl.BlockSpec((2, TOK, HD), lambda j, m: (0, 0, j))] * (REACH + 1)
-            + [history_spec(0, False), history_spec(1, False), history_spec(0, True), history_spec(1, True)]
+            + [history_spec(0, False), history_spec(1, False)] * 2
+            + [history_spec(0, True), history_spec(1, True)] * 2
             + [pl.BlockSpec(pad, lambda j, m: (0, 0, j))] * 2,
             out_specs=pl.BlockSpec((TOK, lanes), lambda j, m: (0, j)),
             scratch_shapes=[
@@ -398,7 +511,9 @@
             transcendentals=2 * TOK * QH * COLUMNS,
         ),
         name="attend",
-    )(meta, queries, *bands, history, history, history, history, sink_keys, sink_values)
+    )(
+        meta, queries, *bands, mine, mine, theirs, theirs, mine, mine, theirs, theirs, sink_keys, sink_values
+    )
 
 
 def shifted(block, axis, distance):
@@ -428,42 +543,74 @@
     place = lax.axis_index("ctx")
     group = lax.axis_index("sess")
     groups = lax.axis_size("sess")
+    devices = lax.axis_size("ctx")
     local = saved_states.shape[2]
+    width = local * N
+    chips = devices // 2
+    same_core = [list(range(core, devices, 2)) for core in range(2)]
     lengths = turn_lengths[0]
+    slots = lax.dynamic_slice_in_dim(home_slot, group * SEQS, SEQS, 0)
+    index = (slots // SEQS - group) % groups * SEQS + slots % SEQS
     meta = jnp.concatenate(
-        [jnp.stack([place, lengths[0], lengths[0] + lengths[1]]), history_lengths[0]]
+        [jnp.stack([place, lengths[0], lengths[0] + lengths[1]]), history_lengths[0], index]
     ).astype(jnp.int32)
     x, rates, steps = mamba_input[0], decay_log[0], step_size[0]
     writes, reads = state_write[0], state_read[0]
+
+    def swapped(block):
+        return lax.ppermute(block, "ctx", [(i, i ^ 1) for i in range(devices)])
 
     stored = [saved_states[0]]
     for j in range(1, groups):
         route = [((i + j) % groups, i) for i in range(groups)]
         stored.append(lax.ppermute(saved_states[0], "sess", route))
-    stored = jnp.concatenate(stored, axis=0)
-    slots = lax.dynamic_slice_in_dim(home_slot, group * SEQS, SEQS, 0)
-    index = (slots // SEQS - group) % groups * SEQS + slots % SEQS
-    restored = jnp.concatenate(
-        [lax.dynamic_slice_in_dim(stored, index[s], 1, 0) for s in range(SEQS)], axis=0
+    stored = jnp.concatenate(stored, axis=0).reshape(groups * SEQS, local, P_SIZE, N)
+
+    keep, send = summaries(meta, x, rates, steps, writes, local)
+    got = swapped(send)
+    [total] = whole(
+        functools.partial(combine_kernel, local), "combine", meta, [keep, got], [(keep.shape, jnp.bfloat16)]
     )
-    restored = jnp.swapaxes(restored.reshape(SEQS, local, P_SIZE, N), 2, 3).reshape(SEQS, local * N, P_SIZE)
-
-    history = lax.all_gather(jnp.stack([cache_keys[0], cache_values[0]]), "ctx", axis=0)
+    total = lax.all_to_all(total, "ctx", 0, 0, axis_index_groups=same_core, tiled=True)
+
+    share = cache_keys.shape[2]
+    rows = 2 * SEQS * KVH * share + 2 * width
+    packed, restored = whole(
+        functools.partial(pack_kernel, local),
+        "pack",
+        meta,
+        [stored, cache_keys[0], cache_values[0]],
+        [((rows, P_SIZE), jnp.bfloat16), ((SEQS, width, P_SIZE), jnp.float32)],
+    )
+    mine = lax.all_gather(packed, "ctx", axis=0, axis_index_groups=same_core)
+    theirs = swapped(mine)
+    part = intra(meta, skip_gain, x, rates, steps, writes, reads)
+
+    shape = (chips, width, P_SIZE)
+    [entering] = whole(
+        functools.partial(recurrence_kernel, local), "recurrence", meta, [total, restored], [(shape, jnp.bfloat16)]
+    )
+    entering = lax.all_to_all(entering, "ctx", 0, 0, axis_index_groups=same_core, tiled=True)
+    own, other = whole(
+        functools.partial(middle_kernel, local),
+        "middle",
+        meta,
+        [entering, keep, got, mine],
+        [(shape, jnp.bfloat16), (shape, jnp.bfloat16)],
+        4,
+    )
+    other = swapped(other)
+
     key_value = jnp.stack([turn_keys[0], turn_values[0]])
-    bands = [shifted(key_value, "ctx", k) for k in range(REACH, 0, -1)] + [key_value]
-
-    sent = summaries(meta, x, rates, steps, writes, local)
-    got = lax.all_to_all(sent, "ctx", 0, 0, tiled=True)
-    resumed = lax.all_gather(restored[1:].astype(jnp.bfloat16), "ctx", axis=0)
-    part = intra(meta, skip_gain, x, rates, steps, writes, reads)
-    entering = recurrence(meta, got, restored, local)
-    entering = lax.all_to_all(entering, "ctx", 0, 0, tiled=True)
-
+    two, four = shifted(key_value, "ctx", 2), shifted(key_value, "ctx", 4)
+    even = place % 2 == 0
+    pair = swapped(jnp.where(even, jnp.stack([key_value, two]), jnp.stack([two, four])))
+    bands = [four, pair[1], two, pair[0], key_value]
     sinks = [
         jnp.pad(s[0], ((0, 0), (0, COLUMNS - SPAN - SINKS), (0, 0))) for s in (sink_keys, sink_values)
     ]
-    attended = attend(meta, queries[0], bands, history, *sinks)
-    mixed = finish(meta, part, rates, steps, reads, entering, resumed, local)
+    attended = attend(meta, queries[0], bands, mine, theirs, *sinks)
+    mixed = finish(meta, part, rates, steps, reads, own, other, mine, theirs, local)
     return mixed[None], attended[None]
 
 

time: 169 us -> 173 us (1.024); the launches traced: 168 us -> 173 us
  blocking collectives: 0 us -> 18.4 us
  Pallas kernels: 26.6 us -> 37.5 us
  starting transfers between devices: 22.4 us -> 14.3 us
  local copies, waits for them, and re-layouts: 18.9 us -> 12.2 us
  between operations: 21.5 us -> 15.6 us
  waiting for transfers between devices: 74 us -> 71.4 us
    all_gather x2 -> x1, waiting for transfers between devices: 0.01 us -> 51.8 us  [shards(): mine = lax.all_gather(packed, 'ctx', axis=0, axis_index_groups=same_core)]
    all_to_all x2 -> x1, waiting for transfers between devices: 46.5 us -> 0.01 us  [shards(): lax.all_to_all(entering, 'ctx', 0, 0, axis_index_groups=same_core, tiled=...]
    all_to_all x0 -> x1, blocking collectives: none -> 18.4 us  [shards(): lax.all_to_all(total, 'ctx', 0, 0, axis_index_groups=same_core, tiled=True)]
    ppermute x4 -> x2, waiting for transfers between devices: 24.2 us -> 15.2 us  [shifted(): lax.ppermute(block, axis, [(i - distance, i) for i in devices if i - dist...]
    unnamed x43 -> x41, local copies, waits for them, and re-layouts: 11.4 us -> 4.77 us
    pallas_call x1, Pallas kernels: 12 us -> 17.5 us  [attend(): pl.pallas_call(attend_kernel, out_shape=jax.ShapeDtypeStruct((TOK, QH * H...]
    pallas_call x2 -> x5, Pallas kernels: 3.21 us -> 8.52 us  [the longest x4 5.27 us: whole(): pl.pallas_call(kernel, out_shape=[jax.ShapeDtypeStruct(s, t) for s, t in...]
    all_to_all x2 -> x1, starting transfers between devices: 11.2 us -> 6.31 us  [shards(): lax.all_to_all(entering, 'ctx', 0, 0, axis_index_groups=same_core, tiled=...]
  transfers between devices with their start and end apart: 9 -> 9, of which waited for: 7 -> 4; matrix products, arithmetic and copies ran while one was open for 7% -> 6% of each run, Pallas kernels for 9% -> 7%
where the time goes in v2:
time: 173 us
  waiting for transfers between devices  71.4 us (41%)
  Pallas kernels  37.5 us (22%)
  blocking collectives  18.4 us (11%)
  between operations  15.6 us (9%)
  starting transfers between devices  14.3 us (8%)
  local copies, waits for them, and re-layouts  12.2 us (7%)
  other arithmetic  4.2 us (2%)
    all_gather x1, waiting for transfers between devices, shards(): mine = lax.all_gather(packed, 'ctx', axis=0, axis_index_groups=same_core)  51.8 us
    all_to_all x1, blocking collectives, shards(): lax.all_to_all(total, 'ctx', 0, 0, axis_index_groups=same_core, tiled=True)  18.4 us
    pallas_call x1, Pallas kernels, attend(): pl.pallas_call(attend_kernel, out_shape=jax.ShapeDtypeStruct((TOK, QH * H...  17.5 us
    ppermute x2, waiting for transfers between devices, shifted(): lax.ppermute(block, axis, [(i - distance, i) for i in devices if i - dist...  15.2 us
    ppermute x2, starting transfers between devices, shifted(): lax.ppermute(block, axis, [(i - distance, i) for i in devices if i - dist...  6.76 us
    all_to_all x1, starting transfers between devices, shards(): lax.all_to_all(entering, 'ctx', 0, 0, axis_index_groups=same_core, tiled=...  6.31 us
    pallas_call x1, Pallas kernels, finish(): pl.pallas_call(functools.partial(finish_kernel, local), out_shape=jax.Sha...  6.2 us
    pallas_call x4, Pallas kernels, whole(): pl.pallas_call(kernel, out_shape=[jax.ShapeDtypeStruct(s, t) for s, t in...  5.27 us
  transfers between devices with their start and end apart: 9, of which 4 were waited for; matrix products, arithmetic and copies ran while one was open for 6% of the time, Pallas kernels for 7%

profile of v2, /device:TPU:18, one launch (start us, length us, event | category | flops | bytes accessed | tf_op | source)
XLA Modules:
  0.0 173.5 jit_solution(15513566495478935023)
XLA Ops:
  7.2 0.0 all-gather.3.cloned.1.call-start
  7.2 0.6 collective-permute-start.1
  7.8 1.4 concatenate.12
  9.2 1.3 fusion.3
  11.9 0.8 fusion
  12.6 1.4 concatenate.11.meta
  14.0 0.0 copy-start.12
  14.0 0.0 copy-start.13
  14.0 4.3 %collective-permute-done.1 = f32[3,4,8192]{2,1,0:T(4,128)S(1)} collective-permute-done((f32[3,4,8192]{2,1,0:T(4,128)}, f32[3,4,8192]{2,1,0:T(4,128)S(1)}, u32[]{:S(2)}, u32[]{:S(2)}) %collective-permute-start.1) | collective-permute-done | bytes 393248 | tf_op jit(solution)/shard_map/ppermute | solution.py:566
  18.3 1.3 concatenate.13
  19.6 1.4 pad_maximum_fusion.stored_ref
  21.1 0.0 copy-done.12
  21.1 0.0 copy-done.13
  21.1 1.5 pack.1
  22.6 0.7 copy-done.10
  23.4 0.0 all-gather.3.cloned.1.call-update
  23.4 0.0 copy-done.15
  23.4 0.1 copy.21
  23.5 0.0 copy-done.16
  23.5 0.1 copy.22
  23.6 0.0 copy-done.1
  23.7 0.0 copy-done.8
  23.7 3.3 %summaries.1 = (bf16[8,272,128]{2,1,0:T(8,128)(2,1)S(1)}, bf16[8,272,128]{2,1,0:T(8,128)(2,1)}) custom-call(s32[9]{0:T(128)S(1)} %concatenate.11.meta, bf16[128,8192]{1,0:T(8,128)(2,1)S(1)} %bitcast.32, bf16[128,64]{1,0:T(8,128)(2,1)S(1)} %bitcast.36, bf16[128,64]{1,0:T(8,128)(2,1)S(1)} %bitcast.39, bf16[128,512]{1,0:T(8,128)(2,1)S(1)} %bitcast.44), custom_call_target="tpu_custom_call" | custom-call | flops 134217728 | bytes 3145728 | tf_op jit(solution)/shard_map/summaries/pallas_call | solution.py:119
  26.9 0.0 collective-permute-start
  26.9 51.8 %all-gather.3.cloned.1.call-done = bf16[10240,128]{1,0:T(8,128)(2,1)} async-done(((bf16[1280,128]{1,0:T(8,128)(2,1)}), bf16[10240,128]{1,0:T(8,128)(2,1)}) %all-gather.3.cloned.1.call-update) | async-done | bytes 2621456 | tf_op jit(solution)/shard_map/all_gather | solution.py:585
  78.7 0.0 collective-permute-start.3
  78.7 0.0 collective-permute-done.got_ref
  78.8 0.8 combine.1
  79.6 18.4 %all_to_all.10.got_ref = bf16[8,272,128]{2,1,0:T(8,128)(2,1)S(1)} all-to-all(bf16[8,272,128]{2,1,0:T(8,128)(2,1)S(1)} %combine.1), channel_id=1, replica_groups={{0,2,4,6,8,10,12,14},{1,3,5,7,9,11,13,15},{16,18,20,22,24,26,28,30},{17..., dimensions={0} | all-to-all | bytes 1114112 | tf_op jit(solution)/shard_map/all_to_all | solution.py:574
  97.9 0.0 copy-done.3
  97.9 1.0 copy-done.11
  98.9 0.7 recurrence.1
  99.7 0.0 copy-start.5
  99.7 0.8 copy-done.5
  100.5 6.3 %all-to-all-start.1 = ((bf16[8,256,128]{2,1,0:T(8,128)(2,1)}), bf16[8,256,128]{2,1,0:T(8,128)(2,1)}, u32[]{:S(2)}, u32[]{:S(2)}) async-start(bf16[8,256,128]{2,1,0:T(8,128)(2,1)} %copy-done.5), calls=%async_computation.1 | async-start | bytes 1048576 | tf_op jit(solution)/shard_map/all_to_all | solution.py:593
  106.8 0.9 constant_dynamic-update-slice_fusion.1
  107.7 0.9 constant_dynamic-update-slice_fusion.band0
  108.6 3.4 %collective-permute-start.4 = (bf16[2,128,512]{2,1,0:T(8,128)(2,1)S(1)}, bf16[2,128,512]{2,1,0:T(8,128)(2,1)}, u32[]{:S(2)}, u32[]{:S(2)}) collective-permute-start(bf16[2,128,512]{2,1,0:T(8,128)(2,1)S(1)} %constant_dynamic-update-slice_fusion.band0), channel_id=1, source_target_pairs={{0,4},{1,5},{2,6},{3,7},{4,8},{5,9},{6,10},{7,11},{8,12},{9,13},{1... | collective-permute-start | bytes 786440 | tf_op jit(solution)/shard_map/ppermute | solution.py:521
  112.0 3.4 %collective-permute-start.5 = (bf16[2,128,512]{2,1,0:T(8,128)(2,1)S(1)}, bf16[2,128,512]{2,1,0:T(8,128)(2,1)}, u32[]{:S(2)}, u32[]{:S(2)}) collective-permute-start(bf16[2,128,512]{2,1,0:T(8,128)(2,1)S(1)} %constant_dynamic-update-slice_fusion.band0), channel_id=1, source_target_pairs={{0,2},{1,3},{2,4},{3,5},{4,6},{5,7},{6,8},{7,9},{8,10},{9,11},{10,... | collective-permute-start | bytes 786440 | tf_op jit(solution)/shard_map/ppermute | solution.py:521
  115.4 8.4 %collective-permute-done.4.band4 = bf16[2,128,512]{2,1,0:T(8,128)(2,1)} collective-permute-done((bf16[2,128,512]{2,1,0:T(8,128)(2,1)S(1)}, bf16[2,128,512]{2,1,0:T(8,128)(2,1)}, u32[]{:S(2)}, u32[]{:S(2)}) %collective-permute-start.4) | collective-permute-done | bytes 262176 | tf_op jit(solution)/shard_map/ppermute | solution.py:521
  123.8 6.8 %collective-permute-done.5.band2 = bf16[2,128,512]{2,1,0:T(8,128)(2,1)} collective-permute-done((bf16[2,128,512]{2,1,0:T(8,128)(2,1)S(1)}, bf16[2,128,512]{2,1,0:T(8,128)(2,1)}, u32[]{:S(2)}, u32[]{:S(2)}) %collective-permute-start.5) | collective-permute-done | bytes 262176 | tf_op jit(solution)/shard_map/ppermute | solution.py:521
  130.6 2.0 %maximum_select_fusion = bf16[2,2,128,512]{3,2,1,0:T(8,128)(2,1)} fusion(bf16[1,2,128,512]{3,2,1,0:T(8,128)(2,1)} %bitcast.16, bf16[1,2,128,512]{3,2,1,0:T(8,128)(2,1)S(1)} %bitcast.34, bf16[1,2,128,512]{3,2,1,0:T(8,128)(2,1)} %bitcast.17, pred[]{:T(512)S(6)} %eq.8), kind=kLoop, calls=%fused_computation.1 | loop fusion | flops 786432 | bytes 1310721 | tf_op jit(solution)/shard_map/jit(_where)/select_n | solution.py:607
  132.6 0.0 collective-permute-start.6
  132.6 0.0 all-to-all-done.1.entering_ref
  132.6 0.0 copy-done
  132.6 0.0 copy-start.4
  132.6 1.0 copy-done.4
  133.7 2.2 %middle.1 = (bf16[8,256,128]{2,1,0:T(8,128)(2,1)S(1)}, bf16[8,256,128]{2,1,0:T(8,128)(2,1)S(1)}) custom-call(s32[9]{0:T(128)S(1)} %concatenate.11.meta, bf16[8,256,128]{2,1,0:T(8,128)(2,1)} %all-to-all-done.1.entering_ref, bf16[8,272,128]{2,1,0:T(8,128)(2,1)S(1)} %get-tuple-element.8.keep_ref, bf16[8,272,128]{2,1,0:T(8,128)(2,1)S(1)} %copy-done.4, ...), custom_call_target="tpu_custom_call" | custom-call | flops 2097152 | bytes 4194304 | tf_op jit(solution)/shard_map/middle/pallas_call | solution.py:148
  135.9 0.6 collective-permute-start.2
  136.5 0.0 copy-done.17
  136.5 0.0 copy-done.18
  136.5 0.0 copy-done.14
  136.5 0.0 copy-done.2
  136.5 0.0 copy-done.7
  136.6 0.0 copy-done.9
  136.6 5.2 %intra.1.part_ref = f32[128,8192]{1,0:T(8,128)} custom-call(s32[9]{0:T(128)S(1)} %concatenate.11.meta, f32[64]{0:T(128)S(1)} %copy-done.14, bf16[128,8192]{1,0:T(8,128)(2,1)S(1)} %bitcast.33, bf16[128,64]{1,0:T(8,128)(2,1)S(1)} %bitcast.37, bf16[128,64]{1,0:T(8,128)(2,1)S(1)} %bitcast.40, bf16[128,512]{1,0:T(8,128)(2,1)S(1)} %bitcast.45, ...), custom_call_target="tpu_custom_call" | custom-call | flops 1073741824 | bytes 7340032 | tf_op jit(solution)/shard_map/intra/pallas_call | solution.py:284
  141.8 0.0 collective-permute-done.6
  141.8 1.1 slice_bitcast_fusion
  142.9 0.0 collective-permute-done.2.other_ref
  142.9 0.0 collective-permute-done.3.theirs_ref.refs_2_.refs_3_.refs_6_.refs_7_
  142.9 0.0 copy-start.6
  142.9 6.2 %finish.1 = bf16[128,8192]{1,0:T(8,128)(2,1)} custom-call(s32[9]{0:T(128)S(1)} %concatenate.11.meta, f32[128,8192]{1,0:T(8,128)} %intra.1.part_ref, bf16[128,64]{1,0:T(8,128)(2,1)S(1)} %bitcast.38, bf16[128,64]{1,0:T(8,128)(2,1)S(1)} %bitcast.41, bf16[128,512]{1,0:T(8,128)(2,1)S(1)} %bitcast.43, bf16[8,256,128]{2,1,0:T(8,128)(2,1)S(1)} %get-tuple-element.12.own_ref, ...), custom_call_target="tpu_custom_call" | custom-call | flops 268435456 | bytes 9437184 | tf_op jit(solution)/shard_map/finish/pallas_call | solution.py:359
  149.1 0.0 copy-done.6
  149.1 17.5 %attend.1 = bf16[128,4096]{1,0:T(8,128)(2,1)} custom-call(s32[9]{0:T(128)S(1)} %concatenate.11.meta, bf16[128,4096]{1,0:T(8,128)(2,1)S(1)} %bitcast.35, bf16[2,128,512]{2,1,0:T(8,128)(2,1)} %collective-permute-done.4.band4, bf16[2,128,512]{2,1,0:T(8,128)(2,1)S(1)} %get-tuple-element.15.band3, bf16[2,128,512]{2,1,0:T(8,128)(2,1)} %collective-permute-done.5.band2, ...), custom_call_target="tpu_custom_call" | custom-call | flops 5368709120 | bytes 8388608 | tf_op jit(solution)/shard_map/attend/pallas_call | solution.py:491
  (16 shorter events, 0.1 us)
Async XLA Ops:
  7.2 71.6 %all-gather.3.cloned.1.call-start = ((), (), s32[]{:S(2)}) async-start(), calls=%async_computation.2 | async-start | bytes 2949120 | tf_op jit(solution)/shard_map/all_gather | solution.py:585
  7.2 11.1 %collective-permute-start.1 = (f32[3,4,8192]{2,1,0:T(4,128)}, f32[3,4,8192]{2,1,0:T(4,128)S(1)}, u32[]{:S(2)}, u32[]{:S(2)}) collective-permute-start(f32[3,4,8192]{2,1,0:T(4,128)} %bitcast.50), channel_id=1, source_target_pairs={{16,0},{0,16},{17,1},{1,17},{18,2},{2,18},{19,3},{3,19},{20,4},{4,... | collective-permute-start | bytes 1179656 | tf_op jit(solution)/shard_map/ppermute | solution.py:566
  14.0 7.1 %copy-start.12 = (bf16[1,3,32,512]{3,2,1,0:T(8,128)(2,1)S(1)}, bf16[1,3,32,512]{3,2,1,0:T(8,128)(2,1)}, u32[]{:S(2)}) copy-start(bf16[1,3,32,512]{3,2,1,0:T(8,128)(2,1)} %param.30) | copy-start | bytes 294916
  14.0 7.1 %copy-start.13 = (bf16[1,3,32,512]{3,2,1,0:T(8,128)(2,1)S(1)}, bf16[1,3,32,512]{3,2,1,0:T(8,128)(2,1)}, u32[]{:S(2)}) copy-start(bf16[1,3,32,512]{3,2,1,0:T(8,128)(2,1)} %param.31) | copy-start | bytes 294916
  19.6 3.8 %copy-start.15 = (bf16[1,128,64]{1,2,0:T(8,128)(2,1)S(1)}, bf16[1,128,64]{1,2,0:T(8,128)(2,1)}, u32[]{:S(2)}) copy-start(bf16[1,128,64]{1,2,0:T(8,128)(2,1)} %param.19) | copy-start | bytes 49156
  19.6 3.9 %copy-start.16 = (bf16[1,128,64]{1,2,0:T(8,128)(2,1)S(1)}, bf16[1,128,64]{1,2,0:T(8,128)(2,1)}, u32[]{:S(2)}) copy-start(bf16[1,128,64]{1,2,0:T(8,128)(2,1)} %param.18) | copy-start | bytes 49156
  19.6 4.0 %copy-start.1 = (bf16[1,128,8192]{2,1,0:T(8,128)(2,1)S(1)}, bf16[1,128,8192]{2,1,0:T(8,128)(2,1)}, u32[]{:S(2)}) copy-start(bf16[1,128,8192]{2,1,0:T(8,128)(2,1)} %param.17) | copy-start | bytes 6291460
  19.6 4.0 %copy-start.8 = (bf16[1,128,512]{2,1,0:T(8,128)(2,1)S(1)}, bf16[1,128,512]{2,1,0:T(8,128)(2,1)}, u32[]{:S(2)}) copy-start(bf16[1,128,512]{2,1,0:T(8,128)(2,1)} %param.20) | copy-start | bytes 393220
  22.6 0.7 copy-start.10
  26.9 51.8 %collective-permute-start = (bf16[8,272,128]{2,1,0:T(8,128)(2,1)}, bf16[8,272,128]{2,1,0:T(8,128)(2,1)S(1)}, u32[]{:S(2)}, u32[]{:S(2)}) collective-permute-start(bf16[8,272,128]{2,1,0:T(8,128)(2,1)} %get-tuple-element.9), channel_id=1, source_target_pairs={{0,1},{1,0},{2,3},{3,2},{4,5},{5,4},{6,7},{7,6},{8,9},{9,8},{10,11... | collective-permute-start | bytes 1671176 | tf_op jit(solution)/shard_map/ppermute | solution.py:561
  78.7 64.1 %collective-permute-start.3 = (bf16[8,1280,128]{2,1,0:T(8,128)(2,1)}, bf16[8,1280,128]{2,1,0:T(8,128)(2,1)}, u32[]{:S(2)}, u32[]{:S(2)}) collective-permute-start(bf16[8,1280,128]{2,1,0:T(8,128)(2,1)} %bitcast.25), channel_id=1, source_target_pairs={{0,1},{1,0},{2,3},{3,2},{4,5},{5,4},{6,7},{7,6},{8,9},{9,8},{10,11... | collective-permute-start | bytes 7864328 | tf_op jit(solution)/shard_map/ppermute | solution.py:561
  78.8 19.2 %copy-start.3 = (bf16[8,272,128]{2,1,0:T(8,128)(2,1)}, bf16[8,272,128]{2,1,0:T(8,128)(2,1)S(1)}, u32[]{:S(2)}) copy-start(bf16[8,272,128]{2,1,0:T(8,128)(2,1)S(1)} %collective-permute-done.got_ref) | copy-start | bytes 1671172
  97.9 1.0 copy-start.11
  98.9 33.7 %copy-start = (bf16[10240,128]{1,0:T(8,128)(2,1)S(1)}, bf16[10240,128]{1,0:T(8,128)(2,1)}, u32[]{:S(2)}) copy-start(bf16[10240,128]{1,0:T(8,128)(2,1)} %all-gather.3.cloned.1.call-done) | copy-start | bytes 7864324
  99.7 0.8 copy-start.5
  100.5 32.2 %all-to-all-start.1 = ((bf16[8,256,128]{2,1,0:T(8,128)(2,1)}), bf16[8,256,128]{2,1,0:T(8,128)(2,1)}, u32[]{:S(2)}, u32[]{:S(2)}) async-start(bf16[8,256,128]{2,1,0:T(8,128)(2,1)} %copy-done.5), calls=%async_computation.1 | async-start | bytes 1048576 | tf_op jit(solution)/shard_map/all_to_all | solution.py:593
  108.6 15.2 %collective-permute-start.4 = (bf16[2,128,512]{2,1,0:T(8,128)(2,1)S(1)}, bf16[2,128,512]{2,1,0:T(8,128)(2,1)}, u32[]{:S(2)}, u32[]{:S(2)}) collective-permute-start(bf16[2,128,512]{2,1,0:T(8,128)(2,1)S(1)} %constant_dynamic-update-slice_fusion.band0), channel_id=1, source_target_pairs={{0,4},{1,5},{2,6},{3,7},{4,8},{5,9},{6,10},{7,11},{8,12},{9,13},{1... | collective-permute-start | bytes 786440 | tf_op jit(solution)/shard_map/ppermute | solution.py:521
  112.0 18.6 %collective-permute-start.5 = (bf16[2,128,512]{2,1,0:T(8,128)(2,1)S(1)}, bf16[2,128,512]{2,1,0:T(8,128)(2,1)}, u32[]{:S(2)}, u32[]{:S(2)}) collective-permute-start(bf16[2,128,512]{2,1,0:T(8,128)(2,1)S(1)} %constant_dynamic-update-slice_fusion.band0), channel_id=1, source_target_pairs={{0,2},{1,3},{2,4},{3,5},{4,6},{5,7},{6,8},{7,9},{8,10},{9,11},{10,... | collective-permute-start | bytes 786440 | tf_op jit(solution)/shard_map/ppermute | solution.py:521
  130.6 5.9 %copy-start.17 = (bf16[1,3,4,512]{3,2,1,0:T(4,128)(2,1)S(1)}, bf16[1,3,4,512]{3,2,1,0:T(4,128)(2,1)}, u32[]{:S(2)}) copy-start(bf16[1,3,4,512]{3,2,1,0:T(4,128)(2,1)} %param.32) | copy-start | bytes 36868
  130.6 5.9 %copy-start.18 = (bf16[1,3,4,512]{3,2,1,0:T(4,128)(2,1)S(1)}, bf16[1,3,4,512]{3,2,1,0:T(4,128)(2,1)}, u32[]{:S(2)}) copy-start(bf16[1,3,4,512]{3,2,1,0:T(4,128)(2,1)} %param.33) | copy-start | bytes 36868
  130.6 5.9 %copy-start.14 = (f32[64]{0:T(128)S(1)}, f32[64]{0:T(128)}, u32[]{:S(2)}) copy-start(f32[64]{0:T(128)} %skip.1) | copy-start | bytes 772
  132.6 9.2 %collective-permute-start.6 = (bf16[2,2,128,512]{3,2,1,0:T(8,128)(2,1)}, bf16[2,2,128,512]{3,2,1,0:T(8,128)(2,1)}, u32[]{:S(2)}, u32[]{:S(2)}) collective-permute-start(bf16[2,2,128,512]{3,2,1,0:T(8,128)(2,1)} %maximum_select_fusion), channel_id=1, source_target_pairs={{0,1},{1,0},{2,3},{3,2},{4,5},{5,4},{6,7},{7,6},{8,9},{9,8},{10,11... | collective-permute-start | bytes 1572872 | tf_op jit(solution)/shard_map/ppermute | solution.py:561
  132.6 1.1 copy-start.4
  133.7 2.8 %copy-start.2 = (bf16[1,128,8192]{2,1,0:T(8,128)(2,1)S(1)}, bf16[1,128,8192]{2,1,0:T(8,128)(2,1)}, u32[]{:S(2)}) copy-start(bf16[1,128,8192]{2,1,0:T(8,128)(2,1)} %param.17) | copy-start | bytes 6291460
  133.7 2.9 %copy-start.7 = (bf16[1,128,512]{2,1,0:T(8,128)(2,1)S(1)}, bf16[1,128,512]{2,1,0:T(8,128)(2,1)}, u32[]{:S(2)}) copy-start(bf16[1,128,512]{2,1,0:T(8,128)(2,1)} %param.21) | copy-start | bytes 393220
  133.7 2.9 %copy-start.9 = (bf16[1,128,512]{2,1,0:T(8,128)(2,1)S(1)}, bf16[1,128,512]{2,1,0:T(8,128)(2,1)}, u32[]{:S(2)}) copy-start(bf16[1,128,512]{2,1,0:T(8,128)(2,1)} %param.20) | copy-start | bytes 393220
  135.9 7.0 %collective-permute-start.2 = (bf16[8,256,128]{2,1,0:T(8,128)(2,1)S(1)}, bf16[8,256,128]{2,1,0:T(8,128)(2,1)S(1)}, u32[]{:S(2)}, u32[]{:S(2)}) collective-permute-start(bf16[8,256,128]{2,1,0:T(8,128)(2,1)S(1)} %get-tuple-element.13), channel_id=1, source_target_pairs={{0,1},{1,0},{2,3},{3,2},{4,5},{5,4},{6,7},{7,6},{8,9},{9,8},{10,11... | collective-permute-start | bytes 1572872 | tf_op jit(solution)/shard_map/ppermute | solution.py:561
  142.9 6.2 %copy-start.6 = (bf16[1,128,4096]{2,1,0:T(8,128)(2,1)S(1)}, bf16[1,128,4096]{2,1,0:T(8,128)(2,1)}, u32[]{:S(2)}) copy-start(bf16[1,128,4096]{2,1,0:T(8,128)(2,1)} %param.27) | copy-start | bytes 3145732
Sparse Core Ops, SparseCore 0:
  23.5 55.1 all-gather.2

commit v3 on v2

--- a/solution.py
+++ b/solution.py
@@ -1,4 +1,3 @@
-import functools
 import math
 
 import jax
@@ -31,17 +30,30 @@
 NEG = -1e30
 
 
-def session_at(position, meta):
-    return (position >= meta[1]).astype(jnp.int32) + (position >= meta[2]).astype(jnp.int32)
-
-
-def start_of(session, meta):
-    return jnp.where(session == 0, 0, jnp.where(session == 1, meta[1], meta[2]))
-
-
-def last_start(meta):
-    first = meta[0] * TOK
-    return jnp.maximum(start_of(session_at(first + TOK - 1, meta), meta) - first, 0)
+class Scalars:
+    def __init__(self, ids, lengths, histories, homes):
+        self.place, self.group = ids[0], ids[1]
+        self.one = lengths[0, 0]
+        self.two = lengths[0, 0] + lengths[0, 1]
+        self.histories, self.homes = histories, homes
+        self.even = self.place % 2 == 0
+
+    def session_at(self, position):
+        return (position >= self.one).astype(jnp.int32) + (position >= self.two).astype(jnp.int32)
+
+    def start_of(self, session):
+        return jnp.where(session == 0, 0, jnp.where(session == 1, self.one, self.two))
+
+    def last_start(self):
+        first = self.place * TOK
+        return jnp.maximum(self.start_of(self.session_at(first + TOK - 1)) - first, 0)
+
+
+def scalars(kernel, *options):
+    def body(ids, lengths, histories, homes, *refs):
+        kernel(*options, Scalars(ids, lengths, histories, homes), *refs)
+
+    return body
 
 
 def params(mib=48):
@@ -66,7 +78,7 @@
     @pl.when(step == 0)
     def _():
         rates, running, steps = running_rows(dl_ref, step_ref)
-        r = last_start(meta)
+        r = meta.last_start()
         lane = lax.broadcasted_iota(jnp.int32, (H, TOK), 1)
         last = running[:, TOK - 1 :]
         base = jnp.sum(jnp.where(lane < r, rates, 0.0), axis=1, keepdims=True)
@@ -74,7 +86,7 @@
         factor_s[...] = jnp.broadcast_to(jnp.exp(last - base), (H, TOK))
         write_s[...] = write_ref[...].astype(jnp.float32).T
 
-    even = meta[0] % 2 == 0
+    even = meta.even
     coef = coef_s[pl.ds(pl.multiple_of(step * PAIR, PAIR), PAIR), :]
     factor = factor_s[pl.ds(pl.multiple_of(step * PAIR, PAIR), PAIR), :]
     writes = write_s[pl.ds(pl.multiple_of(step * 2 * N, 2 * N), 2 * N), :]
@@ -115,18 +127,18 @@
     chips = H // (2 * local)
     rows = local * N + EXTRA
     shape = jax.ShapeDtypeStruct((chips, rows, P_SIZE), jnp.bfloat16)
-    spec = pl.BlockSpec((PAIR // (2 * local), rows, P_SIZE), lambda i, m: (i, 0, 0))
+    spec = pl.BlockSpec((PAIR // (2 * local), rows, P_SIZE), lambda i, *m: (i, 0, 0))
     return pl.pallas_call(
-        functools.partial(summary_kernel, local),
+        scalars(summary_kernel, local),
         out_shape=[shape, shape],
         grid_spec=pltpu.PrefetchScalarGridSpec(
-            num_scalar_prefetch=1,
+            num_scalar_prefetch=4,
             grid=(STEPS,),
             in_specs=[
-                pl.BlockSpec((TOK, PAIR * P_SIZE), lambda i, m: (0, i)),
-                pl.BlockSpec((TOK, H), lambda i, m: (0, 0)),
-                pl.BlockSpec((TOK, H), lambda i, m: (0, 0)),
-                pl.BlockSpec((TOK, G * N), lambda i, m: (0, 0)),
+                pl.BlockSpec((TOK, PAIR * P_SIZE), lambda i, *m: (0, i)),
+                pl.BlockSpec((TOK, H), lambda i, *m: (0, 0)),
+                pl.BlockSpec((TOK, H), lambda i, *m: (0, 0)),
+                pl.BlockSpec((TOK, G * N), lambda i, *m: (0, 0)),
             ],
             out_specs=[spec, spec],
             scratch_shapes=[
@@ -138,18 +150,18 @@
         compiler_params=params(),
         cost_estimate=pl.CostEstimate(flops=2 * H * TOK * N * P_SIZE, bytes_accessed=3 << 20, transcendentals=0),
         name="summaries",
-    )(meta, x, rates, steps, writes)
+    )(*meta, x, rates, steps, writes)
 
 
 def whole(kernel, name, meta, arrays, shapes, size=2):
     def spec(shape):
-        return pl.BlockSpec(shape, lambda i, m: (0,) * len(shape))
+        return pl.BlockSpec(shape, lambda i, *m: (0,) * len(shape))
 
     return pl.pallas_call(
         kernel,
         out_shape=[jax.ShapeDtypeStruct(s, t) for s, t in shapes],
         grid_spec=pltpu.PrefetchScalarGridSpec(
-            num_scalar_prefetch=1,
+            num_scalar_prefetch=4,
             grid=(1,),
             in_specs=[spec(a.shape) for a in arrays],
             out_specs=[spec(s) for s, _ in shapes],
@@ -157,29 +169,38 @@
         compiler_params=params(),
         cost_estimate=pl.CostEstimate(flops=1 << 21, bytes_accessed=size << 20, transcendentals=0),
         name=name,
-    )(meta, *arrays)
-
-
-def pack_kernel(local, meta, stored_ref, keys_ref, values_ref, packed_ref, restored_ref):
+    )(*meta, *arrays)
+
+
+def history_kernel(meta, keys_ref, values_ref, packed_ref):
     rows = keys_ref.shape[1]
     for which, ref in enumerate((keys_ref, values_ref)):
         for s in range(SEQS):
             for j in range(KVH):
                 place = ((which * SEQS + s) * KVH + j) * rows
-                packed_ref[place : place + rows, :] = ref[s, :, j * HD : (j + 1) * HD]
+                packed_ref[0, place : place + rows, :] = ref[s, :, j * HD : (j + 1) * HD]
+
+
+def restore_kernel(local, meta, *refs):
+    stored, (resumed_ref, restored_ref) = refs[:-2], refs[-2:]
+    groups = len(stored)
     for s in range(SEQS):
+        slot = meta.homes[meta.group * SEQS + s]
+        source = (slot // SEQS - meta.group + groups) % groups
         for k in range(local):
-            state = stored_ref[meta[6 + s], k].T
-            restored_ref[s, k * N : (k + 1) * N, :] = state
-            if s > 0:
-                place = 2 * SEQS * KVH * rows + ((s - 1) * local + k) * N
-                packed_ref[place : place + N, :] = state.astype(jnp.bfloat16)
+            state = stored[0][slot % SEQS, k]
+            for j in range(1, groups):
+                state = jnp.where(source == j, stored[j][slot % SEQS, k], state)
+            restored_ref[s, k * N : (k + 1) * N, :] = state.T
+    for chip in range(resumed_ref.shape[0]):
+        closing = meta.session_at((chip + 1) * 2 * TOK - 1)
+        resumed_ref[chip] = restored_ref[closing].astype(jnp.bfloat16)
 
 
 def combine_kernel(local, meta, keep_ref, got_ref, out_ref):
-    even = meta[0] % 2 == 0
-    second = (meta[0] // 2 * 2 + 1) * TOK
-    closes = start_of(session_at(second + TOK - 1, meta), meta) >= second
+    even = meta.even
+    second = (meta.place // 2 * 2 + 1) * TOK
+    closes = meta.start_of(meta.session_at(second + TOK - 1)) >= second
     width = local * N
     for chip in range(keep_ref.shape[0]):
         keep = factors_of(keep_ref[chip, width:, :], local)
@@ -201,10 +222,10 @@
     state = [jnp.zeros((N, P_SIZE), jnp.float32) for _ in range(local)]
     for c in range(got_ref.shape[0]):
         first = c * span
-        opening = session_at(first, meta)
-        closing = session_at(first + span - 1, meta)
-        opens = start_of(opening, meta) >= first
-        closes = start_of(closing, meta) >= first
+        opening = meta.session_at(first)
+        closing = meta.session_at(first + span - 1)
+        opens = meta.start_of(opening) >= first
+        closes = meta.start_of(closing) >= first
         factor = factors_of(got_ref[c, width:, :], local)
         for k in range(local):
             rows = slice(k * N, (k + 1) * N)
@@ -215,33 +236,28 @@
 
 
 def middle_kernel(local, meta, entering_ref, keep_ref, got_ref, resumed_ref, own_ref, send_ref):
-    even = meta[0] % 2 == 0
-    first = meta[0] // 2 * 2 * TOK
+    even = meta.even
+    first = meta.place // 2 * 2 * TOK
     second = first + TOK
-    closing = session_at(second - 1, meta)
-    opening = session_at(second, meta)
-    closes = start_of(closing, meta) > first
-    opens = start_of(opening, meta) >= second
+    start = meta.start_of(meta.session_at(second + TOK - 1))
+    closes = (start > first) & (start < second)
+    opens = start == second
     width = local * N
-    base = resumed_ref.shape[1] - 2 * width
-    closing_row = pl.multiple_of(base + jnp.maximum(closing - 1, 0) * width, width)
-    opening_row = pl.multiple_of(base + jnp.maximum(opening - 1, 0) * width, width)
     for chip in range(entering_ref.shape[0]):
         f0 = jnp.where(
             even,
             factors_of(keep_ref[chip, width:, :], local),
             factors_of(got_ref[chip, width:, :], local),
         )
-        closing_state = resumed_ref[chip, pl.ds(closing_row, width), :].astype(jnp.float32)
-        opening_state = resumed_ref[chip, pl.ds(opening_row, width), :].astype(jnp.float32)
+        resumed = resumed_ref[chip].astype(jnp.float32)
         for k in range(local):
             rows = slice(k * N, (k + 1) * N)
             entering = entering_ref[chip, rows, :].astype(jnp.float32)
             s0 = jnp.where(
                 even, keep_ref[chip, rows, :].astype(jnp.float32), got_ref[chip, rows, :].astype(jnp.float32)
             )
-            middle = f0[k : k + 1] * jnp.where(closes, closing_state[rows], entering) + s0
-            middle = jnp.where(opens, opening_state[rows], middle)
+            middle = f0[k : k + 1] * jnp.where(closes, resumed[rows], entering) + s0
+            middle = jnp.where(opens, resumed[rows], middle)
             own_ref[chip, rows, :] = jnp.where(even, entering, middle).astype(jnp.bfloat16)
             send_ref[chip, rows, :] = jnp.where(even, middle, entering).astype(jnp.bfloat16)
 
@@ -259,7 +275,7 @@
     running = run_s[heads, :]
     sizes = step_s[heads, :]
     columns = running.T
-    r = last_start(meta)
+    r = meta.last_start()
     t = lax.broadcasted_iota(jnp.int32, (TOK, TOK), 0)
     u = lax.broadcasted_iota(jnp.int32, (TOK, TOK), 1)
     causal = (u <= t) & ((u >= r) | (t < r))
@@ -282,19 +298,19 @@
 
 def intra(meta, skip, x, rates, steps, writes, reads):
     return pl.pallas_call(
-        intra_kernel,
+        scalars(intra_kernel),
         out_shape=jax.ShapeDtypeStruct((TOK, H * P_SIZE), jnp.float32),
         grid_spec=pltpu.PrefetchScalarGridSpec(
-            num_scalar_prefetch=2,
+            num_scalar_prefetch=5,
             grid=(STEPS,),
             in_specs=[
-                pl.BlockSpec((TOK, PAIR * P_SIZE), lambda i, m, s: (0, i)),
-                pl.BlockSpec((TOK, H), lambda i, m, s: (0, 0)),
-                pl.BlockSpec((TOK, H), lambda i, m, s: (0, 0)),
-                pl.BlockSpec((TOK, 2 * N), lambda i, m, s: (0, i)),
-                pl.BlockSpec((TOK, 2 * N), lambda i, m, s: (0, i)),
+                pl.BlockSpec((TOK, PAIR * P_SIZE), lambda i, *m: (0, i)),
+                pl.BlockSpec((TOK, H), lambda i, *m: (0, 0)),
+                pl.BlockSpec((TOK, H), lambda i, *m: (0, 0)),
+                pl.BlockSpec((TOK, 2 * N), lambda i, *m: (0, i)),
+                pl.BlockSpec((TOK, 2 * N), lambda i, *m: (0, i)),
             ],
-            out_specs=pl.BlockSpec((TOK, PAIR * P_SIZE), lambda i, m, s: (0, i)),
+            out_specs=pl.BlockSpec((TOK, PAIR * P_SIZE), lambda i, *m: (0, i)),
             scratch_shapes=[
                 pltpu.VMEM((H, TOK), jnp.float32),
                 pltpu.VMEM((H, TOK), jnp.float32),
@@ -305,15 +321,15 @@
             flops=8 * H * TOK * TOK * P_SIZE, bytes_accessed=7 << 20, transcendentals=H * TOK * TOK
         ),
         name="intra",
-    )(meta, skip, x, rates, steps, writes, reads)
+    )(*meta, skip, x, rates, steps, writes, reads)
 
 
 def finish_kernel(
     local, meta, part_ref, dl_ref, step_ref, read_ref, own_ref, other_ref, mine_ref, theirs_ref, out_ref, factor_s
 ):
     step = pl.program_id(0)
-    even = meta[0] % 2 == 0
-    r = last_start(meta)
+    even = meta.even
+    r = meta.last_start()
 
     @pl.when(step == 0)
     def _():
@@ -349,30 +365,24 @@
 def finish(meta, part, rates, steps, reads, own, other, mine, theirs, local):
     chips = PAIR // (2 * local)
     width = local * N
-    ahead = mine.shape[1] // width - 2
-
-    def resumed_index(i, m):
-        return (i, ahead + jnp.maximum(session_at(m[0] * TOK + TOK - 1, m) - 1, 0), 0)
-
-    states = pl.BlockSpec((chips, width, P_SIZE), lambda i, m: (i, 0, 0))
-    resumed = pl.BlockSpec((chips, width, P_SIZE), resumed_index)
+    states = pl.BlockSpec((chips, width, P_SIZE), lambda i, *m: (i, 0, 0))
     return pl.pallas_call(
-        functools.partial(finish_kernel, local),
+        scalars(finish_kernel, local),
         out_shape=jax.ShapeDtypeStruct((TOK, H * P_SIZE), jnp.bfloat16),
         grid_spec=pltpu.PrefetchScalarGridSpec(
-            num_scalar_prefetch=1,
+            num_scalar_prefetch=4,
             grid=(STEPS,),
             in_specs=[
-                pl.BlockSpec((TOK, PAIR * P_SIZE), lambda i, m: (0, i)),
-                pl.BlockSpec((TOK, H), lambda i, m: (0, 0)),
-                pl.BlockSpec((TOK, H), lambda i, m: (0, 0)),
-                pl.BlockSpec((TOK, 2 * N), lambda i, m: (0, i)),
+                pl.BlockSpec((TOK, PAIR * P_SIZE), lambda i, *m: (0, i)),
+                pl.BlockSpec((TOK, H), lambda i, *m: (0, 0)),
+                pl.BlockSpec((TOK, H), lambda i, *m: (0, 0)),
+                pl.BlockSpec((TOK, 2 * N), lambda i, *m: (0, i)),
                 states,
                 states,
-                resumed,
-                resumed,
+                states,
+                states,
             ],
-            out_specs=pl.BlockSpec((TOK, PAIR * P_SIZE), lambda i, m: (0, i)),
+            out_specs=pl.BlockSpec((TOK, PAIR * P_SIZE), lambda i, *m: (0, i)),
             scratch_shapes=[pltpu.VMEM((H, TOK), jnp.float32)],
         ),
         compiler_params=params(),
@@ -380,38 +390,41 @@
             flops=2 * H * TOK * TOK * P_SIZE, bytes_accessed=9 << 20, transcendentals=H * TOK
         ),
         name="finish",
-    )(meta, part, rates, steps, reads, own, other, mine, theirs)
+    )(*meta, part, rates, steps, reads, own, other, mine, theirs)
 
 
 def attend_kernel(
     meta, q_ref, band4, band3, band2, band1, band0, *refs,
 ):
-    history_refs, (sk_ref, sv_ref, out_ref, key_s, value_s) = refs[:8], refs[8:]
+    history_refs, (sk_ref, sv_ref, out_ref, key_s, value_s) = refs[:16], refs[16:]
     factor = 1.0 / math.sqrt(HD)
-    first = meta[0] * TOK
-    r = last_start(meta)
-    opening = session_at(first, meta)
-    closing = session_at(first + TOK - 1, meta)
+    first = meta.place * TOK
+    r = meta.last_start()
+    opening = meta.session_at(first)
+    closing = meta.session_at(first + TOK - 1)
     bands = (band4, band3, band2, band1, band0)
     length = (REACH + 1) * TOK
 
-    def one_session(session, hk_mine, hv_mine, hk_theirs, hv_theirs, resuming, needed):
-        start = start_of(session, meta) - first + WINDOW
-        oldest = start - WINDOW + jnp.maximum(SINKS + WINDOW - meta[3 + session], 0)
+    def one_session(session, key_refs, value_refs, resuming, needed):
+        start = meta.start_of(session) - first + WINDOW
+        oldest = start - WINDOW + jnp.maximum(SINKS + WINDOW - meta.histories[0, session], 0)
 
         @pl.when(needed & (start > 0))
         def _():
             row = lax.broadcasted_iota(jnp.int32, (length, WINDOW), 0)
-            chips, share, _ = hk_mine.shape
+            chips, share, _ = key_refs[0].shape
             index = lax.broadcasted_iota(jnp.int32, (1, WINDOW), 1)
-            second = (index >= WINDOW // 2).astype(jnp.int32)
-            index = index - second * (WINDOW // 2)
-            core = (meta[0] + second) % 2
-            place = (2 * (index // share) + core) * share + index % share
+            piece, index = index // (WINDOW // 4), index % (WINDOW // 4)
+            near, row_in = index // share, index % share
+            far, bits = jnp.zeros_like(near), chips.bit_length() - 1
+            for k in range(bits):
+                far = far + ((near // (1 << k)) % 2) * (1 << (bits - 1 - k))
+            device = meta.place ^ (piece // 2 + piece % 2 * 2 + far * 4)
+            place = device * share + row_in
             moved = (row == place + start - WINDOW).astype(jnp.bfloat16)
-            half = (WINDOW // 2, HD)
-            keys = jnp.concatenate([hk_mine[...].reshape(half), hk_theirs[...].reshape(half)], axis=0)
-            values = jnp.concatenate([hv_mine[...].reshape(half), hv_theirs[...].reshape(half)], axis=0)
+            part = (WINDOW // 4, HD)
+            keys = jnp.concatenate([ref[...].reshape(part) for ref in key_refs], axis=0)
+            values = jnp.concatenate([ref[...].reshape(part) for ref in value_refs], axis=0)
             history = jnp.dot(
                 moved, jnp.concatenate([keys, values], axis=1), preferred_element_type=jnp.float32
             )
@@ -471,35 +484,38 @@
                         result = jnp.where(index >= r, result, before)
                     out_ref[tokens, lanes] = result.astype(jnp.bfloat16)
 
-    one_session(opening, *history_refs[:4], False, r > 0)
-    one_session(closing, *history_refs[4:], True, r >= 0)
-
-
-def attend(meta, queries, bands, mine, theirs, sink_keys, sink_values):
-    chips = mine.shape[0]
-    share = WINDOW // (2 * chips)
+    one_session(opening, history_refs[0:4], history_refs[4:8], False, r > 0)
+    one_session(closing, history_refs[8:12], history_refs[12:], True, r >= 0)
+
+
+def attend(meta, queries, bands, pieces, sink_keys, sink_values):
+    chips = pieces[0].shape[0]
+    share = WINDOW // (4 * chips)
     lanes = QH // KVH * HD
 
     def history_spec(which, last):
-        def index(j, m):
-            session = session_at(m[0] * TOK + (TOK - 1 if last else 0), m)
+        def index(j, *m):
+            known = Scalars(*m)
+            session = known.session_at(known.place * TOK + (TOK - 1 if last else 0))
             return (0, (which * SEQS + session) * KVH + j, 0)
 
         return pl.BlockSpec((chips, share, HD), index)
 
     pad = SEQS, COLUMNS - SPAN, HD
     return pl.pallas_call(
-        attend_kernel,
+        scalars(attend_kernel),
         out_shape=jax.ShapeDtypeStruct((TOK, QH * HD), jnp.bfloat16),
         grid_spec=pltpu.PrefetchScalarGridSpec(
-            num_scalar_prefetch=1,
+            num_scalar_prefetch=4,
             grid=(KVH,),
-            in_specs=[pl.BlockSpec((TOK, lanes), lambda j, m: (0, j))]
-            + [pl.BlockSpec((2, TOK, HD), lambda j, m: (0, 0, j))] * (REACH + 1)
-            + [history_spec(0, False), history_spec(1, False)] * 2
-            + [history_spec(0, True), history_spec(1, True)] * 2
-            + [pl.BlockSpec(pad, lambda j, m: (0, 0, j))] * 2,
-            out_specs=pl.BlockSpec((TOK, lanes), lambda j, m: (0, j)),
+            in_specs=[pl.BlockSpec((TOK, lanes), lambda j, *m: (0, j))]
+            + [pl.BlockSpec((2, TOK, HD), lambda j, *m: (0, 0, j))] * (REACH + 1)
+            + [history_spec(0, False)] * 4
+            + [history_spec(1, False)] * 4
+            + [history_spec(0, True)] * 4
+            + [history_spec(1, True)] * 4
+            + [pl.BlockSpec(pad, lambda j, *m: (0, 0, j))] * 2,
+            out_specs=pl.BlockSpec((TOK, lanes), lambda j, *m: (0, j)),
             scratch_shapes=[
                 pltpu.VMEM(((REACH + 1) * TOK, HD), jnp.bfloat16),
                 pltpu.VMEM(((REACH + 1) * TOK, HD), jnp.bfloat16),
@@ -512,7 +528,7 @@
         ),
         name="attend",
     )(
-        meta, queries, *bands, mine, mine, theirs, theirs, mine, mine, theirs, theirs, sink_keys, sink_values
+        *meta, queries, *bands, *pieces, *pieces, *pieces, *pieces, sink_keys, sink_values
     )
 
 
@@ -548,68 +564,77 @@
     width = local * N
     chips = devices // 2
     same_core = [list(range(core, devices, 2)) for core in range(2)]
-    lengths = turn_lengths[0]
-    slots = lax.dynamic_slice_in_dim(home_slot, group * SEQS, SEQS, 0)
-    index = (slots // SEQS - group) % groups * SEQS + slots % SEQS
-    meta = jnp.concatenate(
-        [jnp.stack([place, lengths[0], lengths[0] + lengths[1]]), history_lengths[0], index]
-    ).astype(jnp.int32)
+    meta = (jnp.stack([place, group]).astype(jnp.int32), turn_lengths, history_lengths, home_slot)
     x, rates, steps = mamba_input[0], decay_log[0], step_size[0]
     writes, reads = state_write[0], state_read[0]
-
-    def swapped(block):
-        return lax.ppermute(block, "ctx", [(i, i ^ 1) for i in range(devices)])
+    shape = (chips, width, P_SIZE)
+
+    def apart(block, distance):
+        return lax.ppermute(block, "ctx", [(i, i ^ distance) for i in range(devices)])
+
+    def exchanged(block):
+        return lax.all_to_all(block, "ctx", 0, 0, axis_index_groups=same_core, tiled=True)
 
     stored = [saved_states[0]]
     for j in range(1, groups):
         route = [((i + j) % groups, i) for i in range(groups)]
         stored.append(lax.ppermute(saved_states[0], "sess", route))
-    stored = jnp.concatenate(stored, axis=0).reshape(groups * SEQS, local, P_SIZE, N)
 
     keep, send = summaries(meta, x, rates, steps, writes, local)
-    got = swapped(send)
-    [total] = whole(
-        functools.partial(combine_kernel, local), "combine", meta, [keep, got], [(keep.shape, jnp.bfloat16)]
+    got = apart(send, 1)
+    [total] = whole(scalars(combine_kernel, local), "combine", meta, [keep, got], [(keep.shape, jnp.bfloat16)])
+    total = exchanged(total)
+
+    stored = [block.reshape(SEQS, local, P_SIZE, N) for block in stored]
+    resumed, restored = whole(
+        scalars(restore_kernel, local),
+        "restore",
+        meta,
+        stored,
+        [(shape, jnp.bfloat16), ((SEQS, width, P_SIZE), jnp.float32)],
     )
-    total = lax.all_to_all(total, "ctx", 0, 0, axis_index_groups=same_core, tiled=True)
+    mine = exchanged(resumed)
+    theirs = apart(mine, 1)
+    part = intra(meta, skip_gain, x, rates, steps, writes, reads)
 
     share = cache_keys.shape[2]
-    rows = 2 * SEQS * KVH * share + 2 * width
-    packed, restored = whole(
-        functools.partial(pack_kernel, local),
-        "pack",
+    [history] = whole(
+        scalars(history_kernel),
+        "history",
         meta,
-        [stored, cache_keys[0], cache_values[0]],
-        [((rows, P_SIZE), jnp.bfloat16), ((SEQS, width, P_SIZE), jnp.float32)],
+        [cache_keys[0], cache_values[0]],
+        [((1, 2 * SEQS * KVH * share, HD), jnp.bfloat16)],
     )
-    mine = lax.all_gather(packed, "ctx", axis=0, axis_index_groups=same_core)
-    theirs = swapped(mine)
-    part = intra(meta, skip_gain, x, rates, steps, writes, reads)
-
-    shape = (chips, width, P_SIZE)
+    distance = devices // 2
+    while distance > 2:
+        history = jnp.concatenate([history, apart(history, distance)], axis=0)
+        distance //= 2
+    beside = apart(history, 2)
+    pieces = [history, beside, apart(history, 1), apart(beside, 1)]
+
     [entering] = whole(
-        functools.partial(recurrence_kernel, local), "recurrence", meta, [total, restored], [(shape, jnp.bfloat16)]
+        scalars(recurrence_kernel, local), "recurrence", meta, [total, restored], [(shape, jnp.bfloat16)]
     )
-    entering = lax.all_to_all(entering, "ctx", 0, 0, axis_index_groups=same_core, tiled=True)
+    entering = exchanged(entering)
     own, other = whole(
-        functools.partial(middle_kernel, local),
+        scalars(middle_kernel, local),
         "middle",
         meta,
         [entering, keep, got, mine],
         [(shape, jnp.bfloat16), (shape, jnp.bfloat16)],
         4,
     )
-    other = swapped(other)
+    other = apart(other, 1)
 
     key_value = jnp.stack([turn_keys[0], turn_values[0]])
     two, four = shifted(key_value, "ctx", 2), shifted(key_value, "ctx", 4)
     even = place % 2 == 0
-    pair = swapped(jnp.where(even, jnp.stack([key_value, two]), jnp.stack([two, four])))
+    pair = apart(jnp.where(even, jnp.stack([key_value, two]), jnp.stack([two, four])), 1)
     bands = [four, pair[1], two, pair[0], key_value]
     sinks = [
         jnp.pad(s[0], ((0, 0), (0, COLUMNS - SPAN - SINKS), (0, 0))) for s in (sink_keys, sink_values)
     ]
-    attended = attend(meta, queries[0], bands, mine, theirs, *sinks)
+    attended = attend(meta, queries[0], bands, pieces, *sinks)
     mixed = finish(meta, part, rates, steps, reads, own, other, mine, theirs, local)
     return mixed[None], attended[None]
 

time: 173 us -> 134 us (0.77)
  the two profiles are of different devices: /device:TPU:18 before, /device:TPU:16 now
where the time goes in v3:
time: 134 us; the launch traced here: 135 us
  waiting for transfers between devices  43.1 us (32%)
  Pallas kernels  37.7 us (28%)
  starting transfers between devices  31.1 us (23%)
  local copies, waits for them, and re-layouts  17.4 us (13%)
  other arithmetic  4.94 us (4%)
    ppermute x9, waiting for transfers between devices, apart(): lax.ppermute(block, 'ctx', [(i, i ^ distance) for i in range(devices)])  21.4 us
    all_to_all x3, starting transfers between devices, exchanged(): lax.all_to_all(block, 'ctx', 0, 0, axis_index_groups=same_core, tiled=True)  18.3 us
    pallas_call x1, Pallas kernels, attend(): pl.pallas_call(scalars(attend_kernel), out_shape=jax.ShapeDtypeStruct((TO...  17.2 us
    ppermute x2, waiting for transfers between devices, shifted(): lax.ppermute(block, axis, [(i - distance, i) for i in devices if i - dist...  15.2 us
    unnamed x61, local copies, waits for them, and re-layouts  12.2 us
    ppermute x2, starting transfers between devices, shifted(): lax.ppermute(block, axis, [(i - distance, i) for i in devices if i - dist...  6.76 us
    pallas_call x5, Pallas kernels, whole(): pl.pallas_call(kernel, out_shape=[jax.ShapeDtypeStruct(s, t) for s, t in...  6.72 us
    all_to_all x3, waiting for transfers between devices, exchanged(): lax.all_to_all(block, 'ctx', 0, 0, axis_index_groups=same_core, tiled=True)  6.48 us
  transfers between devices with their start and end apart: 15, of which 6 were waited for; matrix products, arithmetic and copies ran while one was open for 7% of the time, Pallas kernels for 20%

profile of v3, /device:TPU:16, one launch (start us, length us, event | category | flops | bytes accessed | tf_op | source)
XLA Modules:
  0.0 135.1 jit_solution(4741175517488901113)
XLA Ops:
  0.6 0.8 copy.21
  1.5 0.8 copy.22
  2.3 0.1 pad_add_fusion.ids
  2.4 1.6 %copy-done = bf16[1,128,8192]{2,1,0:T(8,128)(2,1)S(1)} copy-done((bf16[1,128,8192]{2,1,0:T(8,128)(2,1)S(1)}, bf16[1,128,8192]{2,1,0:T(8,128)(2,1)}, u32[]{:S(2)}) %copy-start) | copy-done | bytes 2097176
  4.0 0.9 copy-done.9
  4.9 0.7 copy-done.17
  5.5 0.7 copy-done.19
  6.2 0.7 copy-done.21
  6.9 2.3 %summaries.1 = (bf16[8,272,128]{2,1,0:T(8,128)(2,1)S(1)}, bf16[8,272,128]{2,1,0:T(8,128)(2,1)S(1)}) custom-call(s32[2]{0:T(128)S(1)} %pad_add_fusion.ids, s32[1,3]{1,0:T(1,128)S(1)} %copy-done.17, s32[1,3]{1,0:T(1,128)S(1)} %copy-done.19, s32[6]{0:T(128)S(1)} %copy-done.21, bf16[128,8192]{1,0:T(8,128)(2,1)S(1)} %bitcast.22, bf16[128,64]{1,0:T(8,128)(2,1)S(1)} %bitcast.27, ...), custom_call_target="tpu_custom_call" | custom-call | flops 134217728 | bytes 3145728 | tf_op jit(solution)/shard_map/summaries/pallas_call | solution.py:131
  9.2 0.1 collective-permute-start
  9.2 1.9 %collective-permute-done.refs_1_.refs_2_ = bf16[8,272,128]{2,1,0:T(8,128)(2,1)S(1)} collective-permute-done((bf16[8,272,128]{2,1,0:T(8,128)(2,1)S(1)}, bf16[8,272,128]{2,1,0:T(8,128)(2,1)S(1)}, u32[]{:S(2)}, u32[]{:S(2)}) %collective-permute-start) | collective-permute-done | bytes 557088 | tf_op jit(solution)/shard_map/ppermute | solution.py:573
  11.2 1.6 %combine.1 = bf16[8,272,128]{2,1,0:T(8,128)(2,1)} custom-call(s32[2]{0:T(128)S(1)} %pad_add_fusion.ids, s32[1,3]{1,0:T(1,128)S(1)} %copy-done.17, s32[1,3]{1,0:T(1,128)S(1)} %copy-done.19, s32[6]{0:T(128)S(1)} %copy-done.21, bf16[8,272,128]{2,1,0:T(8,128)(2,1)S(1)} %get-tuple-element.8.refs_0_.refs_1_, ...), custom_call_target="tpu_custom_call" | custom-call | flops 2097152 | bytes 2097152 | tf_op jit(solution)/shard_map/combine/pallas_call | solution.py:160
  12.8 0.8 copy-done.2
  13.6 6.2 %all-to-all-start = ((bf16[8,272,128]{2,1,0:T(8,128)(2,1)}), bf16[8,272,128]{2,1,0:T(8,128)(2,1)S(1)}, u32[]{:S(2)}, u32[]{:S(2)}) async-start(bf16[8,272,128]{2,1,0:T(8,128)(2,1)} %combine.1), calls=%async_computation | async-start | bytes 1114112 | tf_op jit(solution)/shard_map/all_to_all | solution.py:576
  19.8 1.5 %collective-permute-start.1 = (f32[3,4,8192]{2,1,0:T(4,128)S(1)}, f32[3,4,8192]{2,1,0:T(4,128)}, u32[]{:S(2)}, u32[]{:S(2)}) collective-permute-start(f32[3,4,8192]{2,1,0:T(4,128)S(1)} %bitcast.39), channel_id=1, source_target_pairs={{16,0},{0,16},{17,1},{1,17},{18,2},{2,18},{19,3},{3,19},{20,4},{4,... | collective-permute-start | bytes 1179656 | tf_op jit(solution)/shard_map/ppermute | solution.py:581
  21.3 0.6 history.1
  21.9 0.1 collective-permute-start.7
  22.0 18.3 %collective-permute-done.7 = bf16[1,768,128]{2,1,0:T(8,128)(2,1)S(1)} collective-permute-done((bf16[1,768,128]{2,1,0:T(8,128)(2,1)S(1)}, bf16[1,768,128]{2,1,0:T(8,128)(2,1)S(1)}, u32[]{:S(2)}, u32[]{:S(2)}) %collective-permute-start.7) | collective-permute-done | bytes 196640 | tf_op jit(solution)/shard_map/ppermute | solution.py:573
  40.3 0.8 pad_maximum_fusion.1
  41.1 2.2 %collective-permute-start.8 = (bf16[2,768,128]{2,1,0:T(8,128)(2,1)}, bf16[2,768,128]{2,1,0:T(8,128)(2,1)}, u32[]{:S(2)}, u32[]{:S(2)}) collective-permute-start(bf16[2,768,128]{2,1,0:T(8,128)(2,1)} %pad_maximum_fusion.1), channel_id=1, source_target_pairs={{0,4},{1,5},{2,6},{3,7},{4,0},{5,1},{6,2},{7,3},{8,12},{9,13},{10,... | collective-permute-start | bytes 1179656 | tf_op jit(solution)/shard_map/ppermute | solution.py:573
  43.3 0.4 reshape_squeeze.3.refs_0_
  43.7 0.0 collective-permute-done.1
  43.7 1.4 %reshape.7.refs_1_ = f32[3,4,128,64]{3,2,1,0:T(8,128)S(1)} reshape(f32[3,4,8192]{2,1,0:T(4,128)} %collective-permute-done.1) | data formatting | bytes 786432 | tf_op jit(solution)/shard_map/reshape | solution.py:588
  45.1 1.7 %restore.1 = (bf16[8,256,128]{2,1,0:T(8,128)(2,1)}, f32[3,256,128]{2,1,0:T(8,128)S(1)}) custom-call(s32[2]{0:T(128)S(1)} %pad_add_fusion.ids, s32[1,3]{1,0:T(1,128)S(1)} %copy-done.18, s32[1,3]{1,0:T(1,128)S(1)} %copy-done.20, s32[6]{0:T(128)S(1)} %copy-done.22, f32[3,4,128,64]{3,2,1,0:T(8,128)S(1)} %reshape_squeeze.3.refs_0_, ...), custom_call_target="tpu_custom_call" | custom-call | flops 2097152 | bytes 2097152 | tf_op jit(solution)/shard_map/restore/pallas_call | solution.py:160
  46.8 0.8 copy-done.11
  47.6 0.0 all-to-all-done.refs_0_
  47.6 0.8 copy-done.4
  48.4 5.4 %all-to-all-start.2 = ((bf16[8,256,128]{2,1,0:T(8,128)(2,1)}), bf16[8,256,128]{2,1,0:T(8,128)(2,1)S(1)}, u32[]{:S(2)}, u32[]{:S(2)}) async-start(bf16[8,256,128]{2,1,0:T(8,128)(2,1)} %get-tuple-element.11), calls=%async_computation.2 | async-start | bytes 1048576 | tf_op jit(solution)/shard_map/all_to_all | solution.py:576
  53.8 0.0 collective-permute-done.8
  53.8 2.0 %pad_maximum_fusion.refs_6_.refs_10_.refs_14_.refs_18_ = bf16[4,768,128]{2,1,0:T(8,128)(2,1)} fusion(bf16[2,768,128]{2,1,0:T(8,128)(2,1)} %collective-permute-done.8, bf16[1,768,128]{2,1,0:T(8,128)(2,1)S(1)} %collective-permute-done.7, bf16[1,768,128]{2,1,0:T(8,128)(2,1)S(1)} %history.1), kind=kLoop, calls=%fused_computation | loop fusion | flops 786432 | bytes 1572864 | tf_op jit(solution)/shard_map/concatenate | solution.py:610
  55.8 1.5 %collective-permute-start.9 = (bf16[4,768,128]{2,1,0:T(8,128)(2,1)}, bf16[4,768,128]{2,1,0:T(8,128)(2,1)}, u32[]{:S(2)}, u32[]{:S(2)}) collective-permute-start(bf16[4,768,128]{2,1,0:T(8,128)(2,1)} %pad_maximum_fusion.refs_6_.refs_10_.refs_14_.refs_18_), channel_id=1, source_target_pairs={{0,2},{1,3},{2,0},{3,1},{4,6},{5,7},{6,4},{7,5},{8,10},{9,11},{10,... | collective-permute-start | bytes 2359304 | tf_op jit(solution)/shard_map/ppermute | solution.py:573
  57.3 0.0 copy-start.27
  57.3 0.0 copy-start.28
  57.3 0.0 copy-start.1
  57.4 0.0 copy-start.23
  57.4 0.8 recurrence.1
  58.1 0.0 copy-start.6
  58.1 0.8 copy-done.6
  58.9 6.5 %all-to-all-done.2.refs_3_.refs_6_ = bf16[8,256,128]{2,1,0:T(8,128)(2,1)S(1)} async-done(((bf16[8,256,128]{2,1,0:T(8,128)(2,1)}), bf16[8,256,128]{2,1,0:T(8,128)(2,1)S(1)}, u32[]{:S(2)}, u32[]{:S(2)}) %all-to-all-start.2) | async-done | bytes 524320 | tf_op jit(solution)/shard_map/all_to_all | solution.py:576
  65.4 6.8 %all-to-all-start.1 = ((bf16[8,256,128]{2,1,0:T(8,128)(2,1)}), bf16[8,256,128]{2,1,0:T(8,128)(2,1)}, u32[]{:S(2)}, u32[]{:S(2)}) async-start(bf16[8,256,128]{2,1,0:T(8,128)(2,1)} %copy-done.6), calls=%async_computation.1 | async-start | bytes 1048576 | tf_op jit(solution)/shard_map/all_to_all | solution.py:576
  72.2 0.9 constant_dynamic-update-slice_fusion.refs_5_
  73.1 3.4 %collective-permute-start.4 = (bf16[2,128,512]{2,1,0:T(8,128)(2,1)S(1)}, bf16[2,128,512]{2,1,0:T(8,128)(2,1)}, u32[]{:S(2)}, u32[]{:S(2)}) collective-permute-start(bf16[2,128,512]{2,1,0:T(8,128)(2,1)S(1)} %constant_dynamic-update-slice_fusion.refs_5_), channel_id=1, source_target_pairs={{0,4},{1,5},{2,6},{3,7},{4,8},{5,9},{6,10},{7,11},{8,12},{9,13},{1... | collective-permute-start | bytes 786440 | tf_op jit(solution)/shard_map/ppermute | solution.py:537
  76.5 3.4 %collective-permute-start.5 = (bf16[2,128,512]{2,1,0:T(8,128)(2,1)S(1)}, bf16[2,128,512]{2,1,0:T(8,128)(2,1)}, u32[]{:S(2)}, u32[]{:S(2)}) collective-permute-start(bf16[2,128,512]{2,1,0:T(8,128)(2,1)S(1)} %constant_dynamic-update-slice_fusion.refs_5_), channel_id=1, source_target_pairs={{0,2},{1,3},{2,4},{3,5},{4,6},{5,7},{6,8},{7,9},{8,10},{9,11},{10,... | collective-permute-start | bytes 786440 | tf_op jit(solution)/shard_map/ppermute | solution.py:537
  79.9 0.1 collective-permute-start.10
  80.0 1.1 collective-permute-done.9.refs_7_.refs_11_.refs_15_.refs_19_
  81.1 0.0 collective-permute-start.11
  81.1 8.4 %collective-permute-done.4.refs_1_ = bf16[2,128,512]{2,1,0:T(8,128)(2,1)} collective-permute-done((bf16[2,128,512]{2,1,0:T(8,128)(2,1)S(1)}, bf16[2,128,512]{2,1,0:T(8,128)(2,1)}, u32[]{:S(2)}, u32[]{:S(2)}) %collective-permute-start.4) | collective-permute-done | bytes 262176 | tf_op jit(solution)/shard_map/ppermute | solution.py:537
  89.5 6.8 %collective-permute-done.5.refs_3_ = bf16[2,128,512]{2,1,0:T(8,128)(2,1)} collective-permute-done((bf16[2,128,512]{2,1,0:T(8,128)(2,1)S(1)}, bf16[2,128,512]{2,1,0:T(8,128)(2,1)}, u32[]{:S(2)}, u32[]{:S(2)}) %collective-permute-start.5) | collective-permute-done | bytes 262176 | tf_op jit(solution)/shard_map/ppermute | solution.py:537
  96.3 2.0 %maximum_select_fusion = bf16[2,2,128,512]{3,2,1,0:T(8,128)(2,1)} fusion(bf16[1,2,128,512]{3,2,1,0:T(8,128)(2,1)} %bitcast.11, bf16[1,2,128,512]{3,2,1,0:T(8,128)(2,1)S(1)} %bitcast.24, bf16[1,2,128,512]{3,2,1,0:T(8,128)(2,1)} %bitcast.12, pred[]{:T(512)S(6)} %eq.5), kind=kLoop, calls=%fused_computation.1 | loop fusion | flops 786432 | bytes 1310721 | tf_op jit(solution)/shard_map/jit(_where)/select_n | solution.py:632
  98.4 0.7 pad.7.refs_22_
  99.1 0.7 pad.8.refs_23_
  99.8 0.9 copy-done.7
  100.7 0.9 copy-done.10
  101.6 5.3 %intra.1.refs_0_ = f32[128,8192]{1,0:T(8,128)} custom-call(s32[2]{0:T(128)S(1)} %pad_add_fusion.ids, s32[1,3]{1,0:T(1,128)S(1)} %copy-done.18, s32[1,3]{1,0:T(1,128)S(1)} %copy-done.20, s32[6]{0:T(128)S(1)} %copy-done.22, f32[64]{0:T(128)S(1)} %copy-done.23, bf16[128,8192]{1,0:T(8,128)(2,1)S(1)} %bitcast.23, bf16[128,64]{1,0:T(8,128)(2,1)S(1)} %bitcast.28, ...), custom_call_target="tpu_custom_call" | custom-call | flops 1073741824 | bytes 7340032 | tf_op jit(solution)/shard_map/intra/pallas_call | solution.py:300
  106.9 0.5 collective-permute-start.3
  107.4 1.1 copy-done.3
  108.5 2.0 %middle.1 = (bf16[8,256,128]{2,1,0:T(8,128)(2,1)S(1)}, bf16[8,256,128]{2,1,0:T(8,128)(2,1)S(1)}) custom-call(s32[2]{0:T(128)S(1)} %pad_add_fusion.ids, s32[1,3]{1,0:T(1,128)S(1)} %copy-done.18, s32[1,3]{1,0:T(1,128)S(1)} %copy-done.20, s32[6]{0:T(128)S(1)} %copy-done.22, bf16[8,256,128]{2,1,0:T(8,128)(2,1)} %all-to-all-done.1.refs_0_, ...), custom_call_target="tpu_custom_call" | custom-call | flops 2097152 | bytes 4194304 | tf_op jit(solution)/shard_map/middle/pallas_call | solution.py:160
  110.5 0.1 collective-permute-start.2
  110.6 1.1 slice_bitcast_fusion
  111.6 0.0 collective-permute-done.10.refs_8_.refs_12_.refs_16_.refs_20_
  111.7 0.0 copy-start.8
  111.7 17.2 %attend.1 = bf16[128,4096]{1,0:T(8,128)(2,1)} custom-call(s32[2]{0:T(128)S(1)} %pad_add_fusion.ids, s32[1,3]{1,0:T(1,128)S(1)} %copy-done.18, s32[1,3]{1,0:T(1,128)S(1)} %copy-done.20, s32[6]{0:T(128)S(1)} %copy-done.22, bf16[128,4096]{1,0:T(8,128)(2,1)S(1)} %bitcast.37, bf16[2,128,512]{2,1,0:T(8,128)(2,1)} %collective-permute-done.4.refs_1_, ...), custom_call_target="tpu_custom_call" | custom-call | flops 5368709120 | bytes 8388608 | tf_op jit(solution)/shard_map/attend/pallas_call | solution.py:505
  129.0 0.0 collective-permute-done.2.refs_5_
  129.0 6.1 %finish.1 = bf16[128,8192]{1,0:T(8,128)(2,1)} custom-call(s32[2]{0:T(128)S(1)} %pad_add_fusion.ids, s32[1,3]{1,0:T(1,128)S(1)} %copy-done.18, s32[1,3]{1,0:T(1,128)S(1)} %copy-done.20, s32[6]{0:T(128)S(1)} %copy-done.22, f32[128,8192]{1,0:T(8,128)} %intra.1.refs_0_, bf16[128,64]{1,0:T(8,128)(2,1)S(1)} %bitcast.29, bf16[128,64]{1,0:T(8,128)(2,1)S(1)} %bitcast.32, ...), custom_call_target="tpu_custom_call" | custom-call | flops 268435456 | bytes 9437184 | tf_op jit(solution)/shard_map/finish/pallas_call | solution.py:369
  (46 shorter events, 0.1 us)
Async XLA Ops:
  2.4 1.6 %copy-start = (bf16[1,128,8192]{2,1,0:T(8,128)(2,1)S(1)}, bf16[1,128,8192]{2,1,0:T(8,128)(2,1)}, u32[]{:S(2)}) copy-start(bf16[1,128,8192]{2,1,0:T(8,128)(2,1)} %param.17) | copy-start | bytes 6291460
  4.0 0.9 copy-start.9
  4.9 0.7 copy-start.17
  5.5 0.7 copy-start.19
  6.2 0.7 copy-start.21
  6.8 12.9 %copy-start.25 = (f32[1,3,4,8192]{3,2,1,0:T(4,128)S(1)}, f32[1,3,4,8192]{3,2,1,0:T(4,128)}, u32[]{:S(2)}) copy-start(f32[1,3,4,8192]{3,2,1,0:T(4,128)} %param.23) | copy-start | bytes 1179652
  6.8 14.4 %copy-start.15 = (bf16[1,3,32,512]{3,2,1,0:T(8,128)(2,1)S(1)}, bf16[1,3,32,512]{3,2,1,0:T(8,128)(2,1)}, u32[]{:S(2)}) copy-start(bf16[1,3,32,512]{3,2,1,0:T(8,128)(2,1)} %param.30) | copy-start | bytes 294916
  6.9 14.4 %copy-start.16 = (bf16[1,3,32,512]{3,2,1,0:T(8,128)(2,1)S(1)}, bf16[1,3,32,512]{3,2,1,0:T(8,128)(2,1)}, u32[]{:S(2)}) copy-start(bf16[1,3,32,512]{3,2,1,0:T(8,128)(2,1)} %param.31) | copy-start | bytes 294916
  6.9 14.4 %copy-start.18 = (s32[1,3]{1,0:T(1,128)S(1)}, s32[1,3]{1,0:T(1,128)}, u32[]{:S(2)}) copy-start(s32[1,3]{1,0:T(1,128)} %lengths.17) | copy-start | bytes 40
  6.9 14.4 %copy-start.20 = (s32[1,3]{1,0:T(1,128)S(1)}, s32[1,3]{1,0:T(1,128)}, u32[]{:S(2)}) copy-start(s32[1,3]{1,0:T(1,128)} %histories.17) | copy-start | bytes 40
  6.9 14.4 %copy-start.22 = (s32[6]{0:T(128)S(1)}, s32[6]{0:T(128)}, u32[]{:S(2)}) copy-start(s32[6]{0:T(128)} %homes.17) | copy-start | bytes 76
  9.2 2.0 %collective-permute-start = (bf16[8,272,128]{2,1,0:T(8,128)(2,1)S(1)}, bf16[8,272,128]{2,1,0:T(8,128)(2,1)S(1)}, u32[]{:S(2)}, u32[]{:S(2)}) collective-permute-start(bf16[8,272,128]{2,1,0:T(8,128)(2,1)S(1)} %get-tuple-element.9), channel_id=1, source_target_pairs={{0,1},{1,0},{2,3},{3,2},{4,5},{5,4},{6,7},{7,6},{8,9},{9,8},{10,11... | collective-permute-start | bytes 1671176 | tf_op jit(solution)/shard_map/ppermute | solution.py:573
  12.8 0.8 copy-start.2
  13.6 34.0 %all-to-all-start = ((bf16[8,272,128]{2,1,0:T(8,128)(2,1)}), bf16[8,272,128]{2,1,0:T(8,128)(2,1)S(1)}, u32[]{:S(2)}, u32[]{:S(2)}) async-start(bf16[8,272,128]{2,1,0:T(8,128)(2,1)} %combine.1), calls=%async_computation | async-start | bytes 1114112 | tf_op jit(solution)/shard_map/all_to_all | solution.py:576
  19.8 23.9 %collective-permute-start.1 = (f32[3,4,8192]{2,1,0:T(4,128)S(1)}, f32[3,4,8192]{2,1,0:T(4,128)}, u32[]{:S(2)}, u32[]{:S(2)}) collective-permute-start(f32[3,4,8192]{2,1,0:T(4,128)S(1)} %bitcast.39), channel_id=1, source_target_pairs={{16,0},{0,16},{17,1},{1,17},{18,2},{2,18},{19,3},{3,19},{20,4},{4,... | collective-permute-start | bytes 1179656 | tf_op jit(solution)/shard_map/ppermute | solution.py:581
  21.9 18.4 %collective-permute-start.7 = (bf16[1,768,128]{2,1,0:T(8,128)(2,1)S(1)}, bf16[1,768,128]{2,1,0:T(8,128)(2,1)S(1)}, u32[]{:S(2)}, u32[]{:S(2)}) collective-permute-start(bf16[1,768,128]{2,1,0:T(8,128)(2,1)S(1)} %history.1), channel_id=1, source_target_pairs={{0,8},{1,9},{2,10},{3,11},{4,12},{5,13},{6,14},{7,15},{8,0},{9,1},... | collective-permute-start | bytes 589832 | tf_op jit(solution)/shard_map/ppermute | solution.py:573
  41.1 12.7 %collective-permute-start.8 = (bf16[2,768,128]{2,1,0:T(8,128)(2,1)}, bf16[2,768,128]{2,1,0:T(8,128)(2,1)}, u32[]{:S(2)}, u32[]{:S(2)}) collective-permute-start(bf16[2,768,128]{2,1,0:T(8,128)(2,1)} %pad_maximum_fusion.1), channel_id=1, source_target_pairs={{0,4},{1,5},{2,6},{3,7},{4,0},{5,1},{6,2},{7,3},{8,12},{9,13},{10,... | collective-permute-start | bytes 1179656 | tf_op jit(solution)/shard_map/ppermute | solution.py:573
  46.8 0.8 copy-start.11
  47.6 9.7 %copy-start.26 = (bf16[1,128,512]{2,1,0:T(8,128)(2,1)S(1)}, bf16[1,128,512]{2,1,0:T(8,128)(2,1)}, u32[]{:S(2)}) copy-start(bf16[1,128,512]{2,1,0:T(8,128)(2,1)} %param.28) | copy-start | bytes 393220
  47.6 0.8 copy-start.4
  48.4 17.0 %all-to-all-start.2 = ((bf16[8,256,128]{2,1,0:T(8,128)(2,1)}), bf16[8,256,128]{2,1,0:T(8,128)(2,1)S(1)}, u32[]{:S(2)}, u32[]{:S(2)}) async-start(bf16[8,256,128]{2,1,0:T(8,128)(2,1)} %get-tuple-element.11), calls=%async_computation.2 | async-start | bytes 1048576 | tf_op jit(solution)/shard_map/all_to_all | solution.py:576
  53.8 3.5 %copy-start.5 = (bf16[8,272,128]{2,1,0:T(8,128)(2,1)S(1)}, bf16[8,272,128]{2,1,0:T(8,128)(2,1)}, u32[]{:S(2)}) copy-start(bf16[8,272,128]{2,1,0:T(8,128)(2,1)} %copy-done.4) | copy-start | bytes 1671172
  53.8 3.5 %copy-start.12 = (f32[3,256,128]{2,1,0:T(8,128)S(1)}, f32[3,256,128]{2,1,0:T(8,128)}, u32[]{:S(2)}) copy-start(f32[3,256,128]{2,1,0:T(8,128)} %copy-done.11) | copy-start | bytes 1179652
  55.8 25.3 %collective-permute-start.9 = (bf16[4,768,128]{2,1,0:T(8,128)(2,1)}, bf16[4,768,128]{2,1,0:T(8,128)(2,1)}, u32[]{:S(2)}, u32[]{:S(2)}) collective-permute-start(bf16[4,768,128]{2,1,0:T(8,128)(2,1)} %pad_maximum_fusion.refs_6_.refs_10_.refs_14_.refs_18_), channel_id=1, source_target_pairs={{0,2},{1,3},{2,0},{3,1},{4,6},{5,7},{6,4},{7,5},{8,10},{9,11},{10,... | collective-permute-start | bytes 2359304 | tf_op jit(solution)/shard_map/ppermute | solution.py:573
  57.3 41.1 %copy-start.27 = (bf16[1,3,4,512]{3,2,1,0:T(4,128)(2,1)S(1)}, bf16[1,3,4,512]{3,2,1,0:T(4,128)(2,1)}, u32[]{:S(2)}) copy-start(bf16[1,3,4,512]{3,2,1,0:T(4,128)(2,1)} %param.32) | copy-start | bytes 36868
  57.3 41.8 %copy-start.28 = (bf16[1,3,4,512]{3,2,1,0:T(4,128)(2,1)S(1)}, bf16[1,3,4,512]{3,2,1,0:T(4,128)(2,1)}, u32[]{:S(2)}) copy-start(bf16[1,3,4,512]{3,2,1,0:T(4,128)(2,1)} %param.33) | copy-start | bytes 36868
  57.3 42.5 %copy-start.1 = (bf16[1,128,8192]{2,1,0:T(8,128)(2,1)S(1)}, bf16[1,128,8192]{2,1,0:T(8,128)(2,1)}, u32[]{:S(2)}) copy-start(bf16[1,128,8192]{2,1,0:T(8,128)(2,1)} %param.17) | copy-start | bytes 6291460
  57.4 42.4 %copy-start.23 = (f32[64]{0:T(128)S(1)}, f32[64]{0:T(128)}, u32[]{:S(2)}) copy-start(f32[64]{0:T(128)} %refs_0_.1) | copy-start | bytes 772
  58.1 0.8 copy-start.6
  65.4 42.0 %all-to-all-start.1 = ((bf16[8,256,128]{2,1,0:T(8,128)(2,1)}), bf16[8,256,128]{2,1,0:T(8,128)(2,1)}, u32[]{:S(2)}, u32[]{:S(2)}) async-start(bf16[8,256,128]{2,1,0:T(8,128)(2,1)} %copy-done.6), calls=%async_computation.1 | async-start | bytes 1048576 | tf_op jit(solution)/shard_map/all_to_all | solution.py:576
  73.1 16.4 %collective-permute-start.4 = (bf16[2,128,512]{2,1,0:T(8,128)(2,1)S(1)}, bf16[2,128,512]{2,1,0:T(8,128)(2,1)}, u32[]{:S(2)}, u32[]{:S(2)}) collective-permute-start(bf16[2,128,512]{2,1,0:T(8,128)(2,1)S(1)} %constant_dynamic-update-slice_fusion.refs_5_), channel_id=1, source_target_pairs={{0,4},{1,5},{2,6},{3,7},{4,8},{5,9},{6,10},{7,11},{8,12},{9,13},{1... | collective-permute-start | bytes 786440 | tf_op jit(solution)/shard_map/ppermute | solution.py:537
  76.5 19.8 %collective-permute-start.5 = (bf16[2,128,512]{2,1,0:T(8,128)(2,1)S(1)}, bf16[2,128,512]{2,1,0:T(8,128)(2,1)}, u32[]{:S(2)}, u32[]{:S(2)}) collective-permute-start(bf16[2,128,512]{2,1,0:T(8,128)(2,1)S(1)} %constant_dynamic-update-slice_fusion.refs_5_), channel_id=1, source_target_pairs={{0,2},{1,3},{2,4},{3,5},{4,6},{5,7},{6,8},{7,9},{8,10},{9,11},{10,... | collective-permute-start | bytes 786440 | tf_op jit(solution)/shard_map/ppermute | solution.py:537
  79.9 31.7 %collective-permute-start.10 = (bf16[4,768,128]{2,1,0:T(8,128)(2,1)}, bf16[4,768,128]{2,1,0:T(8,128)(2,1)}, u32[]{:S(2)}, u32[]{:S(2)}) collective-permute-start(bf16[4,768,128]{2,1,0:T(8,128)(2,1)} %pad_maximum_fusion.refs_6_.refs_10_.refs_14_.refs_18_), channel_id=1, source_target_pairs={{0,1},{1,0},{2,3},{3,2},{4,5},{5,4},{6,7},{7,6},{8,9},{9,8},{10,11... | collective-permute-start | bytes 2359304 | tf_op jit(solution)/shard_map/ppermute | solution.py:573
  81.1 30.5 %collective-permute-start.11 = (bf16[4,768,128]{2,1,0:T(8,128)(2,1)}, bf16[4,768,128]{2,1,0:T(8,128)(2,1)}, u32[]{:S(2)}, u32[]{:S(2)}) collective-permute-start(bf16[4,768,128]{2,1,0:T(8,128)(2,1)} %collective-permute-done.9.refs_7_.refs_11_.refs_15_.refs_19_), channel_id=1, source_target_pairs={{0,1},{1,0},{2,3},{3,2},{4,5},{5,4},{6,7},{7,6},{8,9},{9,8},{10,11... | collective-permute-start | bytes 2359304 | tf_op jit(solution)/shard_map/ppermute | solution.py:573
  98.4 12.2 %collective-permute-start.6 = (bf16[2,2,128,512]{3,2,1,0:T(8,128)(2,1)}, bf16[2,2,128,512]{3,2,1,0:T(8,128)(2,1)}, u32[]{:S(2)}, u32[]{:S(2)}) collective-permute-start(bf16[2,2,128,512]{3,2,1,0:T(8,128)(2,1)} %maximum_select_fusion), channel_id=1, source_target_pairs={{0,1},{1,0},{2,3},{3,2},{4,5},{5,4},{6,7},{7,6},{8,9},{9,8},{10,11... | collective-permute-start | bytes 1572872 | tf_op jit(solution)/shard_map/ppermute | solution.py:573
  99.8 0.9 copy-start.7
  100.7 0.9 copy-start.10
  106.9 22.1 %collective-permute-start.3 = (bf16[8,256,128]{2,1,0:T(8,128)(2,1)S(1)}, bf16[8,256,128]{2,1,0:T(8,128)(2,1)S(1)}, u32[]{:S(2)}, u32[]{:S(2)}) collective-permute-start(bf16[8,256,128]{2,1,0:T(8,128)(2,1)S(1)} %all-to-all-done.2.refs_3_.refs_6_), channel_id=1, source_target_pairs={{0,1},{1,0},{2,3},{3,2},{4,5},{5,4},{6,7},{7,6},{8,9},{9,8},{10,11... | collective-permute-start | bytes 1572872 | tf_op jit(solution)/shard_map/ppermute | solution.py:573
  107.4 1.1 copy-start.3
  108.5 3.2 %copy-start.13 = (bf16[3,64,512]{2,1,0:T(8,128)(2,1)S(1)}, bf16[3,64,512]{2,1,0:T(8,128)(2,1)}, u32[]{:S(2)}) copy-start(bf16[3,64,512]{2,1,0:T(8,128)(2,1)} %pad.7.refs_22_) | copy-start | bytes 589828
  108.5 3.2 %copy-start.14 = (bf16[3,64,512]{2,1,0:T(8,128)(2,1)S(1)}, bf16[3,64,512]{2,1,0:T(8,128)(2,1)}, u32[]{:S(2)}) copy-start(bf16[3,64,512]{2,1,0:T(8,128)(2,1)} %pad.8.refs_23_) | copy-start | bytes 589828
  108.5 3.2 %copy-start.24 = (bf16[1,128,4096]{2,1,0:T(8,128)(2,1)S(1)}, bf16[1,128,4096]{2,1,0:T(8,128)(2,1)}, u32[]{:S(2)}) copy-start(bf16[1,128,4096]{2,1,0:T(8,128)(2,1)} %param.27) | copy-start | bytes 3145732
  110.5 18.5 %collective-permute-start.2 = (bf16[8,256,128]{2,1,0:T(8,128)(2,1)S(1)}, bf16[8,256,128]{2,1,0:T(8,128)(2,1)S(1)}, u32[]{:S(2)}, u32[]{:S(2)}) collective-permute-start(bf16[8,256,128]{2,1,0:T(8,128)(2,1)S(1)} %get-tuple-element.13), channel_id=1, source_target_pairs={{0,1},{1,0},{2,3},{3,2},{4,5},{5,4},{6,7},{7,6},{8,9},{9,8},{10,11... | collective-permute-start | bytes 1572872 | tf_op jit(solution)/shard_map/ppermute | solution.py:573
  111.7 17.3 %copy-start.8 = (bf16[1,128,512]{2,1,0:T(8,128)(2,1)S(1)}, bf16[1,128,512]{2,1,0:T(8,128)(2,1)}, u32[]{:S(2)}) copy-start(bf16[1,128,512]{2,1,0:T(8,128)(2,1)} %param.21) | copy-start | bytes 393220

commit v4 on v3

--- a/solution.py
+++ b/solution.py
@@ -56,18 +56,16 @@
     return body
 
 
-def params(mib=48):
+def params(mib=60):
     return pltpu.CompilerParams(vmem_limit_bytes=mib * 1024 * 1024)
 
 
-def running_rows(dl_ref, step_ref):
-    both = jnp.concatenate([dl_ref[...], step_ref[...]], axis=1).astype(jnp.float32).T
-    rates, steps = both[:H], both[H:]
+def running_rows(dl_ref):
     k = lax.broadcasted_iota(jnp.int32, (TOK, TOK), 0)
     u = lax.broadcasted_iota(jnp.int32, (TOK, TOK), 1)
     upto = (k <= u).astype(jnp.bfloat16)
-    running = jnp.dot(rates.astype(jnp.bfloat16), upto, preferred_element_type=jnp.float32)
-    return rates, running, steps
+    running = jnp.dot(dl_ref[...], upto, preferred_element_type=jnp.float32)
+    return dl_ref[...].astype(jnp.float32), running
 
 
 def summary_kernel(
@@ -77,7 +75,8 @@
 
     @pl.when(step == 0)
     def _():
-        rates, running, steps = running_rows(dl_ref, step_ref)
+        rates, running = running_rows(dl_ref)
+        steps = step_ref[...].astype(jnp.float32)
         r = meta.last_start()
         lane = lax.broadcasted_iota(jnp.int32, (H, TOK), 1)
         last = running[:, TOK - 1 :]
@@ -136,8 +135,8 @@
             grid=(STEPS,),
             in_specs=[
                 pl.BlockSpec((TOK, PAIR * P_SIZE), lambda i, *m: (0, i)),
-                pl.BlockSpec((TOK, H), lambda i, *m: (0, 0)),
-                pl.BlockSpec((TOK, H), lambda i, *m: (0, 0)),
+                pl.BlockSpec((H, TOK), lambda i, *m: (0, 0)),
+                pl.BlockSpec((H, TOK), lambda i, *m: (0, 0)),
                 pl.BlockSpec((TOK, G * N), lambda i, *m: (0, 0)),
             ],
             out_specs=[spec, spec],
@@ -153,7 +152,7 @@
     )(*meta, x, rates, steps, writes)
 
 
-def whole(kernel, name, meta, arrays, shapes, size=2):
+def whole(kernel, name, meta, arrays, shapes, size=2, idle=()):
     def spec(shape):
         return pl.BlockSpec(shape, lambda i, *m: (0,) * len(shape))
 
@@ -163,27 +162,19 @@
         grid_spec=pltpu.PrefetchScalarGridSpec(
             num_scalar_prefetch=4,
             grid=(1,),
-            in_specs=[spec(a.shape) for a in arrays],
+            in_specs=[spec(a.shape) for a in arrays] + [pl.BlockSpec(memory_space=pl.ANY)] * len(idle),
             out_specs=[spec(s) for s, _ in shapes],
         ),
         compiler_params=params(),
         cost_estimate=pl.CostEstimate(flops=1 << 21, bytes_accessed=size << 20, transcendentals=0),
         name=name,
-    )(*meta, *arrays)
-
-
-def history_kernel(meta, keys_ref, values_ref, packed_ref):
+    )(*meta, *arrays, *idle)
+
+
+def restore_kernel(local, half, groups, meta, *refs):
+    stored, (keys_ref, values_ref) = refs[:groups], refs[groups : groups + 2]
+    home_ref, away_ref, restored_ref = refs[-3:]
     rows = keys_ref.shape[1]
-    for which, ref in enumerate((keys_ref, values_ref)):
-        for s in range(SEQS):
-            for j in range(KVH):
-                place = ((which * SEQS + s) * KVH + j) * rows
-                packed_ref[0, place : place + rows, :] = ref[s, :, j * HD : (j + 1) * HD]
-
-
-def restore_kernel(local, meta, *refs):
-    stored, (resumed_ref, restored_ref) = refs[:-2], refs[-2:]
-    groups = len(stored)
     for s in range(SEQS):
         slot = meta.homes[meta.group * SEQS + s]
         source = (slot // SEQS - meta.group + groups) % groups
@@ -192,9 +183,21 @@
             for j in range(1, groups):
                 state = jnp.where(source == j, stored[j][slot % SEQS, k], state)
             restored_ref[s, k * N : (k + 1) * N, :] = state.T
-    for chip in range(resumed_ref.shape[0]):
-        closing = meta.session_at((chip + 1) * 2 * TOK - 1)
-        resumed_ref[chip] = restored_ref[closing].astype(jnp.bfloat16)
+    upper = (meta.place >= half).astype(jnp.int32)
+    for out_ref, first in ((home_ref, upper), (away_ref, 1 - upper)):
+        for which, ref in enumerate((keys_ref, values_ref)):
+            for s in range(2):
+                for j in range(KVH):
+                    place = ((which * 2 + s) * KVH + j) * rows
+                    out_ref[0, place : place + rows, :] = ref[first + s, :, j * HD : (j + 1) * HD]
+        out_ref[0, 4 * KVH * rows :, :] = restored_ref[first + 1].astype(jnp.bfloat16)
+
+
+def far_place(distance, bits):
+    place = distance * 0
+    for k in range(bits):
+        place = place + ((distance // (1 << k)) % 2) * (1 << (bits - 1 - k))
+    return place
 
 
 def combine_kernel(local, meta, keep_ref, got_ref, out_ref):
@@ -216,7 +219,8 @@
             out_ref[chip, rows, :] = (carry[k : k + 1] * s0 + s1).astype(jnp.bfloat16)
 
 
-def recurrence_kernel(local, meta, got_ref, restored_ref, out_ref):
+def recurrence_kernel(local, meta, got_ref, restored_ref, *refs):
+    out_ref = refs[-1]
     width = local * N
     span = 2 * TOK
     state = [jnp.zeros((N, P_SIZE), jnp.float32) for _ in range(local)]
@@ -235,7 +239,7 @@
             state[k] = factor[k : k + 1] * source + got_ref[c, rows, :].astype(jnp.float32)
 
 
-def middle_kernel(local, meta, entering_ref, keep_ref, got_ref, resumed_ref, own_ref, send_ref):
+def middle_kernel(local, meta, entering_ref, keep_ref, got_ref, near_ref, beside_ref, own_ref, send_ref):
     even = meta.even
     first = meta.place // 2 * 2 * TOK
     second = first + TOK
@@ -243,13 +247,16 @@
     closes = (start > first) & (start < second)
     opens = start == second
     width = local * N
+    bits = near_ref.shape[0].bit_length() - 1
     for chip in range(entering_ref.shape[0]):
         f0 = jnp.where(
             even,
             factors_of(keep_ref[chip, width:, :], local),
             factors_of(got_ref[chip, width:, :], local),
         )
-        resumed = resumed_ref[chip].astype(jnp.float32)
+        distance = (meta.place // 2) ^ chip
+        far = far_place(distance // 2, bits)
+        resumed = jnp.where(distance % 2 == 0, near_ref[far], beside_ref[far]).astype(jnp.float32)
         for k in range(local):
             rows = slice(k * N, (k + 1) * N)
             entering = entering_ref[chip, rows, :].astype(jnp.float32)
@@ -267,9 +274,9 @@
 
     @pl.when(step == 0)
     def _():
-        _, running, steps = running_rows(dl_ref, step_ref)
+        _, running = running_rows(dl_ref)
         run_s[...] = running
-        step_s[...] = steps
+        step_s[...] = step_ref[...].astype(jnp.float32)
 
     heads = pl.ds(pl.multiple_of(step * PAIR, PAIR), PAIR)
     running = run_s[heads, :]
@@ -305,8 +312,8 @@
             grid=(STEPS,),
             in_specs=[
                 pl.BlockSpec((TOK, PAIR * P_SIZE), lambda i, *m: (0, i)),
-                pl.BlockSpec((TOK, H), lambda i, *m: (0, 0)),
-                pl.BlockSpec((TOK, H), lambda i, *m: (0, 0)),
+                pl.BlockSpec((H, TOK), lambda i, *m: (0, 0)),
+                pl.BlockSpec((H, TOK), lambda i, *m: (0, 0)),
                 pl.BlockSpec((TOK, 2 * N), lambda i, *m: (0, i)),
                 pl.BlockSpec((TOK, 2 * N), lambda i, *m: (0, i)),
             ],
@@ -325,15 +332,18 @@
 
 
 def finish_kernel(
-    local, meta, part_ref, dl_ref, step_ref, read_ref, own_ref, other_ref, mine_ref, theirs_ref, out_ref, factor_s
+    local, meta, part_ref, dl_ref, step_ref, read_ref, own_ref, other_ref, *refs
 ):
+    pieces, (out_ref, factor_s) = refs[:4], refs[4:]
+    bits = pieces[0].shape[0].bit_length() - 1
     step = pl.program_id(0)
     even = meta.even
+    own_chip = meta.place // 2
     r = meta.last_start()
 
     @pl.when(step == 0)
     def _():
-        rates, running, _ = running_rows(dl_ref, step_ref)
+        rates, running = running_rows(dl_ref)
         lane = lax.broadcasted_iota(jnp.int32, (H, TOK), 1)
         base = jnp.sum(jnp.where(lane < r, rates, 0.0), axis=1, keepdims=True)
         factor_s[...] = jnp.exp(jnp.minimum(running - jnp.where(lane >= r, base, 0.0), 0.0))
@@ -350,10 +360,18 @@
             chip, half = k // (2 * local), k // local % 2
             rows = slice((k % local) * N, (k % local + 1) * N)
             own = even if half == 0 else jnp.logical_not(even)
+            distance = (step * (PAIR // (2 * local)) + chip) ^ own_chip
+            far = far_place(distance // 2, bits)
+            near = distance % 2 == 0
+            resume = [piece[far, rows, :] for piece in pieces]
             states = jnp.concatenate(
                 [
                     jnp.where(own, own_ref[chip, rows, :], other_ref[chip, rows, :]),
-                    jnp.where(own, mine_ref[chip, rows, :], theirs_ref[chip, rows, :]),
+                    jnp.where(
+                        own,
+                        jnp.where(near, resume[0], resume[1]),
+                        jnp.where(near, resume[2], resume[3]),
+                    ),
                 ],
                 axis=0,
             )
@@ -362,7 +380,33 @@
             out_ref[:, place] = (part_ref[:, place] + factor[:, k : k + 1] * carried).astype(jnp.bfloat16)
 
 
-def finish(meta, part, rates, steps, reads, own, other, mine, theirs, local):
+def middle(meta, entering, keep, got, near, beside, local):
+    width = local * N
+
+    def spec(shape):
+        return pl.BlockSpec(shape, lambda i, *m: (0,) * len(shape))
+
+    return pl.pallas_call(
+        scalars(middle_kernel, local),
+        out_shape=[jax.ShapeDtypeStruct(entering.shape, jnp.bfloat16)] * 2,
+        grid_spec=pltpu.PrefetchScalarGridSpec(
+            num_scalar_prefetch=4,
+            grid=(1,),
+            in_specs=[spec(a.shape) for a in (entering, keep, got)] + [resumed_spec(near, width)] * 2,
+            out_specs=[spec(entering.shape)] * 2,
+        ),
+        compiler_params=params(),
+        cost_estimate=pl.CostEstimate(flops=1 << 21, bytes_accessed=4 << 20, transcendentals=0),
+        name="middle",
+    )(*meta, entering, keep, got, near, beside)
+
+
+def resumed_spec(piece, width):
+    count, rows, _ = piece.shape
+    return pl.BlockSpec((count, width, P_SIZE), lambda i, *m: (0, rows // width - 1, 0))
+
+
+def finish(meta, part, rates, steps, reads, own, other, pieces, local):
     chips = PAIR // (2 * local)
     width = local * N
     states = pl.BlockSpec((chips, width, P_SIZE), lambda i, *m: (i, 0, 0))
@@ -374,14 +418,13 @@
             grid=(STEPS,),
             in_specs=[
                 pl.BlockSpec((TOK, PAIR * P_SIZE), lambda i, *m: (0, i)),
-                pl.BlockSpec((TOK, H), lambda i, *m: (0, 0)),
-                pl.BlockSpec((TOK, H), lambda i, *m: (0, 0)),
+                pl.BlockSpec((H, TOK), lambda i, *m: (0, 0)),
+                pl.BlockSpec((H, TOK), lambda i, *m: (0, 0)),
                 pl.BlockSpec((TOK, 2 * N), lambda i, *m: (0, i)),
                 states,
                 states,
-                states,
-                states,
-            ],
+            ]
+            + [resumed_spec(pieces[0], width)] * 4,
             out_specs=pl.BlockSpec((TOK, PAIR * P_SIZE), lambda i, *m: (0, i)),
             scratch_shapes=[pltpu.VMEM((H, TOK), jnp.float32)],
         ),
@@ -390,7 +433,7 @@
             flops=2 * H * TOK * TOK * P_SIZE, bytes_accessed=9 << 20, transcendentals=H * TOK
         ),
         name="finish",
-    )(*meta, part, rates, steps, reads, own, other, mine, theirs)
+    )(*meta, part, rates, steps, reads, own, other, *pieces)
 
 
 def attend_kernel(
@@ -416,9 +459,7 @@
             index = lax.broadcasted_iota(jnp.int32, (1, WINDOW), 1)
             piece, index = index // (WINDOW // 4), index % (WINDOW // 4)
             near, row_in = index // share, index % share
-            far, bits = jnp.zeros_like(near), chips.bit_length() - 1
-            for k in range(bits):
-                far = far + ((near // (1 << k)) % 2) * (1 << (bits - 1 - k))
+            far = far_place(near, chips.bit_length() - 1)
             device = meta.place ^ (piece // 2 + piece % 2 * 2 + far * 4)
             place = device * share + row_in
             moved = (row == place + start - WINDOW).astype(jnp.bfloat16)
@@ -488,7 +529,7 @@
     one_session(closing, history_refs[8:12], history_refs[12:], True, r >= 0)
 
 
-def attend(meta, queries, bands, pieces, sink_keys, sink_values):
+def attend(meta, queries, bands, pieces, half, sink_keys, sink_values):
     chips = pieces[0].shape[0]
     share = WINDOW // (4 * chips)
     lanes = QH // KVH * HD
@@ -497,7 +538,8 @@
         def index(j, *m):
             known = Scalars(*m)
             session = known.session_at(known.place * TOK + (TOK - 1 if last else 0))
-            return (0, (which * SEQS + session) * KVH + j, 0)
+            session = session - (known.place >= half).astype(jnp.int32)
+            return (0, (which * 2 + session) * KVH + j, 0)
 
         return pl.BlockSpec((chips, share, HD), index)
 
@@ -565,7 +607,7 @@
     chips = devices // 2
     same_core = [list(range(core, devices, 2)) for core in range(2)]
     meta = (jnp.stack([place, group]).astype(jnp.int32), turn_lengths, history_lengths, home_slot)
-    x, rates, steps = mamba_input[0], decay_log[0], step_size[0]
+    x, rates, steps = mamba_input[0], decay_log[0].T, step_size[0].T
     writes, reads = state_write[0], state_read[0]
     shape = (chips, width, P_SIZE)
 
@@ -582,60 +624,52 @@
 
     keep, send = summaries(meta, x, rates, steps, writes, local)
     got = apart(send, 1)
-    [total] = whole(scalars(combine_kernel, local), "combine", meta, [keep, got], [(keep.shape, jnp.bfloat16)])
-    total = exchanged(total)
+    [chip] = whole(scalars(combine_kernel, local), "combine", meta, [keep, got], [(keep.shape, jnp.bfloat16)])
+    total = exchanged(chip)
+
+    part = intra(meta, skip_gain, x, rates, steps, writes, reads)
 
     stored = [block.reshape(SEQS, local, P_SIZE, N) for block in stored]
-    resumed, restored = whole(
-        scalars(restore_kernel, local),
+    parcel = (1, 4 * KVH * cache_keys.shape[2] + width, P_SIZE)
+    near, away, restored = whole(
+        scalars(restore_kernel, local, devices // 2, groups),
         "restore",
         meta,
-        stored,
-        [(shape, jnp.bfloat16), ((SEQS, width, P_SIZE), jnp.float32)],
-    )
-    mine = exchanged(resumed)
-    theirs = apart(mine, 1)
-    part = intra(meta, skip_gain, x, rates, steps, writes, reads)
-
-    share = cache_keys.shape[2]
-    [history] = whole(
-        scalars(history_kernel),
-        "history",
-        meta,
-        [cache_keys[0], cache_values[0]],
-        [((1, 2 * SEQS * KVH * share, HD), jnp.bfloat16)],
+        [*stored, cache_keys[0], cache_values[0]],
+        [(parcel, jnp.bfloat16), (parcel, jnp.bfloat16), ((SEQS, width, P_SIZE), jnp.float32)],
+        idle=[chip],
     )
     distance = devices // 2
     while distance > 2:
-        history = jnp.concatenate([history, apart(history, distance)], axis=0)
+        near = jnp.concatenate([near, apart(away, distance)], axis=0)
+        away = near
         distance //= 2
-    beside = apart(history, 2)
-    pieces = [history, beside, apart(history, 1), apart(beside, 1)]
+    beside = apart(near, 2)
+    pieces = [near, beside, apart(near, 1), apart(beside, 1)]
 
     [entering] = whole(
-        scalars(recurrence_kernel, local), "recurrence", meta, [total, restored], [(shape, jnp.bfloat16)]
+        scalars(recurrence_kernel, local),
+        "recurrence",
+        meta,
+        [total, restored],
+        [(shape, jnp.bfloat16)],
+        idle=[part],
     )
     entering = exchanged(entering)
-    own, other = whole(
-        scalars(middle_kernel, local),
-        "middle",
-        meta,
-        [entering, keep, got, mine],
-        [(shape, jnp.bfloat16), (shape, jnp.bfloat16)],
-        4,
-    )
+    own, other = middle(meta, entering, keep, got, near, beside, local)
     other = apart(other, 1)
 
     key_value = jnp.stack([turn_keys[0], turn_values[0]])
-    two, four = shifted(key_value, "ctx", 2), shifted(key_value, "ctx", 4)
-    even = place % 2 == 0
+    four = shifted(key_value, "ctx", 4)
+    two = apart(jnp.where((place >> 1) & 1 == 0, key_value, four), 2)
+    even = place & 1 == 0
     pair = apart(jnp.where(even, jnp.stack([key_value, two]), jnp.stack([two, four])), 1)
     bands = [four, pair[1], two, pair[0], key_value]
     sinks = [
         jnp.pad(s[0], ((0, 0), (0, COLUMNS - SPAN - SINKS), (0, 0))) for s in (sink_keys, sink_values)
     ]
-    attended = attend(meta, queries[0], bands, pieces, *sinks)
-    mixed = finish(meta, part, rates, steps, reads, own, other, mine, theirs, local)
+    attended = attend(meta, queries[0], bands, pieces, devices // 2, *sinks)
+    mixed = finish(meta, part, rates, steps, reads, own, other, pieces, local)
     return mixed[None], attended[None]
 
 

time: 134 us -> 129 us (0.963)
  the two profiles are of different devices: /device:TPU:16 before, /device:TPU:18 now
where the time goes in v4:
time: 129 us; the launch traced here: 128 us
  Pallas kernels  50.2 us (39%)
  waiting for transfers between devices  36.4 us (28%)
  starting transfers between devices  26.6 us (21%)
  local copies, waits for them, and re-layouts  10.1 us (8%)
  other arithmetic  4.31 us (3%)
    ppermute x9, waiting for transfers between devices, apart(): lax.ppermute(block, 'ctx', [(i, i ^ distance) for i in range(devices)])  26.8 us
    pallas_call x1, Pallas kernels, attend(): pl.pallas_call(scalars(attend_kernel), out_shape=jax.ShapeDtypeStruct((TO...  18.8 us
    all_to_all x2, starting transfers between devices, exchanged(): lax.all_to_all(block, 'ctx', 0, 0, axis_index_groups=same_core, tiled=True)  11.5 us
    ppermute x9, starting transfers between devices, apart(): lax.ppermute(block, 'ctx', [(i, i ^ distance) for i in range(devices)])  10.1 us
    ppermute x1, waiting for transfers between devices, shards(): stored.append(lax.ppermute(saved_states[0], 'sess', route))  9.63 us
    pallas_call x3, Pallas kernels, whole(): pl.pallas_call(kernel, out_shape=[jax.ShapeDtypeStruct(s, t) for s, t in...  9.24 us
    pallas_call x1, Pallas kernels, finish(): pl.pallas_call(scalars(finish_kernel, local), out_shape=jax.ShapeDtypeStr...  6.7 us
    pallas_call x1, Pallas kernels, intra(): pl.pallas_call(scalars(intra_kernel), out_shape=jax.ShapeDtypeStruct((TOK...  6.61 us
  transfers between devices with their start and end apart: 13, of which 4 were waited for; matrix products, arithmetic and copies ran while one was open for 8% of the time, Pallas kernels for 25%

profile of v4, /device:TPU:18, one launch (start us, length us, event | category | flops | bytes accessed | tf_op | source)
XLA Modules:
  0.0 128.4 jit_solution(4318078521517895895)
XLA Ops:
  0.6 0.0 copy-start.10
  0.6 0.6 pad_add_fusion.ids
  1.3 5.1 %summaries.1 = (bf16[8,272,128]{2,1,0:T(8,128)(2,1)}, bf16[8,272,128]{2,1,0:T(8,128)(2,1)}) custom-call(s32[2]{0:T(128)} %pad_add_fusion.ids, s32[1,3]{1,0:T(1,128)} %lengths.15, s32[1,3]{1,0:T(1,128)} %histories.15, s32[6]{0:T(128)} %homes.15, bf16[128,8192]{1,0:T(8,128)(2,1)} %bitcast.26, bf16[64,128]{1,0:T(8,128)(2,1)} %bitcast.36, ...), custom_call_target="tpu_custom_call" | custom-call | flops 134217728 | bytes 3145728 | tf_op jit(solution)/shard_map/summaries/pallas_call | solution.py:130
  6.4 0.0 collective-permute-start
  6.4 0.0 copy-done.10
  6.4 0.6 collective-permute-start.1
  7.0 1.3 %reshape_squeeze.3.refs_0_ = f32[3,4,128,64]{3,2,1,0:T(8,128)} reshape(f32[1,3,4,8192]{3,2,1,0:T(4,128)S(1)} %copy-done.10) | data formatting | bytes 786432 | tf_op jit(solution)/shard_map/reshape;squeeze | solution.py:632
  8.3 9.6 %collective-permute-done.1 = f32[3,4,8192]{2,1,0:T(4,128)S(1)} collective-permute-done((f32[3,4,8192]{2,1,0:T(4,128)S(1)}, f32[3,4,8192]{2,1,0:T(4,128)S(1)}, u32[]{:S(2)}, u32[]{:S(2)}) %collective-permute-start.1) | collective-permute-done | bytes 393248 | tf_op jit(solution)/shard_map/ppermute | solution.py:623
  17.9 1.3 %reshape.7.refs_1_ = f32[3,4,128,64]{3,2,1,0:T(8,128)} reshape(f32[3,4,8192]{2,1,0:T(4,128)S(1)} %collective-permute-done.1) | data formatting | bytes 786432 | tf_op jit(solution)/shard_map/reshape | solution.py:632
  19.2 0.0 collective-permute-done.refs_1_.refs_2_
  19.2 0.8 copy-done.3
  20.0 3.0 %combine.1.refs_4_ = bf16[8,272,128]{2,1,0:T(8,128)(2,1)} custom-call(s32[2]{0:T(128)} %pad_add_fusion.ids, s32[1,3]{1,0:T(1,128)} %lengths.15, s32[1,3]{1,0:T(1,128)} %histories.15, s32[6]{0:T(128)} %homes.15, bf16[8,272,128]{2,1,0:T(8,128)(2,1)} %get-tuple-element.9.refs_0_.refs_1_, bf16[8,272,128]{2,1,0:T(8,128)(2,1)} %copy-done.3), custom_call_target="tpu_custom_call" | custom-call | flops 2097152 | bytes 2097152 | tf_op jit(solution)/shard_map/combine/pallas_call | solution.py:159
  23.1 3.4 %restore.1 = (bf16[1,768,128]{2,1,0:T(8,128)(2,1)}, bf16[1,768,128]{2,1,0:T(8,128)(2,1)}, f32[3,256,128]{2,1,0:T(8,128)}) custom-call(s32[2]{0:T(128)} %pad_add_fusion.ids, s32[1,3]{1,0:T(1,128)} %lengths.15, s32[1,3]{1,0:T(1,128)} %histories.15, s32[6]{0:T(128)} %homes.15, f32[3,4,128,64]{3,2,1,0:T(8,128)} %reshape_squeeze.3.refs_0_, ...), custom_call_target="tpu_custom_call" | custom-call | flops 2097152 | bytes 2097152 | tf_op jit(solution)/shard_map/restore/pallas_call | solution.py:159
  26.5 0.3 collective-permute-start.2
  26.8 6.4 %all-to-all-start = ((bf16[8,272,128]{2,1,0:T(8,128)(2,1)}), bf16[8,272,128]{2,1,0:T(8,128)(2,1)S(1)}, u32[]{:S(2)}, u32[]{:S(2)}) async-start(bf16[8,272,128]{2,1,0:T(8,128)(2,1)} %combine.1.refs_4_), calls=%async_computation | async-start | bytes 1114112 | tf_op jit(solution)/shard_map/all_to_all | solution.py:618
  33.2 6.1 %collective-permute-done.2 = bf16[1,768,128]{2,1,0:T(8,128)(2,1)S(1)} collective-permute-done((bf16[1,768,128]{2,1,0:T(8,128)(2,1)}, bf16[1,768,128]{2,1,0:T(8,128)(2,1)S(1)}, u32[]{:S(2)}, u32[]{:S(2)}) %collective-permute-start.2) | collective-permute-done | bytes 196640 | tf_op jit(solution)/shard_map/ppermute | solution.py:615
  39.3 1.0 pad_maximum_fusion
  40.3 6.6 %collective-permute-start.3 = (bf16[2,768,128]{2,1,0:T(8,128)(2,1)S(1)}, bf16[2,768,128]{2,1,0:T(8,128)(2,1)S(1)}, u32[]{:S(2)}, u32[]{:S(2)}) collective-permute-start(bf16[2,768,128]{2,1,0:T(8,128)(2,1)S(1)} %pad_maximum_fusion), channel_id=1, source_target_pairs={{0,4},{1,5},{2,6},{3,7},{4,0},{5,1},{6,2},{7,3},{8,12},{9,13},{10,... | collective-permute-start | bytes 1179656 | tf_op jit(solution)/shard_map/ppermute | solution.py:615
  46.8 0.0 copy-done.11
  46.9 0.0 copy-done.8
  46.9 10.7 %collective-permute-done.3 = bf16[2,768,128]{2,1,0:T(8,128)(2,1)S(1)} collective-permute-done((bf16[2,768,128]{2,1,0:T(8,128)(2,1)S(1)}, bf16[2,768,128]{2,1,0:T(8,128)(2,1)S(1)}, u32[]{:S(2)}, u32[]{:S(2)}) %collective-permute-start.3) | collective-permute-done | bytes 393248 | tf_op jit(solution)/shard_map/ppermute | solution.py:615
  57.6 0.1 constant_dynamic-update-slice_fusion.refs_3_.refs_6_.refs_10_.refs_14_.refs_18_
  57.7 0.0 copy-start
  57.7 0.7 collective-permute-start.4
  58.4 0.0 copy-done.12
  58.4 0.0 copy-start.5
  58.4 4.4 %collective-permute-start.8 = (bf16[2,128,512]{2,1,0:T(8,128)(2,1)S(1)}, bf16[2,128,512]{2,1,0:T(8,128)(2,1)S(1)}, u32[]{:S(2)}, u32[]{:S(2)}) collective-permute-start(bf16[2,128,512]{2,1,0:T(8,128)(2,1)S(1)} %constant_dynamic-update-slice_fusion.3.refs_5_), channel_id=1, source_target_pairs={{0,4},{1,5},{2,6},{3,7},{4,8},{5,9},{6,10},{7,11},{8,12},{9,13},{1... | collective-permute-start | bytes 786440 | tf_op jit(solution)/shard_map/ppermute | solution.py:579
  62.8 6.6 %intra.1.refs_2_.refs_0_ = f32[128,8192]{1,0:T(8,128)} custom-call(s32[2]{0:T(128)} %pad_add_fusion.ids, s32[1,3]{1,0:T(1,128)} %lengths.15, s32[1,3]{1,0:T(1,128)} %histories.15, s32[6]{0:T(128)} %homes.15, f32[64]{0:T(128)} %refs_0_.1, bf16[128,8192]{1,0:T(8,128)(2,1)} %bitcast.27, bf16[64,128]{1,0:T(8,128)(2,1)} %bitcast.37, bf16[64,128]{1,0:T(8,128)(2,1)} %bitcast.40, ...), custom_call_target="tpu_custom_call" | custom-call | flops 1073741824 | bytes 7340032 | tf_op jit(solution)/shard_map/intra/pallas_call | solution.py:307
  69.5 0.0 all-to-all-done.refs_0_
  69.5 0.8 copy-done.2
  70.3 2.8 %recurrence.1 = bf16[8,256,128]{2,1,0:T(8,128)(2,1)} custom-call(s32[2]{0:T(128)} %pad_add_fusion.ids, s32[1,3]{1,0:T(1,128)} %lengths.15, s32[1,3]{1,0:T(1,128)} %histories.15, s32[6]{0:T(128)} %homes.15, bf16[8,272,128]{2,1,0:T(8,128)(2,1)} %copy-done.2, f32[3,256,128]{2,1,0:T(8,128)} %get-tuple-element.11.refs_1_, f32[128,8192]{1,0:T(8,128)} %intra.1.refs_2_.refs_0_), custom_call_target="tpu_custom_call" | custom-call | flops 2097152 | bytes 2097152 | tf_op jit(solution)/shard_map/recurrence/pallas_call | solution.py:159
  73.1 5.1 %all-to-all-start.1 = ((bf16[8,256,128]{2,1,0:T(8,128)(2,1)}), bf16[8,256,128]{2,1,0:T(8,128)(2,1)S(1)}, u32[]{:S(2)}, u32[]{:S(2)}) async-start(bf16[8,256,128]{2,1,0:T(8,128)(2,1)} %recurrence.1), calls=%async_computation.1 | async-start | bytes 1048576 | tf_op jit(solution)/shard_map/all_to_all | solution.py:618
  78.2 0.0 collective-permute-done.8.refs_1_
  78.3 0.8 broadcast_select_fusion
  79.1 1.5 %collective-permute-start.9 = (bf16[2,128,512]{2,1,0:T(8,128)(2,1)}, bf16[2,128,512]{2,1,0:T(8,128)(2,1)}, u32[]{:S(2)}, u32[]{:S(2)}) collective-permute-start(bf16[2,128,512]{2,1,0:T(8,128)(2,1)} %broadcast_select_fusion), channel_id=1, source_target_pairs={{0,2},{1,3},{2,0},{3,1},{4,6},{5,7},{6,4},{7,5},{8,10},{9,11},{10,... | collective-permute-start | bytes 786440 | tf_op jit(solution)/shard_map/ppermute | solution.py:615
  80.5 0.0 copy-done
  80.5 0.0 collective-permute-start.6
  80.5 0.0 collective-permute-done.4.refs_4_.refs_7_.refs_11_.refs_15_.refs_19_
  80.5 0.0 copy-start.1
  80.5 0.5 collective-permute-start.7
  81.0 10.0 %collective-permute-done.9.refs_3_ = bf16[2,128,512]{2,1,0:T(8,128)(2,1)} collective-permute-done((bf16[2,128,512]{2,1,0:T(8,128)(2,1)}, bf16[2,128,512]{2,1,0:T(8,128)(2,1)}, u32[]{:S(2)}, u32[]{:S(2)}) %collective-permute-start.9) | collective-permute-done | bytes 262176 | tf_op jit(solution)/shard_map/ppermute | solution.py:615
  91.0 0.0 copy-done.5
  91.0 1.9 %maximum_select_fusion = bf16[2,2,128,512]{3,2,1,0:T(8,128)(2,1)} fusion(bf16[1,2,128,512]{3,2,1,0:T(8,128)(2,1)} %bitcast.17, bf16[1,2,128,512]{3,2,1,0:T(8,128)(2,1)S(1)} %bitcast.29, bf16[1,2,128,512]{3,2,1,0:T(8,128)(2,1)S(1)} %bitcast.30, pred[]{:T(512)S(6)} %eq.6), kind=kLoop, calls=%fused_computation | loop fusion | flops 786432 | bytes 1310721 | tf_op jit(solution)/shard_map/jit(_where)/select_n | solution.py:666
  92.9 0.0 collective-permute-start.10
  92.9 0.0 copy-done.13
  92.9 0.7 pad.7.refs_22_
  93.6 0.0 copy-done.14
  93.6 0.7 pad.8.refs_23_
  94.3 0.0 all-to-all-done.1.refs_0_
  94.3 0.0 copy-done.1
  94.3 0.8 copy-done.4
  95.1 3.6 %middle.1 = (bf16[8,256,128]{2,1,0:T(8,128)(2,1)}, bf16[8,256,128]{2,1,0:T(8,128)(2,1)}) custom-call(s32[2]{0:T(128)} %pad_add_fusion.ids, s32[1,3]{1,0:T(1,128)} %lengths.15, s32[1,3]{1,0:T(1,128)} %histories.15, s32[6]{0:T(128)} %homes.15, bf16[8,256,128]{2,1,0:T(8,128)(2,1)} %copy-done.4, bf16[8,272,128]{2,1,0:T(8,128)(2,1)} %get-tuple-element.9.refs_0_.refs_1_, ...), custom_call_target="tpu_custom_call" | custom-call | flops 2097152 | bytes 4194304 | tf_op jit(solution)/shard_map/middle/pallas_call | solution.py:389
  98.8 0.0 copy-done.6
  98.8 0.5 collective-permute-start.5
  99.3 0.0 collective-permute-done.10
  99.3 1.9 %slice_bitcast_fusion = (bf16[2,128,512]{2,1,0:T(8,128)(2,1)}, bf16[2,128,512]{2,1,0:T(8,128)(2,1)}) fusion(bf16[2,2,128,512]{3,2,1,0:T(8,128)(2,1)} %collective-permute-done.10), kind=kLoop, calls=%fused_computation.2 | loop fusion | bytes 1048576 | tf_op jit(solution)/shard_map/squeeze | solution.py:667
  101.2 0.0 collective-permute-done.6.refs_8_.refs_12_.refs_16_.refs_20_
  101.2 0.0 collective-permute-done.7.refs_9_.refs_13_.refs_17_.refs_21_
  101.2 0.9 copy-done.7
  102.1 18.8 %attend.1 = bf16[128,4096]{1,0:T(8,128)(2,1)} custom-call(s32[2]{0:T(128)} %pad_add_fusion.ids, s32[1,3]{1,0:T(1,128)} %lengths.15, s32[1,3]{1,0:T(1,128)} %histories.15, s32[6]{0:T(128)} %homes.15, bf16[128,4096]{1,0:T(8,128)(2,1)} %bitcast.46, bf16[2,128,512]{2,1,0:T(8,128)(2,1)} %copy-done.6, bf16[2,128,512]{2,1,0:T(8,128)(2,1)} %get-tuple-element.17.refs_2_, ...), custom_call_target="tpu_custom_call" | custom-call | flops 5368709120 | bytes 8388608 | tf_op jit(solution)/shard_map/attend/pallas_call | solution.py:547
  120.9 0.0 collective-permute-done.5.refs_5_
  120.9 0.0 copy-start.9
  120.9 0.8 copy-done.9
  121.7 6.7 %finish.1 = bf16[128,8192]{1,0:T(8,128)(2,1)} custom-call(s32[2]{0:T(128)} %pad_add_fusion.ids, s32[1,3]{1,0:T(1,128)} %lengths.15, s32[1,3]{1,0:T(1,128)} %histories.15, s32[6]{0:T(128)} %homes.15, f32[128,8192]{1,0:T(8,128)} %intra.1.refs_2_.refs_0_, bf16[64,128]{1,0:T(8,128)(2,1)} %bitcast.38, bf16[64,128]{1,0:T(8,128)(2,1)} %bitcast.41, ...), custom_call_target="tpu_custom_call" | custom-call | flops 268435456 | bytes 9437184 | tf_op jit(solution)/shard_map/finish/pallas_call | solution.py:413
  (14 shorter events, 0.1 us)
Async XLA Ops:
  0.6 5.8 %copy-start.10 = (f32[1,3,4,8192]{3,2,1,0:T(4,128)S(1)}, f32[1,3,4,8192]{3,2,1,0:T(4,128)}, u32[]{:S(2)}) copy-start(f32[1,3,4,8192]{3,2,1,0:T(4,128)} %param.23) | copy-start | bytes 1179652
  6.4 12.8 %collective-permute-start = (bf16[8,272,128]{2,1,0:T(8,128)(2,1)}, bf16[8,272,128]{2,1,0:T(8,128)(2,1)S(1)}, u32[]{:S(2)}, u32[]{:S(2)}) collective-permute-start(bf16[8,272,128]{2,1,0:T(8,128)(2,1)} %get-tuple-element.10), channel_id=1, source_target_pairs={{0,1},{1,0},{2,3},{3,2},{4,5},{5,4},{6,7},{7,6},{8,9},{9,8},{10,11... | collective-permute-start | bytes 1671176 | tf_op jit(solution)/shard_map/ppermute | solution.py:615
  6.4 11.5 %collective-permute-start.1 = (f32[3,4,8192]{2,1,0:T(4,128)S(1)}, f32[3,4,8192]{2,1,0:T(4,128)S(1)}, u32[]{:S(2)}, u32[]{:S(2)}) collective-permute-start(f32[3,4,8192]{2,1,0:T(4,128)S(1)} %bitcast.35), channel_id=1, source_target_pairs={{16,0},{0,16},{17,1},{1,17},{18,2},{2,18},{19,3},{3,19},{20,4},{4,... | collective-permute-start | bytes 1179656 | tf_op jit(solution)/shard_map/ppermute | solution.py:623
  19.2 0.8 copy-start.3
  23.1 23.8 %copy-start.11 = (bf16[1,128,512]{2,1,0:T(8,128)(2,1)S(1)}, bf16[1,128,512]{2,1,0:T(8,128)(2,1)}, u32[]{:S(2)}) copy-start(bf16[1,128,512]{2,1,0:T(8,128)(2,1)} %param.28) | copy-start | bytes 393220
  26.5 20.4 %copy-start.8 = (bf16[1,768,128]{2,1,0:T(8,128)(2,1)S(1)}, bf16[1,768,128]{2,1,0:T(8,128)(2,1)}, u32[]{:S(2)}) copy-start(bf16[1,768,128]{2,1,0:T(8,128)(2,1)} %get-tuple-element.12) | copy-start | bytes 589828
  26.5 31.9 %copy-start.12 = (bf16[1,128,512]{2,1,0:T(8,128)(2,1)S(1)}, bf16[1,128,512]{2,1,0:T(8,128)(2,1)}, u32[]{:S(2)}) copy-start(bf16[1,128,512]{2,1,0:T(8,128)(2,1)} %param.29) | copy-start | bytes 393220
  26.5 12.8 %collective-permute-start.2 = (bf16[1,768,128]{2,1,0:T(8,128)(2,1)}, bf16[1,768,128]{2,1,0:T(8,128)(2,1)S(1)}, u32[]{:S(2)}, u32[]{:S(2)}) collective-permute-start(bf16[1,768,128]{2,1,0:T(8,128)(2,1)} %get-tuple-element.13), channel_id=1, source_target_pairs={{0,8},{1,9},{2,10},{3,11},{4,12},{5,13},{6,14},{7,15},{8,0},{9,1},... | collective-permute-start | bytes 589832 | tf_op jit(solution)/shard_map/ppermute | solution.py:615
  26.8 42.7 %all-to-all-start = ((bf16[8,272,128]{2,1,0:T(8,128)(2,1)}), bf16[8,272,128]{2,1,0:T(8,128)(2,1)S(1)}, u32[]{:S(2)}, u32[]{:S(2)}) async-start(bf16[8,272,128]{2,1,0:T(8,128)(2,1)} %combine.1.refs_4_), calls=%async_computation | async-start | bytes 1114112 | tf_op jit(solution)/shard_map/all_to_all | solution.py:618
  40.3 17.4 %collective-permute-start.3 = (bf16[2,768,128]{2,1,0:T(8,128)(2,1)S(1)}, bf16[2,768,128]{2,1,0:T(8,128)(2,1)S(1)}, u32[]{:S(2)}, u32[]{:S(2)}) collective-permute-start(bf16[2,768,128]{2,1,0:T(8,128)(2,1)S(1)} %pad_maximum_fusion), channel_id=1, source_target_pairs={{0,4},{1,5},{2,6},{3,7},{4,0},{5,1},{6,2},{7,3},{8,12},{9,13},{10,... | collective-permute-start | bytes 1179656 | tf_op jit(solution)/shard_map/ppermute | solution.py:615
  57.7 22.8 %copy-start = (bf16[4,768,128]{2,1,0:T(8,128)(2,1)}, bf16[4,768,128]{2,1,0:T(8,128)(2,1)S(1)}, u32[]{:S(2)}) copy-start(bf16[4,768,128]{2,1,0:T(8,128)(2,1)S(1)} %constant_dynamic-update-slice_fusion.refs_3_.refs_6_.refs_10_.refs_14_.refs_18_) | copy-start | bytes 2359300
  57.7 22.8 %collective-permute-start.4 = (bf16[4,768,128]{2,1,0:T(8,128)(2,1)S(1)}, bf16[4,768,128]{2,1,0:T(8,128)(2,1)S(1)}, u32[]{:S(2)}, u32[]{:S(2)}) collective-permute-start(bf16[4,768,128]{2,1,0:T(8,128)(2,1)S(1)} %constant_dynamic-update-slice_fusion.refs_3_.refs_6_.refs_10_.refs_14_.refs_18_), channel_id=1, source_target_pairs={{0,2},{1,3},{2,0},{3,1},{4,6},{5,7},{6,4},{7,5},{8,10},{9,11},{10,... | collective-permute-start | bytes 2359304 | tf_op jit(solution)/shard_map/ppermute | solution.py:615
  58.4 32.6 %copy-start.5 = (bf16[2,128,512]{2,1,0:T(8,128)(2,1)}, bf16[2,128,512]{2,1,0:T(8,128)(2,1)S(1)}, u32[]{:S(2)}) copy-start(bf16[2,128,512]{2,1,0:T(8,128)(2,1)S(1)} %constant_dynamic-update-slice_fusion.3.refs_5_) | copy-start | bytes 786436
  58.4 19.8 %collective-permute-start.8 = (bf16[2,128,512]{2,1,0:T(8,128)(2,1)S(1)}, bf16[2,128,512]{2,1,0:T(8,128)(2,1)S(1)}, u32[]{:S(2)}, u32[]{:S(2)}) collective-permute-start(bf16[2,128,512]{2,1,0:T(8,128)(2,1)S(1)} %constant_dynamic-update-slice_fusion.3.refs_5_), channel_id=1, source_target_pairs={{0,4},{1,5},{2,6},{3,7},{4,8},{5,9},{6,10},{7,11},{8,12},{9,13},{1... | collective-permute-start | bytes 786440 | tf_op jit(solution)/shard_map/ppermute | solution.py:579
  69.5 0.8 copy-start.2
  73.1 19.9 %copy-start.13 = (bf16[1,3,4,512]{3,2,1,0:T(4,128)(2,1)S(1)}, bf16[1,3,4,512]{3,2,1,0:T(4,128)(2,1)}, u32[]{:S(2)}) copy-start(bf16[1,3,4,512]{3,2,1,0:T(4,128)(2,1)} %param.32) | copy-start | bytes 36868
  73.1 20.6 %copy-start.14 = (bf16[1,3,4,512]{3,2,1,0:T(4,128)(2,1)S(1)}, bf16[1,3,4,512]{3,2,1,0:T(4,128)(2,1)}, u32[]{:S(2)}) copy-start(bf16[1,3,4,512]{3,2,1,0:T(4,128)(2,1)} %param.33) | copy-start | bytes 36868
  73.1 21.2 %all-to-all-start.1 = ((bf16[8,256,128]{2,1,0:T(8,128)(2,1)}), bf16[8,256,128]{2,1,0:T(8,128)(2,1)S(1)}, u32[]{:S(2)}, u32[]{:S(2)}) async-start(bf16[8,256,128]{2,1,0:T(8,128)(2,1)} %recurrence.1), calls=%async_computation.1 | async-start | bytes 1048576 | tf_op jit(solution)/shard_map/all_to_all | solution.py:618
  78.2 20.5 %copy-start.6 = (bf16[2,128,512]{2,1,0:T(8,128)(2,1)}, bf16[2,128,512]{2,1,0:T(8,128)(2,1)S(1)}, u32[]{:S(2)}) copy-start(bf16[2,128,512]{2,1,0:T(8,128)(2,1)S(1)} %collective-permute-done.8.refs_1_) | copy-start | bytes 786436
  79.1 11.9 %collective-permute-start.9 = (bf16[2,128,512]{2,1,0:T(8,128)(2,1)}, bf16[2,128,512]{2,1,0:T(8,128)(2,1)}, u32[]{:S(2)}, u32[]{:S(2)}) collective-permute-start(bf16[2,128,512]{2,1,0:T(8,128)(2,1)} %broadcast_select_fusion), channel_id=1, source_target_pairs={{0,2},{1,3},{2,0},{3,1},{4,6},{5,7},{6,4},{7,5},{8,10},{9,11},{10,... | collective-permute-start | bytes 786440 | tf_op jit(solution)/shard_map/ppermute | solution.py:615
  80.5 20.7 %collective-permute-start.6 = (bf16[4,768,128]{2,1,0:T(8,128)(2,1)S(1)}, bf16[4,768,128]{2,1,0:T(8,128)(2,1)S(1)}, u32[]{:S(2)}, u32[]{:S(2)}) collective-permute-start(bf16[4,768,128]{2,1,0:T(8,128)(2,1)S(1)} %constant_dynamic-update-slice_fusion.refs_3_.refs_6_.refs_10_.refs_14_.refs_18_), channel_id=1, source_target_pairs={{0,1},{1,0},{2,3},{3,2},{4,5},{5,4},{6,7},{7,6},{8,9},{9,8},{10,11... | collective-permute-start | bytes 2359304 | tf_op jit(solution)/shard_map/ppermute | solution.py:615
  80.5 13.8 %copy-start.1 = (bf16[4,768,128]{2,1,0:T(8,128)(2,1)}, bf16[4,768,128]{2,1,0:T(8,128)(2,1)S(1)}, u32[]{:S(2)}) copy-start(bf16[4,768,128]{2,1,0:T(8,128)(2,1)S(1)} %collective-permute-done.4.refs_4_.refs_7_.refs_11_.refs_15_.refs_19_) | copy-start | bytes 2359300
  80.5 20.7 %collective-permute-start.7 = (bf16[4,768,128]{2,1,0:T(8,128)(2,1)S(1)}, bf16[4,768,128]{2,1,0:T(8,128)(2,1)}, u32[]{:S(2)}, u32[]{:S(2)}) collective-permute-start(bf16[4,768,128]{2,1,0:T(8,128)(2,1)S(1)} %collective-permute-done.4.refs_4_.refs_7_.refs_11_.refs_15_.refs_19_), channel_id=1, source_target_pairs={{0,1},{1,0},{2,3},{3,2},{4,5},{5,4},{6,7},{7,6},{8,9},{9,8},{10,11... | collective-permute-start | bytes 2359304 | tf_op jit(solution)/shard_map/ppermute | solution.py:615
  92.9 6.3 %collective-permute-start.10 = (bf16[2,2,128,512]{3,2,1,0:T(8,128)(2,1)}, bf16[2,2,128,512]{3,2,1,0:T(8,128)(2,1)}, u32[]{:S(2)}, u32[]{:S(2)}) collective-permute-start(bf16[2,2,128,512]{3,2,1,0:T(8,128)(2,1)} %maximum_select_fusion), channel_id=1, source_target_pairs={{0,1},{1,0},{2,3},{3,2},{4,5},{5,4},{6,7},{7,6},{8,9},{9,8},{10,11... | collective-permute-start | bytes 1572872 | tf_op jit(solution)/shard_map/ppermute | solution.py:615
  94.3 0.8 copy-start.4
  98.8 22.1 %collective-permute-start.5 = (bf16[8,256,128]{2,1,0:T(8,128)(2,1)}, bf16[8,256,128]{2,1,0:T(8,128)(2,1)S(1)}, u32[]{:S(2)}, u32[]{:S(2)}) collective-permute-start(bf16[8,256,128]{2,1,0:T(8,128)(2,1)} %get-tuple-element.15), channel_id=1, source_target_pairs={{0,1},{1,0},{2,3},{3,2},{4,5},{5,4},{6,7},{7,6},{8,9},{9,8},{10,11... | collective-permute-start | bytes 1572872 | tf_op jit(solution)/shard_map/ppermute | solution.py:615
  101.2 0.9 copy-start.7
  120.9 0.9 copy-start.9
